TPU v7x, 768 devices: a whole 4x8x12 slice. The times are simulated.
768 devices in a mesh: grid: 96 (over z, x, core), mesh: 8 (over y).
Axes of the slice: x: 4, y: 8, z: 12, core: 2. Of those that a mesh axis runs over, the one named last changes fastest.
Arguments:
- grid_vars: bfloat16 [196608, 227], P(('grid', 'mesh')), may hold values from -6 to 6
- mesh_init: bfloat16 [98304, 512], P(('grid', 'mesh')), may hold values from -6 to 6
- w_embed: bfloat16 [227, 512], replicated, may hold values from -0.375 to 0.375
- w_send: bfloat16 [512, 512], replicated, may hold values from -0.25 to 0.25
- w_node: bfloat16 [512, 512], replicated, may hold values from -0.25 to 0.25
- node_gain: float32 [512], replicated, may hold values from 0.5 to 2
- w_proc_send: bfloat16 [512, 512], replicated, may hold values from -0.25 to 0.25
- w_proc_recv: bfloat16 [512, 512], replicated, may hold values from -0.25 to 0.25
- w_proc_out: bfloat16 [512, 512], replicated, may hold values from -0.25 to 0.25
- w_dec_send: bfloat16 [512, 512], replicated, may hold values from -0.25 to 0.25
- w_dec_out: bfloat16 [512, 227], replicated, may hold values from -0.25 to 0.25
- enc_src: int32 [294912], P(('grid', 'mesh')), may hold values from 0 to 255
- enc_dst: int32 [294912], P(('grid', 'mesh')), may hold values from 0 to 3071
- proc_src: int32 [786432], P(('grid', 'mesh')), may hold values from 0 to 3071
- proc_dst: int32 [786432], P(('grid', 'mesh')), may hold values from 0 to 127
- dec_src: int32 [589824], P(('grid', 'mesh')), may hold values from 0 to 3071
- dec_dst: int32 [589824], P(('grid', 'mesh')), may hold values from 0 to 255
Outputs:
- next_vars: bfloat16 [196608, 227], P(('grid', 'mesh'))
Inputs may be any that keep to these rules, and one draw needn't show every extreme that they name: `enc_src`: local grid node numbers of the sending device. `enc_dst`: neighbourhood codes: band offset times 8 * 128 plus the node number within the band group. `proc_src`: neighbourhood codes as for enc_dst. `proc_dst`: local mesh node numbers of the receiving device. `dec_src`: neighbourhood codes as for enc_dst. `dec_dst`: local grid node numbers of the receiving device.
All inputs are finite; a program needn't handle non-finite values.
Results may differ from a plain program's by a relative error of at most 0.012.
Values may be sent and summed in bfloat16 or wider, within the bound.
No kernel may reach another device: no remote copies, remote signals or barrier semaphores. Data moves between devices by JAX's collectives and lax.ppermute only.
A program may use at most 32 MiB of HBM per device.

v0:
```python
import jax
import jax.numpy as jnp
from jax import lax
from jax.sharding import PartitionSpec as P


def padded(cells, sides, width):
    for axis, dim in sides:
        count = lax.axis_size(axis)
        ends = count - 1
        head = lax.slice_in_dim(cells, 0, width, axis=dim)
        tail = lax.slice_in_dim(cells, cells.shape[dim] - width, cells.shape[dim], axis=dim)
        cells = jnp.concatenate(
            [
                lax.ppermute(tail, axis, [(i, (i + 1) % count) for i in range(ends)]),
                cells,
                lax.ppermute(head, axis, [((i + 1) % count, i) for i in range(ends)]),
            ],
            axis=dim,
        )
    return cells


def passed_along(block, axis, distance):
    devices = range(lax.axis_size(axis))
    route = [(i - distance, i) for i in devices if i - distance in devices]
    return lax.ppermute(block, axis, route)


def rms_rows(values):
    return values * lax.rsqrt(jnp.mean(values * values, axis=-1, keepdims=True) + 1e-05)


def one_hot_rows(labels, count):
    return (labels[None, :] == jnp.arange(count, dtype=jnp.int32)[:, None]).astype(jnp.bfloat16)


def nearby_rows(node_rows):
    gathered = lax.all_gather(node_rows, "mesh", axis=0, tiled=True)
    widened = padded(gathered[None], (("grid", 0),), 1)
    return widened.reshape(-1, node_rows.shape[1])


def reach_mask(codes, band_nodes):
    target = lax.axis_index("grid") + codes // band_nodes - 1
    return ((target >= 0) & (target < lax.axis_size("grid"))).astype(jnp.float32)[:, None]


def shards(
    grid_vars,
    mesh_init,
    w_embed,
    w_send,
    w_node,
    node_gain,
    w_proc_send,
    w_proc_recv,
    w_proc_out,
    w_dec_send,
    w_dec_out,
    enc_src,
    enc_dst,
    proc_src,
    proc_dst,
    dec_src,
    dec_dst,
):
    mesh_count = lax.axis_size("mesh")
    mesh_rows_here = mesh_init.shape[0]
    width = mesh_init.shape[1]
    band_nodes = mesh_count * mesh_rows_here
    grid_lat = jax.nn.silu(jnp.dot(grid_vars, w_embed, preferred_element_type=jnp.float32)).astype(
        jnp.bfloat16
    )
    enc_out = jax.nn.silu(jnp.dot(grid_lat, w_send, preferred_element_type=jnp.float32)).astype(
        jnp.bfloat16
    )
    partial_sums = jnp.dot(
        one_hot_rows(enc_dst, 3 * band_nodes), enc_out[enc_src], preferred_element_type=jnp.float32
    )
    partial_sums = partial_sums.reshape(3, mesh_count, mesh_rows_here, width)
    from_above = passed_along(partial_sums[0], "grid", -1)
    from_below = passed_along(partial_sums[2], "grid", 1)
    banded = partial_sums[1] + from_above + from_below
    received = lax.all_to_all(banded, "mesh", split_axis=0, concat_axis=0, tiled=True)
    enc_agg = jnp.sum(received, axis=0)
    node_in = jax.nn.silu(rms_rows(enc_agg) * node_gain).astype(jnp.bfloat16)
    mesh_one = (
        mesh_init.astype(jnp.float32) + jnp.dot(node_in, w_node, preferred_element_type=jnp.float32)
    ).astype(jnp.bfloat16)
    nearby_one = nearby_rows(mesh_one)
    send_proj = jnp.dot(nearby_one[proc_src], w_proc_send, preferred_element_type=jnp.float32)
    recv_proj = jnp.dot(mesh_one, w_proc_recv, preferred_element_type=jnp.float32)[proc_dst]
    proc_msg = (jax.nn.silu(send_proj + recv_proj) * reach_mask(proc_src, band_nodes)).astype(
        jnp.bfloat16
    )
    proc_agg = jnp.dot(
        one_hot_rows(proc_dst, mesh_rows_here), proc_msg, preferred_element_type=jnp.float32
    )
    proc_norm = rms_rows(proc_agg).astype(jnp.bfloat16)
    mesh_two = (
        mesh_one.astype(jnp.float32)
        + jnp.dot(proc_norm, w_proc_out, preferred_element_type=jnp.float32)
    ).astype(jnp.bfloat16)
    dec_out = jax.nn.silu(jnp.dot(mesh_two, w_dec_send, preferred_element_type=jnp.float32)).astype(
        jnp.bfloat16
    )
    nearby_two = nearby_rows(dec_out)
    dec_msg = (nearby_two[dec_src].astype(jnp.float32) * reach_mask(dec_src, band_nodes)).astype(
        jnp.bfloat16
    )
    dec_agg = jnp.dot(
        one_hot_rows(dec_dst, grid_vars.shape[0]), dec_msg, preferred_element_type=jnp.float32
    )
    dec_norm = rms_rows(dec_agg).astype(jnp.bfloat16)
    return (
        grid_vars.astype(jnp.float32)
        + jnp.dot(dec_norm, w_dec_out, preferred_element_type=jnp.float32)
    ).astype(jnp.bfloat16)


def solution(mesh):
    in_specs = (
        P(("grid", "mesh"), None),
        P(("grid", "mesh"), None),
        P(),
        P(),
        P(),
        P(),
        P(),
        P(),
        P(),
        P(),
        P(),
        P(("grid", "mesh")),
        P(("grid", "mesh")),
        P(("grid", "mesh")),
        P(("grid", "mesh")),
        P(("grid", "mesh")),
        P(("grid", "mesh")),
    )
    out_specs = P(("grid", "mesh"), None)
    return jax.shard_map(shards, mesh=mesh, in_specs=in_specs, out_specs=out_specs, check_vma=False)
```

profile of v0, /device:TPU:199, one launch (start us, length us, event | category | flops | bytes accessed | tf_op | source)
XLA Modules:
  0.0 272.0 jit_solution(13074362016026540005)
XLA Ops:
  6.5 0.7 compare_select_fusion.1
  7.6 1.6 multiply_convert_fusion.4
  9.2 2.1 gather_fusion
  11.3 1.8 fusion
  13.1 0.7 fusion.35
  13.8 2.6 collective-permute-start
  16.4 6.3 %collective-permute-start.1 = (f32[8,128,512]{2,1,0:T(8,128)S(1)}, f32[8,128,512]{2,1,0:T(8,128)S(1)}, u32[]{:S(2)}, u32[]{:S(2)}) collective-permute-start(f32[8,128,512]{2,1,0:T(8,128)S(1)} %bitcast.22), channel_id=1, source_target_pairs={{0,8},{8,16},{16,24},{24,32},{32,40},{40,48},{48,56},{56,64},{64,7... | collective-permute-start | bytes 6291464 | tf_op jit(solution)/shard_map/ppermute | solution.py:27
  22.7 21.8 %collective-permute-done = f32[8,128,512]{2,1,0:T(8,128)S(1)} collective-permute-done((f32[8,128,512]{2,1,0:T(8,128)S(1)}, f32[8,128,512]{2,1,0:T(8,128)S(1)}, u32[]{:S(2)}, u32[]{:S(2)}) %collective-permute-start) | collective-permute-done | bytes 2097184 | tf_op jit(solution)/shard_map/ppermute | solution.py:27
  44.5 1.2 collective-permute-done.1
  45.7 0.8 add_add_fusion
  46.4 57.2 %all_to_all.5 = f32[8,128,512]{2,1,0:T(8,128)S(1)} all-to-all(f32[8,128,512]{2,1,0:T(8,128)S(1)} %add_add_fusion), channel_id=1, replica_groups=mesh['grid'=96,'mesh'=8] {'mesh'}, dimensions={0} | all-to-all | bytes 4194304 | tf_op jit(solution)/shard_map/all_to_all | solution.py:85
  104.5 2.0 fusion.3
  106.6 38.7 %all-gather.3.cloned.1.call-done = bf16[1024,512]{1,0:T(8,128)(2,1)} async-done(((bf16[128,512]{1,0:T(8,128)(2,1)}), bf16[1024,512]{1,0:T(8,128)(2,1)}) %all-gather.3.cloned.1.call-update) | async-done | bytes 1048592 | tf_op jit(solution)/shard_map/all_gather | solution.py:39
  145.3 8.9 %collective-permute-start.2 = (bf16[1,1024,512]{2,1,0:T(8,128)(2,1)}, bf16[1,1024,512]{2,1,0:T(8,128)(2,1)}, u32[]{:S(2)}, u32[]{:S(2)}) collective-permute-start(bf16[1,1024,512]{2,1,0:T(8,128)(2,1)} %bitcast.24), channel_id=1, source_target_pairs={{0,8},{8,16},{16,24},{24,32},{32,40},{40,48},{48,56},{56,64},{64,7... | collective-permute-start | bytes 3145736 | tf_op jit(solution)/shard_map/ppermute | solution.py:15
  154.3 1.9 collective-permute-start.3
  156.3 1.1 fusion.38
  157.4 3.5 %gather_fusion.2 = f32[1024,512]{1,0:T(8,128)S(1)} fusion(f32[128,512]{1,0:T(8,128)S(1)} %fusion.38, s32[1024]{0:T(1024)S(1)} %fusion.29), kind=kCustom, calls=%fused_computation.2 | custom fusion | bytes 4198400 | tf_op jit(solution)/shard_map/gather | solution.py:93
  160.9 5.4 %collective-permute-done.2 = bf16[1,1024,512]{2,1,0:T(8,128)(2,1)} collective-permute-done((bf16[1,1024,512]{2,1,0:T(8,128)(2,1)}, bf16[1,1024,512]{2,1,0:T(8,128)(2,1)}, u32[]{:S(2)}, u32[]{:S(2)}) %collective-permute-start.2) | collective-permute-done | bytes 1048608 | tf_op jit(solution)/shard_map/ppermute | solution.py:15
  166.3 7.7 %collective-permute-done.3 = bf16[1,1024,512]{2,1,0:T(8,128)(2,1)} collective-permute-done((bf16[1,1024,512]{2,1,0:T(8,128)(2,1)}, bf16[1,1024,512]{2,1,0:T(8,128)(2,1)}, u32[]{:S(2)}, u32[]{:S(2)}) %collective-permute-start.3) | collective-permute-done | bytes 1048608 | tf_op jit(solution)/shard_map/ppermute | solution.py:17
  174.0 3.9 %pad_maximum_fusion = bf16[3,1024,512]{2,1,0:T(8,128)(2,1)} fusion(bf16[1,1024,512]{2,1,0:T(8,128)(2,1)} %collective-permute-done.3, bf16[1,1024,512]{2,1,0:T(8,128)(2,1)} %bitcast.26, bf16[1,1024,512]{2,1,0:T(8,128)(2,1)} %collective-permute-done.2), kind=kLoop, calls=%fused_computation.6 | loop fusion | flops 3145728 | bytes 6291456 | tf_op jit(solution)/shard_map/concatenate | solution.py:13
  177.9 7.5 %gather_fusion.1 = bf16[1024,512]{1,0:T(8,128)(2,1)} fusion(bf16[3072,512]{1,0:T(8,128)(2,1)} %bitcast.19, s32[1024]{0:T(1024)S(1)} %fusion.22), kind=kCustom, calls=%fused_computation.1 | custom fusion | bytes 2101248 | tf_op jit(solution)/shard_map/gather | solution.py:92
  185.3 3.2 %multiply_reduce_fusion.1 = (f32[128]{0:T(128)S(1)}, f32[128,512]{1,0:T(8,128)}) fusion(f32[1024,512]{1,0:T(8,128)S(1)} %gather_fusion.2, bf16[1024,512]{1,0:T(8,128)(2,1)} %gather_fusion.1, bf16[512,512]{1,0:T(8,128)(2,1)S(1)} %copy-done.9, f32[1024]{0:T(1024)S(1)} %and_convert_fusion.1, s32[1024]{0:T(1024)S(1)} %copy-done.8), kind=kOutput, calls=%fused_computation.35 | convolution fusion | flops 675020672 | bytes 3940864 | tf_op jit(solution)/shard_map/dot_general | solution.py:97
  188.5 2.4 multiply_convert_fusion.10
  191.0 35.8 %all-gather.5.cloned.1.call-done = bf16[1024,512]{1,0:T(8,128)(2,1)} async-done(((bf16[128,512]{1,0:T(8,128)(2,1)}), bf16[1024,512]{1,0:T(8,128)(2,1)}) %all-gather.5.cloned.1.call-update) | async-done | bytes 1048592 | tf_op jit(solution)/shard_map/all_gather | solution.py:39
  226.8 8.9 %collective-permute-start.4 = (bf16[1,1024,512]{2,1,0:T(8,128)(2,1)}, bf16[1,1024,512]{2,1,0:T(8,128)(2,1)S(1)}, u32[]{:S(2)}, u32[]{:S(2)}) collective-permute-start(bf16[1,1024,512]{2,1,0:T(8,128)(2,1)} %bitcast.27), channel_id=1, source_target_pairs={{0,8},{8,16},{16,24},{24,32},{32,40},{40,48},{48,56},{56,64},{64,7... | collective-permute-start | bytes 3145736 | tf_op jit(solution)/shard_map/ppermute | solution.py:15
  235.7 1.9 collective-permute-start.5
  237.7 10.1 %collective-permute-done.4 = bf16[1,1024,512]{2,1,0:T(8,128)(2,1)S(1)} collective-permute-done((bf16[1,1024,512]{2,1,0:T(8,128)(2,1)}, bf16[1,1024,512]{2,1,0:T(8,128)(2,1)S(1)}, u32[]{:S(2)}, u32[]{:S(2)}) %collective-permute-start.4) | collective-permute-done | bytes 1048608 | tf_op jit(solution)/shard_map/ppermute | solution.py:15
  247.7 7.6 %collective-permute-done.5 = bf16[1,1024,512]{2,1,0:T(8,128)(2,1)S(1)} collective-permute-done((bf16[1,1024,512]{2,1,0:T(8,128)(2,1)}, bf16[1,1024,512]{2,1,0:T(8,128)(2,1)S(1)}, u32[]{:S(2)}, u32[]{:S(2)}) %collective-permute-start.5) | collective-permute-done | bytes 1048608 | tf_op jit(solution)/shard_map/ppermute | solution.py:17
  255.4 3.2 %pad_maximum_fusion.1 = bf16[3,1024,512]{2,1,0:T(8,128)(2,1)} fusion(bf16[1,1024,512]{2,1,0:T(8,128)(2,1)S(1)} %collective-permute-done.5, bf16[1,1024,512]{2,1,0:T(8,128)(2,1)} %bitcast.29, bf16[1,1024,512]{2,1,0:T(8,128)(2,1)S(1)} %collective-permute-done.4), kind=kLoop, calls=%fused_computation.7 | loop fusion | flops 3145728 | bytes 6291456 | tf_op jit(solution)/shard_map/concatenate | solution.py:13
  258.6 5.0 %gather_fusion.3 = bf16[768,512]{1,0:T(8,128)(2,1)S(1)} fusion(bf16[3072,512]{1,0:T(8,128)(2,1)} %bitcast.20, s32[1024]{0:T(1024)S(1)} %pad_clamp_fusion), kind=kCustom, calls=%fused_computation.3 | custom fusion | bytes 1575936 | tf_op jit(solution)/shard_map/gather | solution.py:109
  263.6 0.5 multiply_reduce_fusion
  264.2 1.0 fusion.5
  (42 shorter events, 1.4 us)
Async XLA Ops:
  6.5 1.1 copy-start
  6.5 138.8 %all-gather.3.cloned.1.call-start = ((), (), s32[]{:S(2)}) async-start(), calls=%async_computation.1 | async-start | bytes 1179648 | tf_op jit(solution)/shard_map/all_gather | solution.py:39
  9.2 2.1 copy-start.7
  13.8 30.7 %collective-permute-start = (f32[8,128,512]{2,1,0:T(8,128)S(1)}, f32[8,128,512]{2,1,0:T(8,128)S(1)}, u32[]{:S(2)}, u32[]{:S(2)}) collective-permute-start(f32[8,128,512]{2,1,0:T(8,128)S(1)} %bitcast.23), channel_id=1, source_target_pairs={{8,0},{16,8},{24,16},{32,24},{40,32},{48,40},{56,48},{64,56},{72,6... | collective-permute-start | bytes 6291464 | tf_op jit(solution)/shard_map/ppermute | solution.py:27
  16.4 29.3 %collective-permute-start.1 = (f32[8,128,512]{2,1,0:T(8,128)S(1)}, f32[8,128,512]{2,1,0:T(8,128)S(1)}, u32[]{:S(2)}, u32[]{:S(2)}) collective-permute-start(f32[8,128,512]{2,1,0:T(8,128)S(1)} %bitcast.22), channel_id=1, source_target_pairs={{0,8},{8,16},{16,24},{24,32},{32,40},{40,48},{48,56},{56,64},{64,7... | collective-permute-start | bytes 6291464 | tf_op jit(solution)/shard_map/ppermute | solution.py:27
  103.6 0.9 copy-start.10
  103.6 0.9 copy-start.12
  103.6 52.6 %copy-start.5 = (s32[1024]{0:T(1024)S(1)}, s32[1024]{0:T(1024)}, u32[]{:S(2)}) copy-start(s32[1024]{0:T(1024)} %param.30) | copy-start | bytes 12292
  103.6 52.6 %copy-start.8 = (s32[1024]{0:T(1024)S(1)}, s32[1024]{0:T(1024)}, u32[]{:S(2)}) copy-start(s32[1024]{0:T(1024)} %param.31) | copy-start | bytes 12292
  103.6 52.6 %copy-start.1 = (bf16[512,512]{1,0:T(8,128)(2,1)S(1)}, bf16[512,512]{1,0:T(8,128)(2,1)}, u32[]{:S(2)}) copy-start(bf16[512,512]{1,0:T(8,128)(2,1)} %param.24) | copy-start | bytes 1572868
  106.6 120.2 %all-gather.5.cloned.1.call-start = ((), (), s32[]{:S(2)}) async-start(), calls=%async_computation.2 | async-start | bytes 1179648 | tf_op jit(solution)/shard_map/all_gather | solution.py:39
  145.3 21.0 %collective-permute-start.2 = (bf16[1,1024,512]{2,1,0:T(8,128)(2,1)}, bf16[1,1024,512]{2,1,0:T(8,128)(2,1)}, u32[]{:S(2)}, u32[]{:S(2)}) collective-permute-start(bf16[1,1024,512]{2,1,0:T(8,128)(2,1)} %bitcast.24), channel_id=1, source_target_pairs={{0,8},{8,16},{16,24},{24,32},{32,40},{40,48},{48,56},{56,64},{64,7... | collective-permute-start | bytes 3145736 | tf_op jit(solution)/shard_map/ppermute | solution.py:15
  154.3 19.8 %collective-permute-start.3 = (bf16[1,1024,512]{2,1,0:T(8,128)(2,1)}, bf16[1,1024,512]{2,1,0:T(8,128)(2,1)}, u32[]{:S(2)}, u32[]{:S(2)}) collective-permute-start(bf16[1,1024,512]{2,1,0:T(8,128)(2,1)} %bitcast.25), channel_id=1, source_target_pairs={{8,0},{16,8},{24,16},{32,24},{40,32},{48,40},{56,48},{64,56},{72,6... | collective-permute-start | bytes 3145736 | tf_op jit(solution)/shard_map/ppermute | solution.py:17
  177.9 7.5 %copy-start.9 = (bf16[512,512]{1,0:T(8,128)(2,1)S(1)}, bf16[512,512]{1,0:T(8,128)(2,1)}, u32[]{:S(2)}) copy-start(bf16[512,512]{1,0:T(8,128)(2,1)} %param.23) | copy-start | bytes 1572868
  185.3 3.2 %copy-start.2 = (bf16[128,512]{1,0:T(8,128)(2,1)S(1)}, bf16[128,512]{1,0:T(8,128)(2,1)}, u32[]{:S(2)}) copy-start(bf16[128,512]{1,0:T(8,128)(2,1)} %fusion.3) | copy-start | bytes 393220
  188.5 49.1 %copy-start.6 = (s32[768]{0:T(1024)S(1)}, s32[768]{0:T(1024)}, u32[]{:S(2)}) copy-start(s32[768]{0:T(1024)} %param.32) | copy-start | bytes 9220
  226.8 21.0 %collective-permute-start.4 = (bf16[1,1024,512]{2,1,0:T(8,128)(2,1)}, bf16[1,1024,512]{2,1,0:T(8,128)(2,1)S(1)}, u32[]{:S(2)}, u32[]{:S(2)}) collective-permute-start(bf16[1,1024,512]{2,1,0:T(8,128)(2,1)} %bitcast.27), channel_id=1, source_target_pairs={{0,8},{8,16},{16,24},{24,32},{32,40},{40,48},{48,56},{56,64},{64,7... | collective-permute-start | bytes 3145736 | tf_op jit(solution)/shard_map/ppermute | solution.py:15
  235.7 19.6 %collective-permute-start.5 = (bf16[1,1024,512]{2,1,0:T(8,128)(2,1)}, bf16[1,1024,512]{2,1,0:T(8,128)(2,1)S(1)}, u32[]{:S(2)}, u32[]{:S(2)}) collective-permute-start(bf16[1,1024,512]{2,1,0:T(8,128)(2,1)} %bitcast.28), channel_id=1, source_target_pairs={{8,0},{16,8},{24,16},{32,24},{40,32},{48,40},{56,48},{64,56},{72,6... | collective-permute-start | bytes 3145736 | tf_op jit(solution)/shard_map/ppermute | solution.py:17
  258.6 5.1 %copy-start.11 = (s32[768]{0:T(1024)S(1)}, s32[768]{0:T(1024)}, u32[]{:S(2)}) copy-start(s32[768]{0:T(1024)} %param.33) | copy-start | bytes 9220
  258.6 5.6 %copy-start.3 = (bf16[512,227]{0,1:T(8,128)(2,1)S(1)}, bf16[512,227]{0,1:T(8,128)(2,1)}, u32[]{:S(2)}) copy-start(bf16[512,227]{0,1:T(8,128)(2,1)} %param.27) | copy-start | bytes 697348
  258.6 5.6 %copy-start.4 = (bf16[256,227]{0,1:T(8,128)(2,1)S(1)}, bf16[256,227]{0,1:T(8,128)(2,1)}, u32[]{:S(2)}) copy-start(bf16[256,227]{0,1:T(8,128)(2,1)} %param.17) | copy-start | bytes 348676
Sparse Core Ops, SparseCore 0:
  106.7 38.5 all-gather.2
  191.1 35.5 all-gather.4
where the time goes:
time: 273 us; the launch traced here: 272 us
  waiting for transfers between devices  128 us (47%)
  blocking collectives  57.2 us (21%)
  starting transfers between devices  30.7 us (11%)
  local copies, waits for them, and re-layouts  19.7 us (7%)
  matrix products  13.7 us (5%)
  between operations  13.7 us (5%)
  other arithmetic  8.96 us (3%)
    all_gather x2, waiting for transfers between devices, nearby_rows(): gathered = lax.all_gather(node_rows, 'mesh', axis=0, tiled=True)  74.5 us
    all_to_all x1, blocking collectives, shards(): lax.all_to_all(banded, 'mesh', split_axis=0, concat_axis=0, tiled=True)  57.2 us
    ppermute x2, waiting for transfers between devices, passed_along(): return lax.ppermute(block, axis, route)  23 us
    ppermute x2, starting transfers between devices, padded(): lax.ppermute(tail, axis, [(i, (i + 1) % count) for i in range(ends)])  17.9 us
    ppermute x2, waiting for transfers between devices, padded(): lax.ppermute(tail, axis, [(i, (i + 1) % count) for i in range(ends)])  15.4 us
    ppermute x2, waiting for transfers between devices, padded(): lax.ppermute(head, axis, [((i + 1) % count, i) for i in range(ends)])  15.3 us
    ppermute x2, starting transfers between devices, passed_along(): return lax.ppermute(block, axis, route)  8.88 us
    gather x1, local copies, waits for them, and re-layouts, shards(): nearby_one[proc_src]  7.47 us
  transfers between devices with their start and end apart: 8, of which 8 were waited for; matrix products, arithmetic and copies ran while one was open for 2% of the time, Pallas kernels for 0%

commit v1 on v0

v1 whole, which is shorter than its diff:
```python
import functools

import jax
import jax.numpy as jnp
from jax import lax
from jax.experimental import pallas as pl
from jax.experimental.pallas import tpu as pltpu
from jax.sharding import PartitionSpec as P

LANES = 128
VMEM_BYTES = 56 * 1024 * 1024


def silu(v):
    return v * (0.5 + 0.5 * jnp.tanh(0.5 * v))


def rms(v):
    return v * lax.rsqrt(jnp.mean(v * v, axis=-1, keepdims=True) + 1e-05)


def mm(a, b):
    return jnp.dot(a, b, preferred_element_type=jnp.float32)


def mm_nt(a, b):
    return lax.dot_general(a, b, (((1,), (1,)), ((), ())), preferred_element_type=jnp.float32)


def hot_by_row(keys, count):
    spots = lax.broadcasted_iota(jnp.int32, (count, keys.shape[1]), 0)
    return jnp.where(spots == keys, 1.0, 0.0).astype(jnp.bfloat16)


def columns_of(row):
    return jnp.transpose(jnp.broadcast_to(row, (LANES, LANES)))


def hot_by_column(spread, count):
    lanes = lax.broadcasted_iota(jnp.int32, (LANES, LANES), 1)
    parts = [
        jnp.where(spread == lanes + LANES * k, 1.0, 0.0).astype(jnp.bfloat16)
        for k in range(count // LANES)
    ]
    return jnp.concatenate(parts, axis=1)


def band_sums(pick, buf, w_embed, w_send, out, rows, edges):
    grid_rows = rows - 16
    chunks = edges // LANES
    nodes = out.shape[0]
    patches = buf.shape[0] // rows

    def device(s, carry):
        base = pl.multiple_of(s * rows, 16)
        lat = silu(mm(buf[pl.ds(base, grid_rows), :], w_embed[...])).astype(jnp.bfloat16)
        sent = silu(mm(lat, w_send[...])).astype(jnp.bfloat16)
        notes = buf[pl.ds(pl.multiple_of(base + grid_rows, 16), 16), :LANES]
        notes = notes.astype(jnp.float32).astype(jnp.int32)
        src = notes[0:chunks]
        high = notes[chunks : 2 * chunks]
        low = notes[2 * chunks : 3 * chunks]
        key = jnp.where(
            high // patches == pick, (high % patches) * LANES + low, -1
        )
        to = jnp.concatenate([hot_by_row(key[j : j + 1], nodes) for j in range(chunks)], axis=1)
        frm = jnp.concatenate([hot_by_row(src[j : j + 1], grid_rows) for j in range(chunks)], axis=1)
        counts = mm_nt(to, frm).astype(jnp.bfloat16)
        out[...] += mm(counts, sent)
        return carry

    lax.fori_loop(0, patches, device, 0)


def enc_first(pick, buf, w_embed, w_send, out, *, rows, edges):
    out[...] = jnp.zeros_like(out)
    band_sums(pick[0], buf, w_embed, w_send, out, rows, edges)


def enc_more(pick, buf, w_embed, w_send, acc, out, *, rows, edges):
    out[...] = acc[...]
    band_sums(pick[0], buf, w_embed, w_send, out, rows, edges)


def enc_last(pick, buf, w_embed, w_send, acc, init, gain, w_node, out, total, *, rows, edges):
    total[...] = acc[...]
    band_sums(pick[0], buf, w_embed, w_send, total, rows, edges)
    step = 256

    def block(i, carry):
        here = pl.ds(pl.multiple_of(i * step, step), step)
        node_in = silu(rms(total[here, :]) * gain[...]).astype(jnp.bfloat16)
        fresh = init[here, :].astype(jnp.float32) + mm(node_in, w_node[...])
        out[here, :] = fresh.astype(jnp.bfloat16)
        return carry

    lax.fori_loop(0, out.shape[0] // step, block, 0)


def picked_rows(pick, src, nodes, put):
    count = nodes.shape[0]
    for j in range(src.shape[0]):
        code = src[j : j + 1, :]
        key = jnp.where(code // count == pick, code % count, -1)
        put(j, mm(hot_by_column(columns_of(key), count), nodes[...]))


def proc_first(pick, src, nodes, out):
    def put(j, rows):
        out[LANES * j : LANES * (j + 1), :] = rows.astype(jnp.bfloat16)

    picked_rows(pick[0], src, nodes, put)


def proc_more(pick, src, nodes, acc, out):
    def put(j, rows):
        at = slice(LANES * j, LANES * (j + 1))
        out[at, :] = acc[at, :] + rows.astype(jnp.bfloat16)

    picked_rows(pick[0], src, nodes, put)


def proc_last(
    pick, src, dst, nodes, acc, own, w_ps, w_pr, w_po, w_ds, out, *, last_band, band_nodes
):
    recv = mm(own[...], w_pr[...])
    top = recv.astype(jnp.bfloat16)
    rest = (recv - top.astype(jnp.float32)).astype(jnp.bfloat16)
    recv_pair = jnp.concatenate([top, rest], axis=0)
    total = jnp.zeros(own.shape, jnp.float32)
    count = nodes.shape[0]
    band = pick[1]
    for j in range(src.shape[0]):
        at = slice(LANES * j, LANES * (j + 1))
        code = src[j : j + 1, :]
        to = dst[j : j + 1, :]
        key = jnp.where(code // count == pick[0], code % count, -1)
        rows = mm(hot_by_column(columns_of(key), count), nodes[...]).astype(jnp.bfloat16)
        rows = acc[at, :] + rows
        one = hot_by_column(columns_of(to), LANES)
        recv_rows = mm(jnp.concatenate([one, one], axis=1), recv_pair)
        msg = silu(mm(rows, w_ps[...]) + recv_rows).astype(jnp.bfloat16)
        target = band + code // band_nodes - 1
        valid = (target >= 0) & (target <= last_band)
        total += mm(hot_by_row(jnp.where(valid, to, -1), LANES), msg)
    norm = rms(total).astype(jnp.bfloat16)
    two = (own[...].astype(jnp.float32) + mm(norm, w_po[...])).astype(jnp.bfloat16)
    out[...] = silu(mm(two, w_ds[...])).astype(jnp.bfloat16)


def dec_counts(keys, dst, out):
    chunks = dst.shape[0]
    grid_rows = out.shape[0]
    nodes = out.shape[1] // 3
    to = jnp.concatenate([hot_by_row(dst[j : j + 1, :], grid_rows) for j in range(chunks)], axis=1)
    half = nodes // 2
    for k in range(6):
        first = (k // 2) * chunks
        frm = jnp.concatenate(
            [
                hot_by_row(keys[first + j : first + j + 1, :] - (k % 2) * half, half)
                for j in range(chunks)
            ],
            axis=1,
        )
        out[:, k * half : (k + 1) * half] = mm_nt(to, frm).astype(jnp.bfloat16)


def dec_last(counts, a, b, c, d, e, f, grid_vars, w_out, out):
    half = a.shape[0]
    total = jnp.zeros((counts.shape[0], a.shape[1]), jnp.float32)
    for k, part in enumerate((a, b, c, d, e, f)):
        total += mm(counts[:, k * half : (k + 1) * half], part[...])
    norm = rms(total).astype(jnp.bfloat16)
    out[...] = (grid_vars[...].astype(jnp.float32) + mm(norm, w_out[...])).astype(jnp.bfloat16)


def call(body, out, *args, scalars=0, scratch=(), flops=0, **static):
    vmem = pl.BlockSpec(memory_space=pltpu.VMEM)
    smem = pl.BlockSpec(memory_space=pltpu.SMEM)
    moved = sum(a.size * a.dtype.itemsize for a in args) + out.size * out.dtype.itemsize
    return pl.pallas_call(
        functools.partial(body, **static),
        out_shape=out,
        in_specs=[smem] * scalars + [vmem] * (len(args) - scalars),
        out_specs=vmem,
        scratch_shapes=list(scratch),
        compiler_params=pltpu.CompilerParams(vmem_limit_bytes=VMEM_BYTES),
        cost_estimate=pl.CostEstimate(flops=flops, bytes_accessed=moved, transcendentals=0),
        name=body.__name__,
    )(*args)


def pair_groups(bands, patches, step):
    groups = []
    for b in range(bands):
        for p in range(patches):
            if (p + b) % 2 == 0:
                q = (p + 1) % patches if step == 0 else (p - 1) % patches
                groups.append([b * patches + p, b * patches + q])
    return groups


def shards(
    bands,
    patches,
    grid_vars,
    mesh_init,
    w_embed,
    w_send,
    w_node,
    node_gain,
    w_proc_send,
    w_proc_recv,
    w_proc_out,
    w_dec_send,
    w_dec_out,
    enc_src,
    enc_dst,
    proc_src,
    proc_dst,
    dec_src,
    dec_dst,
):
    f32, bf16 = jnp.float32, jnp.bfloat16
    shape = jax.ShapeDtypeStruct
    mine, width = mesh_init.shape
    band_nodes = patches * mine
    grid_rows, columns = grid_vars.shape
    edges = enc_src.shape[0]
    chunks = edges // LANES
    band = lax.axis_index("grid").astype(jnp.int32)
    patch = lax.axis_index("mesh").astype(jnp.int32)
    odd = band % 2
    far = 2 * odd
    near = 2 - far
    far_pairs = [(i, i + 1) for i in range(1, bands - 1, 2)]
    far_pairs += [(j, i) for i, j in far_pairs]
    near_pairs = [(i, i + 1) for i in range(0, bands - 1, 2)]
    near_pairs += [(j, i) for i, j in near_pairs]

    def over_far(block):
        return lax.ppermute(block, "grid", far_pairs)

    def over_near(block):
        return lax.ppermute(block, "grid", near_pairs)

    init_band = lax.all_gather(mesh_init, "mesh", axis=0, tiled=True)

    notes = jnp.concatenate([enc_src, enc_dst // LANES, enc_dst % LANES]).reshape(3 * chunks, LANES)
    notes = jnp.pad(notes.astype(bf16), ((0, 16 - 3 * chunks), (0, columns - LANES)))
    load = jnp.concatenate([grid_vars, notes], axis=0)
    rows = grid_rows + 16
    own = lax.all_gather(load, "mesh", axis=0, tiled=True)
    far_load = over_far(own)
    near_load = over_near(own)

    def scalar(v):
        return jnp.reshape(v, (1,)).astype(jnp.int32)

    enc_flops = 2 * patches * (
        grid_rows * width * (2 * LANES + width)
        + band_nodes * grid_rows * (edges + width)
    )
    acc_shape = shape((band_nodes, width), f32)
    enc = dict(rows=rows, edges=edges, scalars=1, flops=enc_flops)
    acc = call(enc_first, acc_shape, scalar(1), own, w_embed, w_send, **enc)
    acc = call(enc_more, acc_shape, scalar(2 - near), near_load, w_embed, w_send, acc, **enc)
    one = call(
        enc_last,
        shape((band_nodes, width), bf16),
        scalar(2 - far),
        far_load,
        w_embed,
        w_send,
        acc,
        init_band,
        node_gain.reshape(1, width),
        w_node,
        scratch=[pltpu.VMEM((band_nodes, width), f32)],
        **enc,
    )

    far_one = over_far(one)
    near_one = over_near(one)
    own_one = lax.dynamic_slice_in_dim(one, patch * mine, mine, 0)
    src = proc_src.reshape(-1, LANES)
    dst = proc_dst.reshape(-1, LANES)
    proc_edges = proc_src.shape[0]
    pick_flops = 2 * proc_edges * band_nodes * width
    pick_shape = shape((proc_edges, width), bf16)
    got = call(proc_first, pick_shape, scalar(1), src, one, scalars=1, flops=pick_flops)

    code_band = dec_src // band_nodes
    block = (dec_src // mine) % patches
    within = dec_src % mine
    dec_keys = []
    for wanted, parity in ((1, 0), (near, 1), (far, 1)):
        second = (patch + band + parity) % 2
        rel = (block - patch) * (1 - 2 * second)
        turn = (rel + 2) % patches
        spot = jnp.where(turn < 4, turn ^ 2, turn) ^ (3 * second)
        dec_keys.append(jnp.where(code_band == wanted, spot * mine + within, -band_nodes))
    dec_keys = jnp.concatenate(dec_keys).reshape(-1, LANES)
    dec_edges = dec_src.shape[0]
    counts = call(
        dec_counts,
        shape((grid_rows, 3 * band_nodes), bf16),
        dec_keys,
        dec_dst.reshape(-1, LANES),
        flops=6 * grid_rows * band_nodes * dec_edges,
    )

    got = call(proc_more, pick_shape, scalar(near), src, near_one, got, scalars=1, flops=pick_flops)
    sent = call(
        proc_last,
        shape((mine, width), bf16),
        jnp.stack([far, band]).astype(jnp.int32),
        src,
        dst,
        far_one,
        got,
        own_one,
        w_proc_send,
        w_proc_recv,
        w_proc_out,
        w_dec_send,
        scalars=1,
        flops=pick_flops + 2 * proc_edges * width * (width + 3 * LANES),
        last_band=bands - 1,
        band_nodes=band_nodes,
    )

    groups = [pair_groups(bands, patches, step) for step in (0, 1)]

    def meet(rows_here, step):
        return lax.all_gather(
            rows_here, ("grid", "mesh"), axis=0, tiled=True, axis_index_groups=groups[step]
        )

    second = (patch + band) % 2

    def partner_half(both):
        size = both.shape[0] // 2
        return lax.dynamic_slice_in_dim(both, (1 - second) * size, size, 0)

    four = meet(meet(sent, 0), 1)
    far_four = over_far(four)
    near_four = over_near(four)
    rest = meet(partner_half(meet(partner_half(four), 0)), 1)
    far_rest = over_far(rest)
    near_rest = over_near(rest)
    return call(
        dec_last,
        shape((grid_rows, columns), bf16),
        counts,
        four,
        rest,
        near_four,
        near_rest,
        far_four,
        far_rest,
        grid_vars,
        w_dec_out,
        flops=6 * grid_rows * band_nodes * width,
    )


def solution(mesh):
    spread = P(("grid", "mesh"), None)
    edge = P(("grid", "mesh"))
    in_specs = (spread, spread) + (P(),) * 9 + (edge,) * 6
    body = functools.partial(shards, mesh.shape["grid"], mesh.shape["mesh"])
    return jax.shard_map(body, mesh=mesh, in_specs=in_specs, out_specs=spread, check_vma=False)
```

time: 273 us -> 196 us (0.72)
  the two profiles are of different devices: /device:TPU:199 before, /device:TPU:7 now
where the time goes in v1:
time: 196 us
  Pallas kernels  68.6 us (35%)
  blocking collectives  49 us (25%)
  starting transfers between devices  39.6 us (20%)
  between operations  13.7 us (7%)
  local copies, waits for them, and re-layouts  12.7 us (6%)
  waiting for transfers between devices  10.1 us (5%)
  other arithmetic  2.11 us (1%)
    pallas_call x8, Pallas kernels, call(): pl.pallas_call(functools.partial(body, **static), out_shape=out, in_specs...  68.6 us
    all_gather x4, blocking collectives, meet(): lax.all_gather(rows_here, ('grid', 'mesh'), axis=0, tiled=True, axis_inde...  25.7 us
    ppermute x4, starting transfers between devices, over_near(): return lax.ppermute(block, 'grid', near_pairs)  24.3 us
    all_gather x1, blocking collectives, shards(): own = lax.all_gather(load, 'mesh', axis=0, tiled=True)  23.3 us
    ppermute x4, starting transfers between devices, over_far(): return lax.ppermute(block, 'grid', far_pairs)  15.4 us
    ppermute x4, waiting for transfers between devices, over_far(): return lax.ppermute(block, 'grid', far_pairs)  9.4 us
    unnamed x26, local copies, waits for them, and re-layouts  4.59 us
  transfers between devices with their start and end apart: 9, of which 2 were waited for; matrix products, arithmetic and copies ran while one was open for 5% of the time, Pallas kernels for 20%

profile of v1, /device:TPU:7, one launch (start us, length us, event | category | flops | bytes accessed | tf_op | source)
XLA Modules:
  0.0 195.7 jit_solution(11558795406718118843)
XLA Ops:
  7.3 1.0 copy.22.grid_vars
  9.1 23.3 %all_gather.18.buf = bf16[2176,227]{1,0:T(8,128)(2,1)S(1)} all-gather(bf16[272,227]{1,0:T(8,128)(2,1)S(1)} %pad_maximum_fusion), channel_id=1, replica_groups=mesh['grid'=96,'mesh'=8] {'mesh'}, dimensions={0}, use_global_device_ids=true | all-gather | bytes 1111392 | tf_op jit(solution)/shard_map/all_gather | solution.py:254
  32.3 0.9 copy.23
  33.3 8.2 %collective-permute-start.1 = (bf16[2176,227]{0,1:T(8,128)(2,1)S(1)}, bf16[2176,227]{0,1:T(8,128)(2,1)}, u32[]{:S(2)}, u32[]{:S(2)}) collective-permute-start(bf16[2176,227]{0,1:T(8,128)(2,1)S(1)} %copy.23), channel_id=1, source_target_pairs={{0,8},{16,24},{32,40},{48,56},{64,72},{80,88},{96,104},{112,120},{... | collective-permute-start | bytes 2963720 | tf_op jit(solution)/shard_map/ppermute | solution.py:246
  41.4 3.7 %collective-permute-start = (bf16[2176,227]{0,1:T(8,128)(2,1)S(1)}, bf16[2176,227]{0,1:T(8,128)(2,1)S(1)}, u32[]{:S(2)}, u32[]{:S(2)}) collective-permute-start(bf16[2176,227]{0,1:T(8,128)(2,1)S(1)} %copy.23), channel_id=1, source_target_pairs={{8,16},{24,32},{40,48},{56,64},{72,80},{88,96},{104,112},{120,128}... | collective-permute-start | bytes 2963720 | tf_op jit(solution)/shard_map/ppermute | solution.py:243
  45.2 14.2 %enc_first.1.acc = f32[1024,512]{1,0:T(8,128)} custom-call(s32[1]{0:T(128)} %constant.126.clone.1.pick, bf16[2176,227]{1,0:T(8,128)(2,1)} %copy-done, bf16[227,512]{1,0:T(8,128)(2,1)} %w_embed.5, bf16[512,512]{1,0:T(8,128)(2,1)} %w_send.5), custom_call_target="tpu_custom_call" | custom-call | flops 5368709120 | bytes 3841796 | tf_op jit(solution)/shard_map/enc_first/pallas_call | solution.py:182
  59.4 2.4 %copy.25.buf = bf16[2176,227]{1,0:T(8,128)(2,1)} copy(bf16[2176,227]{0,1:T(8,128)(2,1)} %collective-permute-done.1) | data formatting | bytes 1975808 | tf_op jit(solution)/shard_map/ppermute | solution.py:246
  61.8 1.5 copy.26.buf
  63.3 14.9 %enc_more.1.acc = f32[1024,512]{1,0:T(8,128)} custom-call(s32[1]{0:T(128)} %bitcast.4.pick, bf16[2176,227]{1,0:T(8,128)(2,1)} %copy.25.buf, bf16[227,512]{1,0:T(8,128)(2,1)} %w_embed.5, bf16[512,512]{1,0:T(8,128)(2,1)} %w_send.5, f32[1024,512]{1,0:T(8,128)} %enc_first.1.acc), custom_call_target="tpu_custom_call" | custom-call | flops 5368709120 | bytes 5938948 | tf_op jit(solution)/shard_map/enc_more/pallas_call | solution.py:182
  78.2 16.6 %enc_last.1.nodes = bf16[1024,512]{1,0:T(8,128)(2,1)} custom-call(s32[1]{0:T(128)} %bitcast.8.pick, bf16[2176,227]{1,0:T(8,128)(2,1)} %copy.26.buf, bf16[227,512]{1,0:T(8,128)(2,1)} %w_embed.5, bf16[512,512]{1,0:T(8,128)(2,1)} %w_send.5, f32[1024,512]{1,0:T(8,128)} %enc_more.1.acc, bf16[1024,512]{1,0:T(8,128)(2,1)} %all-gather.2.cloned.1.call-done.init, ...), custom_call_target="tpu_custom_call" | custom-call | flops 5368709120 | bytes 6465284 | tf_op jit(solution)/shard_map/enc_last/pallas_call | solution.py:182
  94.8 1.9 collective-permute-start.3
  96.8 4.0 %collective-permute-start.2 = (bf16[1024,512]{1,0:T(8,128)(2,1)}, bf16[1024,512]{1,0:T(8,128)(2,1)S(1)}, u32[]{:S(2)}, u32[]{:S(2)}) collective-permute-start(bf16[1024,512]{1,0:T(8,128)(2,1)} %enc_last.1.nodes), channel_id=1, source_target_pairs={{8,16},{24,32},{40,48},{56,64},{72,80},{88,96},{104,112},{120,128}... | collective-permute-start | bytes 3145736 | tf_op jit(solution)/shard_map/ppermute | solution.py:243
  101.4 3.6 %proc_first.1.acc = bf16[1024,512]{1,0:T(8,128)(2,1)} custom-call(s32[1]{0:T(128)} %constant.126.clone.1.pick, s32[8,128]{1,0:T(8,128)} %bitcast.19, bf16[1024,512]{1,0:T(8,128)(2,1)} %enc_last.1.nodes), custom_call_target="tpu_custom_call" | custom-call | flops 1073741824 | bytes 2101252 | tf_op jit(solution)/shard_map/proc_first/pallas_call | solution.py:182
  105.0 1.6 constant_dynamic-slice_fusion.2.own
  106.6 1.0 copy-done.11
  107.6 4.0 %proc_more.1.acc = bf16[1024,512]{1,0:T(8,128)(2,1)} custom-call(s32[1]{0:T(128)} %bitcast.8.pick, s32[8,128]{1,0:T(8,128)} %bitcast.20, bf16[1024,512]{1,0:T(8,128)(2,1)} %copy-done.11, bf16[1024,512]{1,0:T(8,128)(2,1)} %proc_first.1.acc), custom_call_target="tpu_custom_call" | custom-call | flops 1073741824 | bytes 3149828 | tf_op jit(solution)/shard_map/proc_more/pallas_call | solution.py:182
  111.6 3.6 %collective-permute-done.2.nodes = bf16[1024,512]{1,0:T(8,128)(2,1)S(1)} collective-permute-done((bf16[1024,512]{1,0:T(8,128)(2,1)}, bf16[1024,512]{1,0:T(8,128)(2,1)S(1)}, u32[]{:S(2)}, u32[]{:S(2)}) %collective-permute-start.2) | collective-permute-done | bytes 1048608 | tf_op jit(solution)/shard_map/ppermute | solution.py:243
  115.2 1.0 copy-done.10
  116.2 7.5 %proc_last.1 = bf16[128,512]{1,0:T(8,128)(2,1)} custom-call(s32[2]{0:T(128)} %pad_add_fusion.1.pick, s32[8,128]{1,0:T(8,128)} %bitcast.21, s32[8,128]{1,0:T(8,128)} %bitcast.22, bf16[1024,512]{1,0:T(8,128)(2,1)} %copy-done.10, bf16[1024,512]{1,0:T(8,128)(2,1)} %proc_more.1.acc, bf16[128,512]{1,0:T(8,128)(2,1)} %constant_dynamic-slice_fusion.2.own, ...), custom_call_target="tpu_custom_call" | custom-call | flops 2013265920 | bytes 4464648 | tf_op jit(solution)/shard_map/proc_last/pallas_call | solution.py:182
  123.7 6.1 %all_gather.20 = bf16[256,512]{1,0:T(8,128)(2,1)S(1)} all-gather(bf16[128,512]{1,0:T(8,128)(2,1)} %proc_last.1), channel_id=1, replica_groups={{0,1},{2,3},{4,5},{6,7},{9,10},{11,12},{13,14},{15,8},{16,17},{18,19},{..., dimensions={0}, use_global_device_ids=true | all-gather | bytes 393216 | tf_op jit(solution)/shard_map/all_gather | solution.py:337
  129.8 6.3 %all_gather.21.a = bf16[512,512]{1,0:T(8,128)(2,1)S(1)} all-gather(bf16[256,512]{1,0:T(8,128)(2,1)S(1)} %all_gather.20), channel_id=1, replica_groups={{0,7},{2,1},{4,3},{6,5},{9,8},{11,10},{13,12},{15,14},{16,23},{18,17},{..., dimensions={0}, use_global_device_ids=true | all-gather | bytes 786432 | tf_op jit(solution)/shard_map/all_gather | solution.py:337
  136.1 7.1 %all_gather.22 = bf16[512,512]{1,0:T(8,128)(2,1)S(1)} all-gather(bf16[256,512]{1,0:T(8,128)(2,1)S(1)} %constant_dynamic-slice_fusion.1), channel_id=1, replica_groups={{0,1},{2,3},{4,5},{6,7},{9,10},{11,12},{13,14},{15,8},{16,17},{18,19},{..., dimensions={0}, use_global_device_ids=true | all-gather | bytes 786432 | tf_op jit(solution)/shard_map/all_gather | solution.py:337
  143.2 6.2 %all_gather.23.b = bf16[512,512]{1,0:T(8,128)(2,1)S(1)} all-gather(bf16[256,512]{1,0:T(8,128)(2,1)S(1)} %constant_dynamic-slice_fusion), channel_id=1, replica_groups={{0,7},{2,1},{4,3},{6,5},{9,8},{11,10},{13,12},{15,14},{16,23},{18,17},{..., dimensions={0}, use_global_device_ids=true | all-gather | bytes 786432 | tf_op jit(solution)/shard_map/all_gather | solution.py:337
  149.4 4.3 %collective-permute-start.5 = (bf16[512,512]{1,0:T(8,128)(2,1)S(1)}, bf16[512,512]{1,0:T(8,128)(2,1)S(1)}, u32[]{:S(2)}, u32[]{:S(2)}) collective-permute-start(bf16[512,512]{1,0:T(8,128)(2,1)S(1)} %all_gather.23.b), channel_id=1, source_target_pairs={{0,8},{16,24},{32,40},{48,56},{64,72},{80,88},{96,104},{112,120},{... | collective-permute-start | bytes 1572872 | tf_op jit(solution)/shard_map/ppermute | solution.py:246
  153.7 5.8 %collective-permute-start.7 = (bf16[512,512]{1,0:T(8,128)(2,1)S(1)}, bf16[512,512]{1,0:T(8,128)(2,1)S(1)}, u32[]{:S(2)}, u32[]{:S(2)}) collective-permute-start(bf16[512,512]{1,0:T(8,128)(2,1)S(1)} %all_gather.23.b), channel_id=1, source_target_pairs={{8,16},{24,32},{40,48},{56,64},{72,80},{88,96},{104,112},{120,128}... | collective-permute-start | bytes 1572872 | tf_op jit(solution)/shard_map/ppermute | solution.py:243
  159.5 9.9 %collective-permute-start.4 = (bf16[512,512]{1,0:T(8,128)(2,1)S(1)}, bf16[512,512]{1,0:T(8,128)(2,1)S(1)}, u32[]{:S(2)}, u32[]{:S(2)}) collective-permute-start(bf16[512,512]{1,0:T(8,128)(2,1)S(1)} %all_gather.21.a), channel_id=1, source_target_pairs={{0,8},{16,24},{32,40},{48,56},{64,72},{80,88},{96,104},{112,120},{... | collective-permute-start | bytes 1572872 | tf_op jit(solution)/shard_map/ppermute | solution.py:246
  169.4 1.9 collective-permute-start.6
  171.4 0.8 copy.28.w_out
  172.9 3.3 %dec_counts.1.counts = bf16[256,3072]{1,0:T(8,128)(2,1)} custom-call(s32[18,128]{1,0:T(8,128)} %pad_add_fusion.keys, s32[6,128]{1,0:T(8,128)} %bitcast.23), custom_call_target="tpu_custom_call" | custom-call | flops 1207959552 | bytes 1585152 | tf_op jit(solution)/shard_map/dec_counts/pallas_call | solution.py:182
  176.3 5.8 %collective-permute-done.6.e = bf16[512,512]{1,0:T(8,128)(2,1)S(1)} collective-permute-done((bf16[512,512]{1,0:T(8,128)(2,1)S(1)}, bf16[512,512]{1,0:T(8,128)(2,1)S(1)}, u32[]{:S(2)}, u32[]{:S(2)}) %collective-permute-start.6) | collective-permute-done | bytes 524320 | tf_op jit(solution)/shard_map/ppermute | solution.py:243
  182.8 4.4 %dec_last.1 = bf16[256,227]{1,0:T(8,128)(2,1)} custom-call(bf16[256,3072]{1,0:T(8,128)(2,1)} %dec_counts.1.counts, bf16[512,512]{1,0:T(8,128)(2,1)} %copy-done.1, bf16[512,512]{1,0:T(8,128)(2,1)} %copy-done.2, bf16[512,512]{1,0:T(8,128)(2,1)} %copy-done.6, bf16[512,512]{1,0:T(8,128)(2,1)} %copy-done.4, bf16[512,512]{1,0:T(8,128)(2,1)} %copy-done.7, ...), custom_call_target="tpu_custom_call" | custom-call | flops 805306368 | bytes 5183488 | tf_op jit(solution)/shard_map/dec_last/pallas_call | solution.py:182
  187.2 1.7 copy.29
  (40 shorter events, 3.7 us)
Async XLA Ops:
  6.5 71.7 %all-gather.2.cloned.1.call-start = ((), (), s32[]{:S(2)}) async-start(), calls=%async_computation | async-start | bytes 1179648 | tf_op jit(solution)/shard_map/all_gather | solution.py:248
  8.3 25.0 %copy-start.3 = (bf16[256,227]{1,0:T(8,128)(2,1)}, bf16[256,227]{1,0:T(8,128)(2,1)S(1)}, u32[]{:S(2)}) copy-start(bf16[256,227]{1,0:T(8,128)(2,1)S(1)} %copy.22.grid_vars) | copy-start | bytes 348676
  32.3 12.8 %copy-start = (bf16[2176,227]{1,0:T(8,128)(2,1)}, bf16[2176,227]{1,0:T(8,128)(2,1)S(1)}, u32[]{:S(2)}) copy-start(bf16[2176,227]{1,0:T(8,128)(2,1)S(1)} %all_gather.18.buf) | copy-start | bytes 2963716
  33.3 26.2 %collective-permute-start.1 = (bf16[2176,227]{0,1:T(8,128)(2,1)S(1)}, bf16[2176,227]{0,1:T(8,128)(2,1)}, u32[]{:S(2)}, u32[]{:S(2)}) collective-permute-start(bf16[2176,227]{0,1:T(8,128)(2,1)S(1)} %copy.23), channel_id=1, source_target_pairs={{0,8},{16,24},{32,40},{48,56},{64,72},{80,88},{96,104},{112,120},{... | collective-permute-start | bytes 2963720 | tf_op jit(solution)/shard_map/ppermute | solution.py:246
  41.4 20.4 %collective-permute-start = (bf16[2176,227]{0,1:T(8,128)(2,1)S(1)}, bf16[2176,227]{0,1:T(8,128)(2,1)S(1)}, u32[]{:S(2)}, u32[]{:S(2)}) collective-permute-start(bf16[2176,227]{0,1:T(8,128)(2,1)S(1)} %copy.23), channel_id=1, source_target_pairs={{8,16},{24,32},{40,48},{56,64},{72,80},{88,96},{104,112},{120,128}... | collective-permute-start | bytes 2963720 | tf_op jit(solution)/shard_map/ppermute | solution.py:243
  94.8 11.8 %collective-permute-start.3 = (bf16[1024,512]{1,0:T(8,128)(2,1)}, bf16[1024,512]{1,0:T(8,128)(2,1)S(1)}, u32[]{:S(2)}, u32[]{:S(2)}) collective-permute-start(bf16[1024,512]{1,0:T(8,128)(2,1)} %enc_last.1.nodes), channel_id=1, source_target_pairs={{0,8},{16,24},{32,40},{48,56},{64,72},{80,88},{96,104},{112,120},{... | collective-permute-start | bytes 3145736 | tf_op jit(solution)/shard_map/ppermute | solution.py:246
  96.8 18.4 %collective-permute-start.2 = (bf16[1024,512]{1,0:T(8,128)(2,1)}, bf16[1024,512]{1,0:T(8,128)(2,1)S(1)}, u32[]{:S(2)}, u32[]{:S(2)}) collective-permute-start(bf16[1024,512]{1,0:T(8,128)(2,1)} %enc_last.1.nodes), channel_id=1, source_target_pairs={{8,16},{24,32},{40,48},{56,64},{72,80},{88,96},{104,112},{120,128}... | collective-permute-start | bytes 3145736 | tf_op jit(solution)/shard_map/ppermute | solution.py:243
  106.6 1.0 copy-start.11
  115.2 1.0 copy-start.10
  129.7 41.6 %copy-start.9 = (s32[768]{0:T(1024)S(1)}, s32[768]{0:T(1024)}, u32[]{:S(2)}) copy-start(s32[768]{0:T(1024)} %param.32) | copy-start | bytes 9220
  129.7 41.7 %copy-start.8 = (bf16[512,227]{0,1:T(8,128)(2,1)S(1)}, bf16[512,227]{0,1:T(8,128)(2,1)}, u32[]{:S(2)}) copy-start(bf16[512,227]{0,1:T(8,128)(2,1)} %param.27) | copy-start | bytes 697348
  136.1 36.2 %copy-start.1 = (bf16[512,512]{1,0:T(8,128)(2,1)}, bf16[512,512]{1,0:T(8,128)(2,1)S(1)}, u32[]{:S(2)}) copy-start(bf16[512,512]{1,0:T(8,128)(2,1)S(1)} %all_gather.21.a) | copy-start | bytes 1572868
  149.4 26.8 %copy-start.2 = (bf16[512,512]{1,0:T(8,128)(2,1)}, bf16[512,512]{1,0:T(8,128)(2,1)S(1)}, u32[]{:S(2)}) copy-start(bf16[512,512]{1,0:T(8,128)(2,1)S(1)} %all_gather.23.b) | copy-start | bytes 1572868
  149.4 26.8 %collective-permute-start.5 = (bf16[512,512]{1,0:T(8,128)(2,1)S(1)}, bf16[512,512]{1,0:T(8,128)(2,1)S(1)}, u32[]{:S(2)}, u32[]{:S(2)}) collective-permute-start(bf16[512,512]{1,0:T(8,128)(2,1)S(1)} %all_gather.23.b), channel_id=1, source_target_pairs={{0,8},{16,24},{32,40},{48,56},{64,72},{80,88},{96,104},{112,120},{... | collective-permute-start | bytes 1572872 | tf_op jit(solution)/shard_map/ppermute | solution.py:246
  153.7 22.5 %collective-permute-start.7 = (bf16[512,512]{1,0:T(8,128)(2,1)S(1)}, bf16[512,512]{1,0:T(8,128)(2,1)S(1)}, u32[]{:S(2)}, u32[]{:S(2)}) collective-permute-start(bf16[512,512]{1,0:T(8,128)(2,1)S(1)} %all_gather.23.b), channel_id=1, source_target_pairs={{8,16},{24,32},{40,48},{56,64},{72,80},{88,96},{104,112},{120,128}... | collective-permute-start | bytes 1572872 | tf_op jit(solution)/shard_map/ppermute | solution.py:243
  159.5 16.7 %collective-permute-start.4 = (bf16[512,512]{1,0:T(8,128)(2,1)S(1)}, bf16[512,512]{1,0:T(8,128)(2,1)S(1)}, u32[]{:S(2)}, u32[]{:S(2)}) collective-permute-start(bf16[512,512]{1,0:T(8,128)(2,1)S(1)} %all_gather.21.a), channel_id=1, source_target_pairs={{0,8},{16,24},{32,40},{48,56},{64,72},{80,88},{96,104},{112,120},{... | collective-permute-start | bytes 1572872 | tf_op jit(solution)/shard_map/ppermute | solution.py:246
  169.4 12.6 %collective-permute-start.6 = (bf16[512,512]{1,0:T(8,128)(2,1)S(1)}, bf16[512,512]{1,0:T(8,128)(2,1)S(1)}, u32[]{:S(2)}, u32[]{:S(2)}) collective-permute-start(bf16[512,512]{1,0:T(8,128)(2,1)S(1)} %all_gather.21.a), channel_id=1, source_target_pairs={{8,16},{24,32},{40,48},{56,64},{72,80},{88,96},{104,112},{120,128}... | collective-permute-start | bytes 1572872 | tf_op jit(solution)/shard_map/ppermute | solution.py:243
  176.2 5.8 %copy-start.4 = (bf16[512,512]{1,0:T(8,128)(2,1)}, bf16[512,512]{1,0:T(8,128)(2,1)S(1)}, u32[]{:S(2)}) copy-start(bf16[512,512]{1,0:T(8,128)(2,1)S(1)} %collective-permute-done.5.d) | copy-start | bytes 1572868
  176.2 5.8 %copy-start.5 = (bf16[512,512]{1,0:T(8,128)(2,1)}, bf16[512,512]{1,0:T(8,128)(2,1)S(1)}, u32[]{:S(2)}) copy-start(bf16[512,512]{1,0:T(8,128)(2,1)S(1)} %collective-permute-done.7.f) | copy-start | bytes 1572868
  176.2 5.8 %copy-start.6 = (bf16[512,512]{1,0:T(8,128)(2,1)}, bf16[512,512]{1,0:T(8,128)(2,1)S(1)}, u32[]{:S(2)}) copy-start(bf16[512,512]{1,0:T(8,128)(2,1)S(1)} %collective-permute-done.4.c) | copy-start | bytes 1572868
  182.0 0.8 copy-start.7
Sparse Core Ops, SparseCore 0:
  9.7 46.3 all-gather.1

commit v2 on v1

v2 whole, which is shorter than its diff:
```python
import functools

import jax
import jax.numpy as jnp
from jax import lax
from jax.experimental import pallas as pl
from jax.experimental.pallas import tpu as pltpu
from jax.sharding import PartitionSpec as P

LANES = 128
MIB = 1024 * 1024


def silu(v):
    return v * (0.5 + 0.5 * jnp.tanh(0.5 * v))


def rms(v):
    return v * lax.rsqrt(jnp.mean(v * v, axis=-1, keepdims=True) + 1e-05)


def mm(a, b):
    return jnp.dot(a, b, preferred_element_type=jnp.float32)


def mm_tn(a, b):
    return lax.dot_general(a, b, (((0,), (0,)), ((), ())), preferred_element_type=jnp.float32)


def mm_nt(a, b):
    return lax.dot_general(a, b, (((1,), (1,)), ((), ())), preferred_element_type=jnp.float32)


def hot_by_row(keys, count):
    spots = lax.broadcasted_iota(jnp.int16, (count, keys.shape[1]), 0)
    one, none = jnp.bfloat16(1), jnp.bfloat16(0)
    return jnp.where(spots == keys.astype(jnp.int16), one, none)


def columns_of(row):
    return jnp.transpose(jnp.broadcast_to(row, (LANES, LANES)))


def hot_by_column(spread, count):
    lanes = lax.broadcasted_iota(jnp.int32, (LANES, LANES), 1)
    parts = [
        jnp.where(spread == lanes + LANES * k, 1.0, 0.0).astype(jnp.bfloat16)
        for k in range(count // LANES)
    ]
    return jnp.concatenate(parts, axis=1)


def side(parts):
    return jnp.concatenate(parts, axis=1)


def notes_of(buf, s, columns, count):
    start = columns // 16 * 16
    notes = buf[s, start:, :].astype(jnp.float32).astype(jnp.int32)
    skip = columns - start

    def piece(k):
        row, lane = skip + k // 2, LANES * (k % 2)
        return notes[row : row + 1, lane : lane + LANES]

    return [piece(k) for k in range(count)]


def band_sums(pick, buf, w_embed, w_send, acc, out, lat, sent, counts, chunks):
    patches, _, grid_rows = buf.shape
    columns = w_embed.shape[0]
    nodes = out.shape[0]

    for s in range(patches):
        here = slice(grid_rows * s, grid_rows * (s + 1))
        lat[here, :] = silu(mm_tn(buf[s, :columns, :], w_embed[...])).astype(jnp.bfloat16)
    for s in range(patches):
        here = slice(grid_rows * s, grid_rows * (s + 1))
        sent[here, :] = silu(mm(lat[here, :], w_send[...])).astype(jnp.bfloat16)
    for s in range(patches):
        here = slice(grid_rows * s, grid_rows * (s + 1))
        notes = notes_of(buf, s, columns, 3 * chunks)
        to, frm = [], []
        for j in range(chunks):
            high, low = notes[chunks + j], notes[2 * chunks + j]
            key = jnp.where(high // patches == pick, (high % patches) * LANES + low, -1)
            to.append(hot_by_row(key, nodes))
            frm.append(hot_by_row(notes[j], grid_rows))
        counts[:, here] = mm_nt(side(to), side(frm)).astype(jnp.bfloat16)
    for i in range(nodes // 256):
        here = slice(256 * i, 256 * (i + 1))
        added = mm(counts[here, :], sent[...])
        out[here, :] = added if acc is None else acc[here, :] + added


def enc_first(pick, buf, w_embed, w_send, out, lat, sent, counts, *, chunks):
    band_sums(pick[0], buf, w_embed, w_send, None, out, lat, sent, counts, chunks)


def enc_more(pick, buf, w_embed, w_send, acc, out, lat, sent, counts, *, chunks):
    band_sums(pick[0], buf, w_embed, w_send, acc, out, lat, sent, counts, chunks)


def enc_last(
    pick, buf, w_embed, w_send, acc, init, gain, w_node, out, lat, sent, counts, total, *, chunks
):
    band_sums(pick[0], buf, w_embed, w_send, acc, total, lat, sent, counts, chunks)
    for i in range(out.shape[0] // 256):
        here = slice(256 * i, 256 * (i + 1))
        node_in = silu(rms(total[here, :]) * gain[...]).astype(jnp.bfloat16)
        fresh = init[here, :].astype(jnp.float32) + mm(node_in, w_node[...])
        out[here, :] = fresh.astype(jnp.bfloat16)


def picked_rows(pick, src, nodes, j):
    count = nodes.shape[0]
    hot = []
    for i in range(4 * j, 4 * j + 4):
        code = src[i : i + 1, :]
        key = jnp.where(code // count == pick, code % count, -1)
        hot.append(hot_by_column(columns_of(key), count))
    return mm(jnp.concatenate(hot, axis=0), nodes[...]).astype(jnp.bfloat16)


def proc_first(pick, src, nodes, out):
    for j in range(src.shape[0] // 4):
        out[512 * j : 512 * (j + 1), :] = picked_rows(pick[0], src, nodes, j)


def proc_more(pick, src, nodes, acc, out):
    for j in range(src.shape[0] // 4):
        at = slice(512 * j, 512 * (j + 1))
        out[at, :] = acc[at, :] + picked_rows(pick[0], src, nodes, j)


def proc_last(
    pick, src, dst, nodes, acc, band_one, w_ps, w_pr, w_po, w_ds, out, *, last_band
):
    band, mine = pick[1], out.shape[0]
    band_nodes = nodes.shape[0]
    own = band_one[pl.ds(pl.multiple_of(pick[2] * mine, mine), mine), :]
    recv = mm(own, w_pr[...])
    top = recv.astype(jnp.bfloat16)
    rest = (recv - top.astype(jnp.float32)).astype(jnp.bfloat16)
    recv_pair = jnp.concatenate([top, rest], axis=0)
    total = jnp.zeros(own.shape, jnp.float32)
    for j in range(src.shape[0] // 4):
        at = slice(512 * j, 512 * (j + 1))
        rows = acc[at, :] + picked_rows(pick[0], src, nodes, j)
        recv_hot, back = [], []
        for i in range(4 * j, 4 * j + 4):
            to = dst[i : i + 1, :]
            one = hot_by_column(columns_of(to), LANES)
            recv_hot.append(side([one, one]))
            target = band + src[i : i + 1, :] // band_nodes - 1
            valid = (target >= 0) & (target <= last_band)
            back.append(hot_by_row(jnp.where(valid, to, -1), mine))
        recv_rows = mm(jnp.concatenate(recv_hot, axis=0), recv_pair)
        msg = silu(mm(rows, w_ps[...]) + recv_rows).astype(jnp.bfloat16)
        total += mm(side(back), msg)
    norm = rms(total).astype(jnp.bfloat16)
    two = (own.astype(jnp.float32) + mm(norm, w_po[...])).astype(jnp.bfloat16)
    out[...] = silu(mm(two, w_ds[...])).astype(jnp.bfloat16)


def dec_counts(place, own, near, far, out, *, columns, skip, chunks):
    patches, _, grid_rows = own.shape
    patch, second = place[0], place[1]
    nodes = out.shape[1]
    for k, buf in enumerate((own, near, far)):
        notes = notes_of(buf, patch, columns, skip + 3 * chunks)[skip:]
        to, frm = [], []
        for j in range(chunks):
            high, low, dst = notes[j], notes[chunks + j], notes[2 * chunks + j]
            rel = (high % patches - patch) * (1 - 2 * second)
            turn = (rel + 2) & (patches - 1)
            spot = jnp.where(turn < 4, turn ^ 2, turn) ^ (3 * second)
            key = jnp.where(high // patches == place[2 + k], spot * LANES + low, -1)
            frm.append(hot_by_row(key, nodes))
            to.append(hot_by_row(dst, grid_rows))
        block = mm_nt(side(to), side(frm))
        out[grid_rows * k : grid_rows * (k + 1), :] = block.astype(jnp.bfloat16)


def dec_sums(counts, four, rest, out, *, first):
    half = four.shape[0]
    here = slice(first, first + out.shape[0])
    total = mm(counts[here, :half], four[...]) + mm(counts[here, half:], rest[...])
    out[...] = total.astype(out.dtype)


def dec_last(own, near, far, grid_vars, w_out, out):
    total = own[...] + near[...].astype(jnp.float32) + far[...].astype(jnp.float32)
    norm = rms(total).astype(jnp.bfloat16)
    fresh = grid_vars[...].astype(jnp.float32) + mm_nt(w_out[...], norm)
    out[...] = fresh.astype(jnp.bfloat16)


def call(body, out, *args, vmem=16, scalars=0, scratch=(), flops=0, **static):
    block = pl.BlockSpec(memory_space=pltpu.VMEM)
    smem = pl.BlockSpec(memory_space=pltpu.SMEM)
    moved = sum(a.size * a.dtype.itemsize for a in args) + out.size * out.dtype.itemsize
    return pl.pallas_call(
        functools.partial(body, **static),
        out_shape=out,
        in_specs=[smem] * scalars + [block] * (len(args) - scalars),
        out_specs=block,
        scratch_shapes=list(scratch),
        compiler_params=pltpu.CompilerParams(vmem_limit_bytes=vmem * MIB),
        cost_estimate=pl.CostEstimate(flops=flops, bytes_accessed=moved, transcendentals=0),
        name=body.__name__,
    )(*args)


def pair_groups(bands, patches, step):
    groups = []
    for b in range(bands):
        for p in range(patches):
            if (p + b) % 2 == 0:
                q = (p + 1) % patches if step == 0 else (p - 1) % patches
                groups.append([b * patches + p, b * patches + q])
    return groups


def shards(
    bands,
    patches,
    grid_vars,
    mesh_init,
    w_embed,
    w_send,
    w_node,
    node_gain,
    w_proc_send,
    w_proc_recv,
    w_proc_out,
    w_dec_send,
    w_dec_out,
    enc_src,
    enc_dst,
    proc_src,
    proc_dst,
    dec_src,
    dec_dst,
):
    f32, bf16 = jnp.float32, jnp.bfloat16
    shape = jax.ShapeDtypeStruct
    mine, width = mesh_init.shape
    band_nodes = patches * mine
    grid_rows, columns = grid_vars.shape
    edges = enc_src.shape[0]
    chunks = edges // LANES
    band = lax.axis_index("grid").astype(jnp.int32)
    patch = lax.axis_index("mesh").astype(jnp.int32)
    odd = band % 2
    far = 2 * odd
    near = 2 - far
    far_pairs = [(i, i + 1) for i in range(1, bands - 1, 2)]
    far_pairs += [(j, i) for i, j in far_pairs]
    near_pairs = [(i, i + 1) for i in range(0, bands - 1, 2)]
    near_pairs += [(j, i) for i, j in near_pairs]

    def over_far(block):
        return lax.ppermute(block, "grid", far_pairs)

    def over_near(block):
        return lax.ppermute(block, "grid", near_pairs)

    def scalars(*values):
        return jnp.stack(values).astype(jnp.int32)

    init_band = lax.all_gather(mesh_init, "mesh", axis=0, tiled=True)

    notes = jnp.concatenate(
        [enc_src, enc_dst // mine, enc_dst % mine, dec_src // mine, dec_src % mine, dec_dst]
    )
    note_rows = -(-(columns + -(-notes.size // grid_rows)) // 8) * 8 - columns
    notes = jnp.pad(notes, (0, note_rows * grid_rows - notes.size)).astype(bf16)
    grid_turned = grid_vars.T
    load = jnp.concatenate([grid_turned, notes.reshape(note_rows, grid_rows)], axis=0)
    own = lax.all_gather(load, "mesh", axis=0, tiled=False)
    far_load = over_far(own)
    near_load = over_near(own)

    band_rows = patches * grid_rows
    enc = dict(
        chunks=chunks,
        scalars=1,
        vmem=20,
        flops=2 * band_rows * (width * (columns + width) + band_nodes * (edges + width)),
    )
    scratch = [
        pltpu.VMEM((band_rows, width), bf16),
        pltpu.VMEM((band_rows, width), bf16),
        pltpu.VMEM((band_nodes, band_rows), bf16),
    ]
    acc_shape = shape((band_nodes, width), f32)
    acc = call(enc_first, acc_shape, scalars(1), own, w_embed, w_send, scratch=scratch, **enc)
    acc = call(
        enc_more, acc_shape, scalars(2 - near), near_load, w_embed, w_send, acc, scratch=scratch, **enc
    )
    one = call(
        enc_last,
        shape((band_nodes, width), bf16),
        scalars(2 - far),
        far_load,
        w_embed,
        w_send,
        acc,
        init_band,
        node_gain.reshape(1, width),
        w_node,
        scratch=scratch + [pltpu.VMEM((band_nodes, width), f32)],
        **enc,
    )

    far_one = over_far(one)
    near_one = over_near(one)
    src = proc_src.reshape(-1, LANES)
    dst = proc_dst.reshape(-1, LANES)
    proc_edges = proc_src.shape[0]
    pick = dict(scalars=1, flops=2 * proc_edges * band_nodes * width)
    pick_shape = shape((proc_edges, width), bf16)
    got = call(proc_first, pick_shape, scalars(1), src, one, **pick)

    second = (patch + band) % 2
    dec_edges = dec_src.shape[0]
    counts = call(
        dec_counts,
        shape((3 * grid_rows, band_nodes), bf16),
        scalars(patch, second, 1, 2 - near, 2 - far),
        own,
        near_load,
        far_load,
        scalars=1,
        flops=6 * grid_rows * band_nodes * dec_edges,
        columns=columns,
        skip=3 * chunks,
        chunks=dec_edges // LANES,
    )

    got = call(proc_more, pick_shape, scalars(near), src, near_one, got, **pick)
    sent = call(
        proc_last,
        shape((mine, width), bf16),
        scalars(far, band, patch),
        src,
        dst,
        far_one,
        got,
        one,
        w_proc_send,
        w_proc_recv,
        w_proc_out,
        w_dec_send,
        last_band=bands - 1,
        **pick,
    )

    groups = [pair_groups(bands, patches, step) for step in (0, 1)]

    def meet(rows_here, step):
        return lax.all_gather(
            rows_here, ("grid", "mesh"), axis=0, tiled=True, axis_index_groups=groups[step]
        )

    def partner_half(both):
        size = both.shape[0] // 2
        return lax.dynamic_slice_in_dim(both, (1 - second) * size, size, 0)

    four = meet(meet(sent, 0), 1)
    rest = meet(partner_half(meet(partner_half(four), 0)), 1)
    flops = 2 * grid_rows * band_nodes * width
    part = shape((grid_rows, width), bf16)
    far_sums = over_far(call(dec_sums, part, counts, four, rest, flops=flops, first=2 * grid_rows))
    near_sums = over_near(call(dec_sums, part, counts, four, rest, flops=flops, first=grid_rows))
    own_sums = call(
        dec_sums, shape((grid_rows, width), f32), counts, four, rest, flops=flops, first=0
    )
    return call(
        dec_last,
        shape((columns, grid_rows), bf16),
        own_sums,
        near_sums,
        far_sums,
        grid_turned,
        w_dec_out.T,
        flops=flops,
    ).T


def solution(mesh):
    spread = P(("grid", "mesh"), None)
    edge = P(("grid", "mesh"))
    in_specs = (spread, spread) + (P(),) * 9 + (edge,) * 6
    body = functools.partial(shards, mesh.shape["grid"], mesh.shape["mesh"])
    return jax.shard_map(body, mesh=mesh, in_specs=in_specs, out_specs=spread, check_vma=False)
```

time: 196 us -> 156 us (0.80)
  the two profiles are of different devices: /device:TPU:7 before, /device:TPU:512 now
where the time goes in v2:
time: 156 us; the launch traced here: 155 us
  blocking collectives  60.7 us (39%)
  Pallas kernels  32.8 us (21%)
  starting transfers between devices  16.9 us (11%)
  waiting for transfers between devices  14.5 us (9%)
  between operations  13.8 us (9%)
  local copies, waits for them, and re-layouts  12.4 us (8%)
  other arithmetic  3.76 us (2%)
    pallas_call x11, Pallas kernels, call(): pl.pallas_call(functools.partial(body, **static), out_shape=out, in_specs...  32.8 us
    all_gather x4, blocking collectives, meet(): lax.all_gather(rows_here, ('grid', 'mesh'), axis=0, tiled=True, axis_inde...  30.8 us
    all_gather x1, blocking collectives, shards(): own = lax.all_gather(load, 'mesh', axis=0, tiled=False)  29.9 us
    ppermute x3, waiting for transfers between devices, over_far(): return lax.ppermute(block, 'grid', far_pairs)  13.8 us
    unnamed x49, local copies, waits for them, and re-layouts  12.1 us
    ppermute x3, starting transfers between devices, over_far(): return lax.ppermute(block, 'grid', far_pairs)  11.1 us
    ppermute x3, starting transfers between devices, over_near(): return lax.ppermute(block, 'grid', near_pairs)  5.75 us
  transfers between devices with their start and end apart: 7, of which 2 were waited for; matrix products, arithmetic and copies ran while one was open for 3% of the time, Pallas kernels for 13%

profile of v2, /device:TPU:512, one launch (start us, length us, event | category | flops | bytes accessed | tf_op | source)
XLA Modules:
  0.0 154.9 jit_solution(8356345986561838502)
XLA Ops:
  6.5 0.7 all-gather.3.cloned.1.call-update
  11.3 0.9 pad_maximum_fusion
  12.2 29.9 %all-gather = bf16[1984,256]{1,0:T(8,128)(2,1)S(1)} all-gather(bf16[248,256]{1,0:T(8,128)(2,1)S(1)} %pad_maximum_fusion), channel_id=2, replica_groups=mesh['grid'=96,'mesh'=8] {'mesh'}, dimensions={0}, use_global_device_ids=true | all-gather | bytes 1142784 | tf_op jit(solution)/shard_map/all_gather | solution.py:281
  42.1 1.9 %collective-permute-start = (bf16[8,248,256]{2,1,0:T(8,128)(2,1)S(1)}, bf16[8,248,256]{2,1,0:T(8,128)(2,1)S(1)}, u32[]{:S(2)}, u32[]{:S(2)}) collective-permute-start(bf16[8,248,256]{2,1,0:T(8,128)(2,1)S(1)} %bitcast.12), channel_id=1, source_target_pairs={{0,8},{16,24},{32,40},{48,56},{64,72},{80,88},{96,104},{112,120},{... | collective-permute-start | bytes 3047432 | tf_op jit(solution)/shard_map/ppermute | solution.py:267
  44.0 5.4 %collective-permute-start.1 = (bf16[8,248,256]{2,1,0:T(8,128)(2,1)S(1)}, bf16[8,248,256]{2,1,0:T(8,128)(2,1)S(1)}, u32[]{:S(2)}, u32[]{:S(2)}) collective-permute-start(bf16[8,248,256]{2,1,0:T(8,128)(2,1)S(1)} %bitcast.13), channel_id=1, source_target_pairs={{8,16},{24,32},{40,48},{56,64},{72,80},{88,96},{104,112},{120,128}... | collective-permute-start | bytes 3047432 | tf_op jit(solution)/shard_map/ppermute | solution.py:264
  49.5 1.0 copy-done.13
  50.5 0.9 copy-done.17
  51.5 6.8 %enc_first.1.acc = f32[1024,512]{1,0:T(8,128)S(1)} custom-call(s32[1]{0:T(128)} %constant.70.clone.1.pick, bf16[8,248,256]{2,1,0:T(8,128)(2,1)S(1)} %bitcast.14, bf16[227,512]{1,0:T(8,128)(2,1)S(1)} %copy-done.17, bf16[512,512]{1,0:T(8,128)(2,1)S(1)} %copy-done.13), custom_call_target="tpu_custom_call" | custom-call | flops 5307891712 | bytes 3869700 | tf_op jit(solution)/shard_map/enc_first/pallas_call | solution.py:203
  58.4 6.6 %enc_more.1.acc = f32[1024,512]{1,0:T(8,128)S(1)} custom-call(s32[1]{0:T(128)} %bitcast.2.pick, bf16[8,248,256]{2,1,0:T(8,128)(2,1)S(1)} %collective-permute-done.near.buf, bf16[227,512]{1,0:T(8,128)(2,1)S(1)} %copy-done.17, bf16[512,512]{1,0:T(8,128)(2,1)S(1)} %copy-done.14, f32[1024,512]{1,0:T(8,128)S(1)} %enc_first.1.acc), custom_call_target="tpu_custom_call" | custom-call | flops 5307891712 | bytes 5966852 | tf_op jit(solution)/shard_map/enc_more/pallas_call | solution.py:203
  65.0 1.4 copy-done.20
  66.4 1.6 %copy-done.12 = bf16[1024,512]{1,0:T(8,128)(2,1)S(1)} copy-done((bf16[1024,512]{1,0:T(8,128)(2,1)S(1)}, bf16[1024,512]{1,0:T(8,128)(2,1)}, u32[]{:S(2)}) %copy-start.12) | copy-done | bytes 1048600
  68.0 1.0 copy-done.15
  69.0 1.0 copy-done.16
  70.1 1.6 %copy-done.21 = f32[1024,512]{1,0:T(8,128)S(1)} copy-done((f32[1024,512]{1,0:T(8,128)S(1)}, f32[1024,512]{1,0:T(8,128)}, u32[]{:S(2)}) %copy-start.21) | copy-done | bytes 2097176
  71.7 7.5 %enc_last.1.nodes.band_one = bf16[1024,512]{1,0:T(8,128)(2,1)S(1)} custom-call(s32[1]{0:T(128)} %bitcast.3.pick, bf16[8,248,256]{2,1,0:T(8,128)(2,1)S(1)} %collective-permute-done.1.far.buf, bf16[227,512]{1,0:T(8,128)(2,1)S(1)} %copy-done.18, bf16[512,512]{1,0:T(8,128)(2,1)S(1)} %copy-done.15, f32[1024,512]{1,0:T(8,128)S(1)} %copy-done.21, ...), custom_call_target="tpu_custom_call" | custom-call | flops 5307891712 | bytes 6493188 | tf_op jit(solution)/shard_map/enc_last/pallas_call | solution.py:203
  79.2 1.9 %collective-permute-start.3 = (bf16[1024,512]{1,0:T(8,128)(2,1)S(1)}, bf16[1024,512]{1,0:T(8,128)(2,1)}, u32[]{:S(2)}, u32[]{:S(2)}) collective-permute-start(bf16[1024,512]{1,0:T(8,128)(2,1)S(1)} %enc_last.1.nodes.band_one), channel_id=1, source_target_pairs={{0,8},{16,24},{32,40},{48,56},{64,72},{80,88},{96,104},{112,120},{... | collective-permute-start | bytes 3145736 | tf_op jit(solution)/shard_map/ppermute | solution.py:267
  81.1 3.6 %collective-permute-start.2 = (bf16[1024,512]{1,0:T(8,128)(2,1)S(1)}, bf16[1024,512]{1,0:T(8,128)(2,1)S(1)}, u32[]{:S(2)}, u32[]{:S(2)}) collective-permute-start(bf16[1024,512]{1,0:T(8,128)(2,1)S(1)} %enc_last.1.nodes.band_one), channel_id=1, source_target_pairs={{8,16},{24,32},{40,48},{56,64},{72,80},{88,96},{104,112},{120,128}... | collective-permute-start | bytes 3145736 | tf_op jit(solution)/shard_map/ppermute | solution.py:264
  84.9 1.2 copy-done.1
  86.2 1.2 copy-done.3
  87.4 2.0 %dec_counts.1.counts = bf16[768,1024]{1,0:T(8,128)(2,1)S(1)} custom-call(s32[5]{0:T(128)S(1)} %stack.30.place, bf16[8,248,256]{2,1,0:T(8,128)(2,1)S(1)} %bitcast.15, bf16[8,248,256]{2,1,0:T(8,128)(2,1)S(1)} %copy-done.1, bf16[8,248,256]{2,1,0:T(8,128)(2,1)S(1)} %copy-done.3), custom_call_target="tpu_custom_call" | custom-call | flops 1207959552 | bytes 4620308 | tf_op jit(solution)/shard_map/dec_counts/pallas_call | solution.py:203
  89.4 1.3 proc_first.1.acc
  90.8 2.7 %proc_more.1.acc = bf16[1024,512]{1,0:T(8,128)(2,1)S(1)} custom-call(s32[1]{0:T(128)} %bitcast.3.pick, s32[8,128]{1,0:T(8,128)S(1)} %bitcast.20, bf16[1024,512]{1,0:T(8,128)(2,1)} %collective-permute-done.3.nodes, bf16[1024,512]{1,0:T(8,128)(2,1)S(1)} %proc_first.1.acc), custom_call_target="tpu_custom_call" | custom-call | flops 1073741824 | bytes 3149828 | tf_op jit(solution)/shard_map/proc_more/pallas_call | solution.py:203
  93.4 7.1 %collective-permute-done.2.nodes = bf16[1024,512]{1,0:T(8,128)(2,1)S(1)} collective-permute-done((bf16[1024,512]{1,0:T(8,128)(2,1)S(1)}, bf16[1024,512]{1,0:T(8,128)(2,1)S(1)}, u32[]{:S(2)}, u32[]{:S(2)}) %collective-permute-start.2) | collective-permute-done | bytes 1048608 | tf_op jit(solution)/shard_map/ppermute | solution.py:264
  100.6 3.5 %proc_last.1 = bf16[128,512]{1,0:T(8,128)(2,1)S(1)} custom-call(s32[3]{0:T(128)S(1)} %pad_add_fusion.pick, s32[8,128]{1,0:T(8,128)S(1)} %bitcast.21, s32[8,128]{1,0:T(8,128)S(1)} %bitcast.22, bf16[1024,512]{1,0:T(8,128)(2,1)S(1)} %collective-permute-done.2.nodes, bf16[1024,512]{1,0:T(8,128)(2,1)S(1)} %proc_more.1.acc, ...), custom_call_target="tpu_custom_call" | custom-call | flops 1073741824 | bytes 5382156 | tf_op jit(solution)/shard_map/proc_last/pallas_call | solution.py:203
  104.1 5.6 %all_gather.24 = bf16[256,512]{1,0:T(8,128)(2,1)S(1)} all-gather(bf16[128,512]{1,0:T(8,128)(2,1)S(1)} %proc_last.1), channel_id=1, replica_groups={{0,1},{2,3},{4,5},{6,7},{9,10},{11,12},{13,14},{15,8},{16,17},{18,19},{..., dimensions={0}, use_global_device_ids=true | all-gather | bytes 393216 | tf_op jit(solution)/shard_map/all_gather | solution.py:363
  109.8 8.5 %all_gather.25.four = bf16[512,512]{1,0:T(8,128)(2,1)S(1)} all-gather(bf16[256,512]{1,0:T(8,128)(2,1)S(1)} %all_gather.24), channel_id=1, replica_groups={{0,7},{2,1},{4,3},{6,5},{9,8},{11,10},{13,12},{15,14},{16,23},{18,17},{..., dimensions={0}, use_global_device_ids=true | all-gather | bytes 786432 | tf_op jit(solution)/shard_map/all_gather | solution.py:363
  118.3 8.4 %all_gather.26 = bf16[512,512]{1,0:T(8,128)(2,1)S(1)} all-gather(bf16[256,512]{1,0:T(8,128)(2,1)S(1)} %constant_dynamic-slice_fusion.1), channel_id=1, replica_groups={{0,1},{2,3},{4,5},{6,7},{9,10},{11,12},{13,14},{15,8},{16,17},{18,19},{..., dimensions={0}, use_global_device_ids=true | all-gather | bytes 786432 | tf_op jit(solution)/shard_map/all_gather | solution.py:363
  126.7 8.3 %all_gather.27.rest = bf16[512,512]{1,0:T(8,128)(2,1)S(1)} all-gather(bf16[256,512]{1,0:T(8,128)(2,1)S(1)} %constant_dynamic-slice_fusion), channel_id=1, replica_groups={{0,7},{2,1},{4,3},{6,5},{9,8},{11,10},{13,12},{15,14},{16,23},{18,17},{..., dimensions={0}, use_global_device_ids=true | all-gather | bytes 786432 | tf_op jit(solution)/shard_map/all_gather | solution.py:363
  135.9 2.1 %collective-permute-start.5 = (bf16[256,512]{1,0:T(8,128)(2,1)S(1)}, bf16[256,512]{1,0:T(8,128)(2,1)S(1)}, u32[]{:S(2)}, u32[]{:S(2)}) collective-permute-start(bf16[256,512]{1,0:T(8,128)(2,1)S(1)} %dec_sums.5), channel_id=1, source_target_pairs={{8,16},{24,32},{40,48},{56,64},{72,80},{88,96},{104,112},{120,128}... | collective-permute-start | bytes 786440 | tf_op jit(solution)/shard_map/ppermute | solution.py:264
  137.9 1.9 %collective-permute-start.4 = (bf16[256,512]{1,0:T(8,128)(2,1)S(1)}, bf16[256,512]{1,0:T(8,128)(2,1)S(1)}, u32[]{:S(2)}, u32[]{:S(2)}) collective-permute-start(bf16[256,512]{1,0:T(8,128)(2,1)S(1)} %dec_sums.4), channel_id=1, source_target_pairs={{0,8},{16,24},{32,40},{48,56},{64,72},{80,88},{96,104},{112,120},{... | collective-permute-start | bytes 786440 | tf_op jit(solution)/shard_map/ppermute | solution.py:267
  140.3 6.7 %collective-permute-done.5.far = bf16[256,512]{1,0:T(8,128)(2,1)S(1)} collective-permute-done((bf16[256,512]{1,0:T(8,128)(2,1)S(1)}, bf16[256,512]{1,0:T(8,128)(2,1)S(1)}, u32[]{:S(2)}, u32[]{:S(2)}) %collective-permute-start.5) | collective-permute-done | bytes 262176 | tf_op jit(solution)/shard_map/ppermute | solution.py:264
  147.0 1.0 dec_last.1
  (61 shorter events, 5.6 us)
Async XLA Ops:
  6.5 59.8 %all-gather.3.cloned.1.call-start = ((), (), s32[]{:S(2)}) async-start(), calls=%async_computation | async-start | bytes 1179648 | tf_op jit(solution)/shard_map/all_gather | solution.py:272
  42.1 16.2 %collective-permute-start = (bf16[8,248,256]{2,1,0:T(8,128)(2,1)S(1)}, bf16[8,248,256]{2,1,0:T(8,128)(2,1)S(1)}, u32[]{:S(2)}, u32[]{:S(2)}) collective-permute-start(bf16[8,248,256]{2,1,0:T(8,128)(2,1)S(1)} %bitcast.12), channel_id=1, source_target_pairs={{0,8},{16,24},{32,40},{48,56},{64,72},{80,88},{96,104},{112,120},{... | collective-permute-start | bytes 3047432 | tf_op jit(solution)/shard_map/ppermute | solution.py:267
  44.0 22.3 %collective-permute-start.1 = (bf16[8,248,256]{2,1,0:T(8,128)(2,1)S(1)}, bf16[8,248,256]{2,1,0:T(8,128)(2,1)S(1)}, u32[]{:S(2)}, u32[]{:S(2)}) collective-permute-start(bf16[8,248,256]{2,1,0:T(8,128)(2,1)S(1)} %bitcast.13), channel_id=1, source_target_pairs={{8,16},{24,32},{40,48},{56,64},{72,80},{88,96},{104,112},{120,128}... | collective-permute-start | bytes 3047432 | tf_op jit(solution)/shard_map/ppermute | solution.py:264
  49.5 1.0 copy-start.13
  50.5 0.9 copy-start.17
  51.5 6.8 %copy-start.14 = (bf16[512,512]{1,0:T(8,128)(2,1)S(1)}, bf16[512,512]{1,0:T(8,128)(2,1)}, u32[]{:S(2)}) copy-start(bf16[512,512]{1,0:T(8,128)(2,1)} %w_send.5) | copy-start | bytes 1572868
  58.3 6.7 %copy-start = (bf16[8,248,256]{2,1,0:T(8,128)(2,1)}, bf16[8,248,256]{2,1,0:T(8,128)(2,1)S(1)}, u32[]{:S(2)}) copy-start(bf16[8,248,256]{2,1,0:T(8,128)(2,1)S(1)} %collective-permute-done.near.buf) | copy-start | bytes 3047428
  58.3 8.0 %copy-start.18 = (bf16[227,512]{1,0:T(8,128)(2,1)S(1)}, bf16[227,512]{1,0:T(8,128)(2,1)}, u32[]{:S(2)}) copy-start(bf16[227,512]{1,0:T(8,128)(2,1)} %w_embed.5) | copy-start | bytes 697348
  58.3 8.0 %copy-start.19 = (f32[512]{0:T(512)S(1)}, f32[512]{0:T(512)}, u32[]{:S(2)}) copy-start(f32[512]{0:T(512)} %param.22) | copy-start | bytes 6148
  65.0 1.4 copy-start.20
  66.4 12.8 %copy-start.2 = (bf16[8,248,256]{2,1,0:T(8,128)(2,1)}, bf16[8,248,256]{2,1,0:T(8,128)(2,1)S(1)}, u32[]{:S(2)}) copy-start(bf16[8,248,256]{2,1,0:T(8,128)(2,1)S(1)} %collective-permute-done.1.far.buf) | copy-start | bytes 3047428
  66.4 1.6 %copy-start.12 = (bf16[1024,512]{1,0:T(8,128)(2,1)S(1)}, bf16[1024,512]{1,0:T(8,128)(2,1)}, u32[]{:S(2)}) copy-start(bf16[1024,512]{1,0:T(8,128)(2,1)} %all-gather.3.cloned.1.call-done.init) | copy-start | bytes 3145732
  68.0 1.0 copy-start.15
  69.0 1.0 copy-start.16
  70.1 1.6 %copy-start.21 = (f32[1024,512]{1,0:T(8,128)S(1)}, f32[1024,512]{1,0:T(8,128)}, u32[]{:S(2)}) copy-start(f32[1024,512]{1,0:T(8,128)} %copy-done.20) | copy-start | bytes 6291460
  79.2 11.6 %collective-permute-start.3 = (bf16[1024,512]{1,0:T(8,128)(2,1)S(1)}, bf16[1024,512]{1,0:T(8,128)(2,1)}, u32[]{:S(2)}, u32[]{:S(2)}) collective-permute-start(bf16[1024,512]{1,0:T(8,128)(2,1)S(1)} %enc_last.1.nodes.band_one), channel_id=1, source_target_pairs={{0,8},{16,24},{32,40},{48,56},{64,72},{80,88},{96,104},{112,120},{... | collective-permute-start | bytes 3145736 | tf_op jit(solution)/shard_map/ppermute | solution.py:267
  81.1 19.4 %collective-permute-start.2 = (bf16[1024,512]{1,0:T(8,128)(2,1)S(1)}, bf16[1024,512]{1,0:T(8,128)(2,1)S(1)}, u32[]{:S(2)}, u32[]{:S(2)}) collective-permute-start(bf16[1024,512]{1,0:T(8,128)(2,1)S(1)} %enc_last.1.nodes.band_one), channel_id=1, source_target_pairs={{8,16},{24,32},{40,48},{56,64},{72,80},{88,96},{104,112},{120,128}... | collective-permute-start | bytes 3145736 | tf_op jit(solution)/shard_map/ppermute | solution.py:264
  84.9 1.2 copy-start.1
  86.2 1.2 copy-start.3
  87.4 2.0 %copy-start.10 = (s32[1024]{0:T(1024)S(1)}, s32[1024]{0:T(1024)}, u32[]{:S(2)}) copy-start(s32[1024]{0:T(1024)} %param.30) | copy-start | bytes 12292
  90.7 9.9 %copy-start.4 = (bf16[512,512]{1,0:T(8,128)(2,1)S(1)}, bf16[512,512]{1,0:T(8,128)(2,1)}, u32[]{:S(2)}) copy-start(bf16[512,512]{1,0:T(8,128)(2,1)} %w_ps.1) | copy-start | bytes 1572868
  90.7 9.8 %copy-start.5 = (bf16[512,512]{1,0:T(8,128)(2,1)S(1)}, bf16[512,512]{1,0:T(8,128)(2,1)}, u32[]{:S(2)}) copy-start(bf16[512,512]{1,0:T(8,128)(2,1)} %w_pr.1) | copy-start | bytes 1572868
  90.7 9.8 %copy-start.6 = (bf16[512,512]{1,0:T(8,128)(2,1)S(1)}, bf16[512,512]{1,0:T(8,128)(2,1)}, u32[]{:S(2)}) copy-start(bf16[512,512]{1,0:T(8,128)(2,1)} %w_po.1) | copy-start | bytes 1572868
  90.7 9.8 %copy-start.7 = (bf16[512,512]{1,0:T(8,128)(2,1)S(1)}, bf16[512,512]{1,0:T(8,128)(2,1)}, u32[]{:S(2)}) copy-start(bf16[512,512]{1,0:T(8,128)(2,1)} %w_ds.1) | copy-start | bytes 1572868
  90.7 9.8 %copy-start.11 = (s32[1024]{0:T(1024)S(1)}, s32[1024]{0:T(1024)}, u32[]{:S(2)}) copy-start(s32[1024]{0:T(1024)} %param.31) | copy-start | bytes 12292
  135.8 11.2 %copy-start.8 = (bf16[256,227]{0,1:T(8,128)(2,1)S(1)}, bf16[256,227]{0,1:T(8,128)(2,1)}, u32[]{:S(2)}) copy-start(bf16[256,227]{0,1:T(8,128)(2,1)} %param.17) | copy-start | bytes 348676
  135.9 11.2 %copy-start.9 = (bf16[512,227]{0,1:T(8,128)(2,1)S(1)}, bf16[512,227]{0,1:T(8,128)(2,1)}, u32[]{:S(2)}) copy-start(bf16[512,227]{0,1:T(8,128)(2,1)} %param.27) | copy-start | bytes 697348
  135.9 11.1 %collective-permute-start.5 = (bf16[256,512]{1,0:T(8,128)(2,1)S(1)}, bf16[256,512]{1,0:T(8,128)(2,1)S(1)}, u32[]{:S(2)}, u32[]{:S(2)}) collective-permute-start(bf16[256,512]{1,0:T(8,128)(2,1)S(1)} %dec_sums.5), channel_id=1, source_target_pairs={{8,16},{24,32},{40,48},{56,64},{72,80},{88,96},{104,112},{120,128}... | collective-permute-start | bytes 786440 | tf_op jit(solution)/shard_map/ppermute | solution.py:264
  137.9 9.1 %collective-permute-start.4 = (bf16[256,512]{1,0:T(8,128)(2,1)S(1)}, bf16[256,512]{1,0:T(8,128)(2,1)S(1)}, u32[]{:S(2)}, u32[]{:S(2)}) collective-permute-start(bf16[256,512]{1,0:T(8,128)(2,1)S(1)} %dec_sums.4), channel_id=1, source_target_pairs={{0,8},{16,24},{32,40},{48,56},{64,72},{80,88},{96,104},{112,120},{... | collective-permute-start | bytes 786440 | tf_op jit(solution)/shard_map/ppermute | solution.py:267
Sparse Core Ops, SparseCore 0:
  9.7 45.0 all-gather.2

commit v3 on v2

--- a/solution.py
+++ b/solution.py
@@ -66,17 +66,42 @@
     return [piece(k) for k in range(count)]
 
 
-def band_sums(pick, buf, w_embed, w_send, acc, out, lat, sent, counts, chunks):
+def pack(*refs):
+    out, sems = refs[5], refs[11]
+    waits(fetch(sems, *zip(refs[:5], refs[6:11])))()
+    grid_turned, enc_src, enc_dst, dec_src, dec_dst = refs[6:11]
+    columns, grid_rows = grid_turned.shape
+    start = columns // 16 * 16
+    out[:start, :] = grid_turned[:start, :]
+    pieces = []
+    for part in (
+        enc_src[...],
+        enc_dst[...] // LANES,
+        enc_dst[...] % LANES,
+        dec_src[...] // LANES,
+        dec_src[...] % LANES,
+        dec_dst[...],
+    ):
+        part = part.astype(jnp.float32)
+        pieces += [part[j : j + 1, :] for j in range(part.shape[0])]
+    pieces += [jnp.zeros_like(pieces[0])] * (len(pieces) % 2)
+    notes = [side(pieces[k : k + 2]) for k in range(0, len(pieces), 2)]
+    blank = jnp.zeros((out.shape[0] - columns - len(notes), grid_rows), jnp.float32)
+    rows = [grid_turned[start:, :].astype(jnp.float32)] + notes + [blank]
+    out[start:, :] = jnp.concatenate(rows, axis=0).astype(jnp.bfloat16)
+
+
+def fetch(sems, *pairs):
+    copies = [pltpu.make_async_copy(a, b, sems.at[i]) for i, (a, b) in enumerate(pairs)]
+    for copy in copies:
+        copy.start()
+    return copies
+
+
+def band_sums(pick, buf, w_embed, w_send, lat, sent, counts, chunks, ready):
     patches, _, grid_rows = buf.shape
     columns = w_embed.shape[0]
-    nodes = out.shape[0]
-
-    for s in range(patches):
-        here = slice(grid_rows * s, grid_rows * (s + 1))
-        lat[here, :] = silu(mm_tn(buf[s, :columns, :], w_embed[...])).astype(jnp.bfloat16)
-    for s in range(patches):
-        here = slice(grid_rows * s, grid_rows * (s + 1))
-        sent[here, :] = silu(mm(lat[here, :], w_send[...])).astype(jnp.bfloat16)
+    nodes = counts.shape[0]
     for s in range(patches):
         here = slice(grid_rows * s, grid_rows * (s + 1))
         notes = notes_of(buf, s, columns, 3 * chunks)
@@ -87,28 +112,78 @@
             to.append(hot_by_row(key, nodes))
             frm.append(hot_by_row(notes[j], grid_rows))
         counts[:, here] = mm_nt(side(to), side(frm)).astype(jnp.bfloat16)
-    for i in range(nodes // 256):
-        here = slice(256 * i, 256 * (i + 1))
-        added = mm(counts[here, :], sent[...])
-        out[here, :] = added if acc is None else acc[here, :] + added
-
-
-def enc_first(pick, buf, w_embed, w_send, out, lat, sent, counts, *, chunks):
-    band_sums(pick[0], buf, w_embed, w_send, None, out, lat, sent, counts, chunks)
-
-
-def enc_more(pick, buf, w_embed, w_send, acc, out, lat, sent, counts, *, chunks):
-    band_sums(pick[0], buf, w_embed, w_send, acc, out, lat, sent, counts, chunks)
+    ready()
+    for s in range(patches):
+        here = slice(grid_rows * s, grid_rows * (s + 1))
+        lat[here, :] = silu(mm_tn(buf[s, :columns, :], w_embed[...])).astype(jnp.bfloat16)
+    for s in range(patches):
+        here = slice(grid_rows * s, grid_rows * (s + 1))
+        sent[here, :] = silu(mm(lat[here, :], w_send[...])).astype(jnp.bfloat16)
+
+
+def waits(copies):
+    def ready():
+        for copy in copies:
+            copy.wait()
+
+    return ready
+
+
+def blocks(count):
+    return [slice(i, i + 256) for i in range(0, count, 256)]
+
+
+def enc_first(pick, buf, w_embed, w_send, out, lat, sent, counts, embed, send, sems, *, chunks):
+    copies = fetch(sems, (w_embed, embed), (w_send, send))
+    band_sums(pick[0], buf, embed, send, lat, sent, counts, chunks, waits(copies))
+    for here in blocks(out.shape[0]):
+        out[here, :] = mm(counts[here, :], sent[...])
+
+
+def enc_more(
+    pick, buf, acc, w_embed, w_send, out, lat, sent, counts, embed, send, sems, total, *, chunks
+):
+    copies = fetch(sems, (w_embed, embed), (w_send, send))
+    band_sums(pick[0], buf, embed, send, lat, sent, counts, chunks, waits(copies))
+    leaving = []
+    for i, here in enumerate(blocks(out.shape[0])):
+        total[here, :] = acc[here, :] + mm(counts[here, :], sent[...])
+        copy = pltpu.make_async_copy(total.at[here, :], out.at[here, :], sems.at[2 + i])
+        copy.start()
+        leaving.append(copy)
+    waits(leaving)()
 
 
 def enc_last(
-    pick, buf, w_embed, w_send, acc, init, gain, w_node, out, lat, sent, counts, total, *, chunks
+    pick,
+    buf,
+    gain,
+    w_embed,
+    w_send,
+    acc,
+    init,
+    w_node,
+    out,
+    lat,
+    sent,
+    counts,
+    embed,
+    send,
+    sems,
+    total,
+    init_here,
+    node,
+    *,
+    chunks,
 ):
-    band_sums(pick[0], buf, w_embed, w_send, acc, total, lat, sent, counts, chunks)
-    for i in range(out.shape[0] // 256):
-        here = slice(256 * i, 256 * (i + 1))
-        node_in = silu(rms(total[here, :]) * gain[...]).astype(jnp.bfloat16)
-        fresh = init[here, :].astype(jnp.float32) + mm(node_in, w_node[...])
+    copies = fetch(
+        sems, (w_embed, embed), (w_send, send), (acc, total), (w_node, node), (init, init_here)
+    )
+    band_sums(pick[0], buf, embed, send, lat, sent, counts, chunks, waits(copies))
+    for here in blocks(out.shape[0]):
+        summed = total[here, :] + mm(counts[here, :], sent[...])
+        node_in = silu(rms(summed) * gain[...]).astype(jnp.bfloat16)
+        fresh = init_here[here, :].astype(jnp.float32) + mm(node_in, node[...])
         out[here, :] = fresh.astype(jnp.bfloat16)
 
 
@@ -196,15 +271,20 @@
     out[...] = fresh.astype(jnp.bfloat16)
 
 
-def call(body, out, *args, vmem=16, scalars=0, scratch=(), flops=0, **static):
+def call(body, out, *args, vmem=16, scalars=0, remote=0, out_remote=False, scratch=(), flops=0, **static):
     block = pl.BlockSpec(memory_space=pltpu.VMEM)
     smem = pl.BlockSpec(memory_space=pltpu.SMEM)
+    away = pl.BlockSpec(memory_space=pltpu.HBM)
+    args = list(args)
+    args[len(args) - remote :] = [
+        pltpu.with_memory_space_constraint(a, pltpu.HBM) for a in args[len(args) - remote :]
+    ]
     moved = sum(a.size * a.dtype.itemsize for a in args) + out.size * out.dtype.itemsize
     return pl.pallas_call(
         functools.partial(body, **static),
-        out_shape=out,
-        in_specs=[smem] * scalars + [block] * (len(args) - scalars),
-        out_specs=block,
+        out_shape=pltpu.HBM(out.shape, out.dtype) if out_remote else out,
+        in_specs=[smem] * scalars + [block] * (len(args) - scalars - remote) + [away] * remote,
+        out_specs=away if out_remote else block,
         scratch_shapes=list(scratch),
         compiler_params=pltpu.CompilerParams(vmem_limit_bytes=vmem * MIB),
         cost_estimate=pl.CostEstimate(flops=flops, bytes_accessed=moved, transcendentals=0),
@@ -271,13 +351,18 @@
 
     init_band = lax.all_gather(mesh_init, "mesh", axis=0, tiled=True)
 
-    notes = jnp.concatenate(
-        [enc_src, enc_dst // mine, enc_dst % mine, dec_src // mine, dec_src % mine, dec_dst]
-    )
-    note_rows = -(-(columns + -(-notes.size // grid_rows)) // 8) * 8 - columns
-    notes = jnp.pad(notes, (0, note_rows * grid_rows - notes.size)).astype(bf16)
+    note_count = -(-(3 * edges + 3 * dec_src.size) // grid_rows)
+    load_rows = -(-(columns + note_count) // 8) * 8
     grid_turned = grid_vars.T
-    load = jnp.concatenate([grid_turned, notes.reshape(note_rows, grid_rows)], axis=0)
+    parts = [grid_turned]
+    parts += [a.reshape(-1, LANES) for a in (enc_src, enc_dst, dec_src, dec_dst)]
+    load = call(
+        pack,
+        shape((load_rows, grid_rows), bf16),
+        *parts,
+        remote=5,
+        scratch=[pltpu.VMEM(a.shape, a.dtype) for a in parts] + [pltpu.SemaphoreType.DMA((5,))],
+    )
     own = lax.all_gather(load, "mesh", axis=0, tiled=False)
     far_load = over_far(own)
     near_load = over_near(own)
@@ -293,24 +378,42 @@
         pltpu.VMEM((band_rows, width), bf16),
         pltpu.VMEM((band_rows, width), bf16),
         pltpu.VMEM((band_nodes, band_rows), bf16),
+        pltpu.VMEM((columns, width), bf16),
+        pltpu.VMEM((width, width), bf16),
+        pltpu.SemaphoreType.DMA((6,)),
     ]
+    held = pltpu.VMEM((band_nodes, width), f32)
     acc_shape = shape((band_nodes, width), f32)
-    acc = call(enc_first, acc_shape, scalars(1), own, w_embed, w_send, scratch=scratch, **enc)
     acc = call(
-        enc_more, acc_shape, scalars(2 - near), near_load, w_embed, w_send, acc, scratch=scratch, **enc
+        enc_first, acc_shape, scalars(1), own, w_embed, w_send, remote=2, scratch=scratch, **enc
+    )
+    acc = call(
+        enc_more,
+        acc_shape,
+        scalars(2 - near),
+        near_load,
+        acc,
+        w_embed,
+        w_send,
+        remote=2,
+        out_remote=True,
+        scratch=scratch + [held],
+        **enc,
     )
     one = call(
         enc_last,
         shape((band_nodes, width), bf16),
         scalars(2 - far),
         far_load,
+        node_gain.reshape(1, width),
         w_embed,
         w_send,
         acc,
         init_band,
-        node_gain.reshape(1, width),
         w_node,
-        scratch=scratch + [pltpu.VMEM((band_nodes, width), f32)],
+        remote=5,
+        scratch=scratch
+        + [held, pltpu.VMEM((band_nodes, width), bf16), pltpu.VMEM((width, width), bf16)],
         **enc,
     )
 

time: 156 us -> 144 us (0.923)
  local copies, waits for them, and re-layouts: 12.4 us -> 2.61 us
  other arithmetic: 3.76 us -> 0.08 us
  Pallas kernels: 32.8 us -> 35.6 us
  starting transfers between devices: 16.9 us -> 19 us
  blocking collectives: 60.7 us -> 59.1 us
    unnamed x49 -> x26, local copies, waits for them, and re-layouts: 12.1 us -> 2.49 us
    pallas_call x11 -> x12, Pallas kernels: 32.8 us -> 35.6 us  [call(): pl.pallas_call(functools.partial(body, **static), out_shape=pltpu.HBM(out...]
    another operation x4 -> x0, other arithmetic: 2.77 us -> none
    ppermute x3, starting transfers between devices: 11.1 us -> 13.2 us  [over_far(): return lax.ppermute(block, 'grid', far_pairs)]
    all_gather x1, blocking collectives: 29.9 us -> 28.3 us  [shards(): own = lax.all_gather(load, 'mesh', axis=0, tiled=False)]
  transfers between devices with their start and end apart: 7 -> 7, of which waited for: 2 -> 2; matrix products, arithmetic and copies ran while one was open for 3% -> 0% of each run, Pallas kernels for 13% -> 15%
where the time goes in v3:
time: 144 us
  blocking collectives  59.1 us (41%)
  Pallas kernels  35.6 us (25%)
  starting transfers between devices  19 us (13%)
  between operations  13.7 us (10%)
  waiting for transfers between devices  13.6 us (9%)
  local copies, waits for them, and re-layouts  2.61 us (2%)
    pallas_call x12, Pallas kernels, call(): pl.pallas_call(functools.partial(body, **static), out_shape=pltpu.HBM(out...  35.6 us
    all_gather x4, blocking collectives, meet(): lax.all_gather(rows_here, ('grid', 'mesh'), axis=0, tiled=True, axis_inde...  30.8 us
    all_gather x1, blocking collectives, shards(): own = lax.all_gather(load, 'mesh', axis=0, tiled=False)  28.3 us
    ppermute x3, starting transfers between devices, over_far(): return lax.ppermute(block, 'grid', far_pairs)  13.2 us
    ppermute x3, waiting for transfers between devices, over_far(): return lax.ppermute(block, 'grid', far_pairs)  12.9 us
    ppermute x3, starting transfers between devices, over_near(): return lax.ppermute(block, 'grid', near_pairs)  5.75 us
  transfers between devices with their start and end apart: 7, of which 2 were waited for; matrix products, arithmetic and copies ran while one was open for 0% of the time, Pallas kernels for 15%

profile of v3, /device:TPU:512, one launch (start us, length us, event | category | flops | bytes accessed | tf_op | source)
XLA Modules:
  0.0 143.7 jit_solution(10901314857006520786)
XLA Ops:
  6.5 0.7 all-gather.3.cloned.1.call-update
  7.3 1.0 pack.1
  8.2 28.3 %all-gather = bf16[1984,256]{1,0:T(8,128)(2,1)S(1)} all-gather(bf16[248,256]{1,0:T(8,128)(2,1)S(1)} %pack.1), channel_id=2, replica_groups=mesh['grid'=96,'mesh'=8] {'mesh'}, dimensions={0}, use_global_device_ids=true | all-gather | bytes 1142784 | tf_op jit(solution)/shard_map/all_gather | solution.py:366
  36.5 1.9 %collective-permute-start = (bf16[8,248,256]{2,1,0:T(8,128)(2,1)S(1)}, bf16[8,248,256]{2,1,0:T(8,128)(2,1)S(1)}, u32[]{:S(2)}, u32[]{:S(2)}) collective-permute-start(bf16[8,248,256]{2,1,0:T(8,128)(2,1)S(1)} %bitcast.16), channel_id=1, source_target_pairs={{0,8},{16,24},{32,40},{48,56},{64,72},{80,88},{96,104},{112,120},{... | collective-permute-start | bytes 3047432 | tf_op jit(solution)/shard_map/ppermute | solution.py:347
  38.5 6.6 %collective-permute-start.1 = (bf16[8,248,256]{2,1,0:T(8,128)(2,1)S(1)}, bf16[8,248,256]{2,1,0:T(8,128)(2,1)S(1)}, u32[]{:S(2)}, u32[]{:S(2)}) collective-permute-start(bf16[8,248,256]{2,1,0:T(8,128)(2,1)S(1)} %bitcast.17), channel_id=1, source_target_pairs={{8,16},{24,32},{40,48},{56,64},{72,80},{88,96},{104,112},{120,128}... | collective-permute-start | bytes 3047432 | tf_op jit(solution)/shard_map/ppermute | solution.py:344
  45.1 6.8 %enc_first.1.acc = f32[1024,512]{1,0:T(8,128)S(1)} custom-call(s32[1]{0:T(128)} %constant.30.clone.1.pick, bf16[8,248,256]{2,1,0:T(8,128)(2,1)S(1)} %bitcast.18, bf16[227,512]{1,0:T(8,128)(2,1)} %w_embed.5, bf16[512,512]{1,0:T(8,128)(2,1)} %w_send.5), custom_call_target="tpu_custom_call" | custom-call | flops 5307891712 | bytes 3869700 | tf_op jit(solution)/shard_map/enc_first/pallas_call | solution.py:283
  51.9 7.6 %enc_more.1.acc = f32[1024,512]{1,0:T(8,128)} custom-call(s32[1]{0:T(128)} %bitcast.2.pick, bf16[8,248,256]{2,1,0:T(8,128)(2,1)S(1)} %collective-permute-done.near.buf, f32[1024,512]{1,0:T(8,128)S(1)} %enc_first.1.acc, bf16[227,512]{1,0:T(8,128)(2,1)} %w_embed.5, bf16[512,512]{1,0:T(8,128)(2,1)} %w_send.5), custom_call_target="tpu_custom_call" | custom-call | flops 5307891712 | bytes 5966852 | tf_op jit(solution)/shard_map/enc_more/pallas_call | solution.py:283
  59.6 0.0 all-gather.3.cloned.1.call-done.init
  59.6 8.4 %enc_last.1.nodes.band_one = bf16[1024,512]{1,0:T(8,128)(2,1)S(1)} custom-call(s32[1]{0:T(128)} %bitcast.3.pick, bf16[8,248,256]{2,1,0:T(8,128)(2,1)S(1)} %collective-permute-done.1.far.buf, f32[1,512]{1,0:T(1,128)S(1)} %bitcast.27, bf16[227,512]{1,0:T(8,128)(2,1)} %w_embed.5, bf16[512,512]{1,0:T(8,128)(2,1)} %w_send.5, f32[1024,512]{1,0:T(8,128)} %enc_more.1.acc, ...), custom_call_target="tpu_custom_call" | custom-call | flops 5307891712 | bytes 6493188 | tf_op jit(solution)/shard_map/enc_last/pallas_call | solution.py:283
  68.0 1.9 %collective-permute-start.3 = (bf16[1024,512]{1,0:T(8,128)(2,1)S(1)}, bf16[1024,512]{1,0:T(8,128)(2,1)}, u32[]{:S(2)}, u32[]{:S(2)}) collective-permute-start(bf16[1024,512]{1,0:T(8,128)(2,1)S(1)} %enc_last.1.nodes.band_one), channel_id=1, source_target_pairs={{0,8},{16,24},{32,40},{48,56},{64,72},{80,88},{96,104},{112,120},{... | collective-permute-start | bytes 3145736 | tf_op jit(solution)/shard_map/ppermute | solution.py:347
  69.9 4.6 %collective-permute-start.2 = (bf16[1024,512]{1,0:T(8,128)(2,1)S(1)}, bf16[1024,512]{1,0:T(8,128)(2,1)S(1)}, u32[]{:S(2)}, u32[]{:S(2)}) collective-permute-start(bf16[1024,512]{1,0:T(8,128)(2,1)S(1)} %enc_last.1.nodes.band_one), channel_id=1, source_target_pairs={{8,16},{24,32},{40,48},{56,64},{72,80},{88,96},{104,112},{120,128}... | collective-permute-start | bytes 3145736 | tf_op jit(solution)/shard_map/ppermute | solution.py:344
  74.5 0.1 stack.30.place
  74.6 0.1 pad_add_fusion.pick
  74.7 1.2 copy-done.1
  75.9 1.2 copy-done.3
  77.1 2.0 %dec_counts.1.counts = bf16[768,1024]{1,0:T(8,128)(2,1)S(1)} custom-call(s32[5]{0:T(128)S(1)} %stack.30.place, bf16[8,248,256]{2,1,0:T(8,128)(2,1)S(1)} %bitcast.19, bf16[8,248,256]{2,1,0:T(8,128)(2,1)S(1)} %copy-done.1, bf16[8,248,256]{2,1,0:T(8,128)(2,1)S(1)} %copy-done.3), custom_call_target="tpu_custom_call" | custom-call | flops 1207959552 | bytes 4620308 | tf_op jit(solution)/shard_map/dec_counts/pallas_call | solution.py:283
  79.1 1.3 proc_first.1.acc
  80.4 0.0 copy-start.4
  80.5 2.7 %proc_more.1.acc = bf16[1024,512]{1,0:T(8,128)(2,1)S(1)} custom-call(s32[1]{0:T(128)} %bitcast.3.pick, s32[8,128]{1,0:T(8,128)S(1)} %bitcast.24, bf16[1024,512]{1,0:T(8,128)(2,1)} %collective-permute-done.3.nodes, bf16[1024,512]{1,0:T(8,128)(2,1)S(1)} %proc_first.1.acc), custom_call_target="tpu_custom_call" | custom-call | flops 1073741824 | bytes 3149828 | tf_op jit(solution)/shard_map/proc_more/pallas_call | solution.py:283
  83.2 6.2 %collective-permute-done.2.nodes = bf16[1024,512]{1,0:T(8,128)(2,1)S(1)} collective-permute-done((bf16[1024,512]{1,0:T(8,128)(2,1)S(1)}, bf16[1024,512]{1,0:T(8,128)(2,1)S(1)}, u32[]{:S(2)}, u32[]{:S(2)}) %collective-permute-start.2) | collective-permute-done | bytes 1048608 | tf_op jit(solution)/shard_map/ppermute | solution.py:344
  89.4 3.5 %proc_last.1 = bf16[128,512]{1,0:T(8,128)(2,1)S(1)} custom-call(s32[3]{0:T(128)S(1)} %pad_add_fusion.pick, s32[8,128]{1,0:T(8,128)S(1)} %bitcast.25, s32[8,128]{1,0:T(8,128)S(1)} %bitcast.26, bf16[1024,512]{1,0:T(8,128)(2,1)S(1)} %collective-permute-done.2.nodes, bf16[1024,512]{1,0:T(8,128)(2,1)S(1)} %proc_more.1.acc, ...), custom_call_target="tpu_custom_call" | custom-call | flops 1073741824 | bytes 5382156 | tf_op jit(solution)/shard_map/proc_last/pallas_call | solution.py:283
  92.9 5.6 %all_gather.24 = bf16[256,512]{1,0:T(8,128)(2,1)S(1)} all-gather(bf16[128,512]{1,0:T(8,128)(2,1)S(1)} %proc_last.1), channel_id=1, replica_groups={{0,1},{2,3},{4,5},{6,7},{9,10},{11,12},{13,14},{15,8},{16,17},{18,19},{..., dimensions={0}, use_global_device_ids=true | all-gather | bytes 393216 | tf_op jit(solution)/shard_map/all_gather | solution.py:466
  98.6 8.5 %all_gather.25.four = bf16[512,512]{1,0:T(8,128)(2,1)S(1)} all-gather(bf16[256,512]{1,0:T(8,128)(2,1)S(1)} %all_gather.24), channel_id=1, replica_groups={{0,7},{2,1},{4,3},{6,5},{9,8},{11,10},{13,12},{15,14},{16,23},{18,17},{..., dimensions={0}, use_global_device_ids=true | all-gather | bytes 786432 | tf_op jit(solution)/shard_map/all_gather | solution.py:466
  107.1 8.4 %all_gather.26 = bf16[512,512]{1,0:T(8,128)(2,1)S(1)} all-gather(bf16[256,512]{1,0:T(8,128)(2,1)S(1)} %constant_dynamic-slice_fusion.1), channel_id=1, replica_groups={{0,1},{2,3},{4,5},{6,7},{9,10},{11,12},{13,14},{15,8},{16,17},{18,19},{..., dimensions={0}, use_global_device_ids=true | all-gather | bytes 786432 | tf_op jit(solution)/shard_map/all_gather | solution.py:466
  115.5 8.3 %all_gather.27.rest = bf16[512,512]{1,0:T(8,128)(2,1)S(1)} all-gather(bf16[256,512]{1,0:T(8,128)(2,1)S(1)} %constant_dynamic-slice_fusion), channel_id=1, replica_groups={{0,7},{2,1},{4,3},{6,5},{9,8},{11,10},{13,12},{15,14},{16,23},{18,17},{..., dimensions={0}, use_global_device_ids=true | all-gather | bytes 786432 | tf_op jit(solution)/shard_map/all_gather | solution.py:466
  123.8 0.4 dec_sums.5
  124.2 0.4 dec_sums.4
  124.7 2.1 %collective-permute-start.5 = (bf16[256,512]{1,0:T(8,128)(2,1)S(1)}, bf16[256,512]{1,0:T(8,128)(2,1)S(1)}, u32[]{:S(2)}, u32[]{:S(2)}) collective-permute-start(bf16[256,512]{1,0:T(8,128)(2,1)S(1)} %dec_sums.5), channel_id=1, source_target_pairs={{8,16},{24,32},{40,48},{56,64},{72,80},{88,96},{104,112},{120,128}... | collective-permute-start | bytes 786440 | tf_op jit(solution)/shard_map/ppermute | solution.py:344
  126.8 1.9 %collective-permute-start.4 = (bf16[256,512]{1,0:T(8,128)(2,1)S(1)}, bf16[256,512]{1,0:T(8,128)(2,1)S(1)}, u32[]{:S(2)}, u32[]{:S(2)}) collective-permute-start(bf16[256,512]{1,0:T(8,128)(2,1)S(1)} %dec_sums.4), channel_id=1, source_target_pairs={{0,8},{16,24},{32,40},{48,56},{64,72},{80,88},{96,104},{112,120},{... | collective-permute-start | bytes 786440 | tf_op jit(solution)/shard_map/ppermute | solution.py:347
  128.7 0.4 dec_sums.3.own
  129.1 6.7 %collective-permute-done.5.far = bf16[256,512]{1,0:T(8,128)(2,1)S(1)} collective-permute-done((bf16[256,512]{1,0:T(8,128)(2,1)S(1)}, bf16[256,512]{1,0:T(8,128)(2,1)S(1)}, u32[]{:S(2)}, u32[]{:S(2)}) %collective-permute-start.5) | collective-permute-done | bytes 262176 | tf_op jit(solution)/shard_map/ppermute | solution.py:344
  135.9 1.0 dec_last.1
  (30 shorter events, 0.1 us)
Async XLA Ops:
  6.5 53.1 %all-gather.3.cloned.1.call-start = ((), (), s32[]{:S(2)}) async-start(), calls=%async_computation | async-start | bytes 1179648 | tf_op jit(solution)/shard_map/all_gather | solution.py:352
  36.5 15.3 %collective-permute-start = (bf16[8,248,256]{2,1,0:T(8,128)(2,1)S(1)}, bf16[8,248,256]{2,1,0:T(8,128)(2,1)S(1)}, u32[]{:S(2)}, u32[]{:S(2)}) collective-permute-start(bf16[8,248,256]{2,1,0:T(8,128)(2,1)S(1)} %bitcast.16), channel_id=1, source_target_pairs={{0,8},{16,24},{32,40},{48,56},{64,72},{80,88},{96,104},{112,120},{... | collective-permute-start | bytes 3047432 | tf_op jit(solution)/shard_map/ppermute | solution.py:347
  38.5 21.1 %collective-permute-start.1 = (bf16[8,248,256]{2,1,0:T(8,128)(2,1)S(1)}, bf16[8,248,256]{2,1,0:T(8,128)(2,1)S(1)}, u32[]{:S(2)}, u32[]{:S(2)}) collective-permute-start(bf16[8,248,256]{2,1,0:T(8,128)(2,1)S(1)} %bitcast.17), channel_id=1, source_target_pairs={{8,16},{24,32},{40,48},{56,64},{72,80},{88,96},{104,112},{120,128}... | collective-permute-start | bytes 3047432 | tf_op jit(solution)/shard_map/ppermute | solution.py:344
  51.9 7.7 %copy-start = (bf16[8,248,256]{2,1,0:T(8,128)(2,1)}, bf16[8,248,256]{2,1,0:T(8,128)(2,1)S(1)}, u32[]{:S(2)}) copy-start(bf16[8,248,256]{2,1,0:T(8,128)(2,1)S(1)} %collective-permute-done.near.buf) | copy-start | bytes 3047428
  51.9 7.7 %copy-start.12 = (f32[512]{0:T(512)S(1)}, f32[512]{0:T(512)}, u32[]{:S(2)}) copy-start(f32[512]{0:T(512)} %param.22) | copy-start | bytes 6148
  59.6 8.4 %copy-start.2 = (bf16[8,248,256]{2,1,0:T(8,128)(2,1)}, bf16[8,248,256]{2,1,0:T(8,128)(2,1)S(1)}, u32[]{:S(2)}) copy-start(bf16[8,248,256]{2,1,0:T(8,128)(2,1)S(1)} %collective-permute-done.1.far.buf) | copy-start | bytes 3047428
  68.0 12.5 %collective-permute-start.3 = (bf16[1024,512]{1,0:T(8,128)(2,1)S(1)}, bf16[1024,512]{1,0:T(8,128)(2,1)}, u32[]{:S(2)}, u32[]{:S(2)}) collective-permute-start(bf16[1024,512]{1,0:T(8,128)(2,1)S(1)} %enc_last.1.nodes.band_one), channel_id=1, source_target_pairs={{0,8},{16,24},{32,40},{48,56},{64,72},{80,88},{96,104},{112,120},{... | collective-permute-start | bytes 3145736 | tf_op jit(solution)/shard_map/ppermute | solution.py:347
  69.9 19.4 %collective-permute-start.2 = (bf16[1024,512]{1,0:T(8,128)(2,1)S(1)}, bf16[1024,512]{1,0:T(8,128)(2,1)S(1)}, u32[]{:S(2)}, u32[]{:S(2)}) collective-permute-start(bf16[1024,512]{1,0:T(8,128)(2,1)S(1)} %enc_last.1.nodes.band_one), channel_id=1, source_target_pairs={{8,16},{24,32},{40,48},{56,64},{72,80},{88,96},{104,112},{120,128}... | collective-permute-start | bytes 3145736 | tf_op jit(solution)/shard_map/ppermute | solution.py:344
  74.7 1.2 copy-start.1
  75.9 1.2 copy-start.3
  77.1 2.0 %copy-start.10 = (s32[1024]{0:T(1024)S(1)}, s32[1024]{0:T(1024)}, u32[]{:S(2)}) copy-start(s32[1024]{0:T(1024)} %param.30) | copy-start | bytes 12292
  80.4 8.9 %copy-start.4 = (bf16[512,512]{1,0:T(8,128)(2,1)S(1)}, bf16[512,512]{1,0:T(8,128)(2,1)}, u32[]{:S(2)}) copy-start(bf16[512,512]{1,0:T(8,128)(2,1)} %w_ps.1) | copy-start | bytes 1572868
  80.5 8.9 %copy-start.5 = (bf16[512,512]{1,0:T(8,128)(2,1)S(1)}, bf16[512,512]{1,0:T(8,128)(2,1)}, u32[]{:S(2)}) copy-start(bf16[512,512]{1,0:T(8,128)(2,1)} %w_pr.1) | copy-start | bytes 1572868
  80.5 8.9 %copy-start.6 = (bf16[512,512]{1,0:T(8,128)(2,1)S(1)}, bf16[512,512]{1,0:T(8,128)(2,1)}, u32[]{:S(2)}) copy-start(bf16[512,512]{1,0:T(8,128)(2,1)} %w_po.1) | copy-start | bytes 1572868
  80.5 8.9 %copy-start.7 = (bf16[512,512]{1,0:T(8,128)(2,1)S(1)}, bf16[512,512]{1,0:T(8,128)(2,1)}, u32[]{:S(2)}) copy-start(bf16[512,512]{1,0:T(8,128)(2,1)} %w_ds.1) | copy-start | bytes 1572868
  80.5 8.9 %copy-start.11 = (s32[1024]{0:T(1024)S(1)}, s32[1024]{0:T(1024)}, u32[]{:S(2)}) copy-start(s32[1024]{0:T(1024)} %param.31) | copy-start | bytes 12292
  124.7 11.2 %copy-start.8 = (bf16[256,227]{0,1:T(8,128)(2,1)S(1)}, bf16[256,227]{0,1:T(8,128)(2,1)}, u32[]{:S(2)}) copy-start(bf16[256,227]{0,1:T(8,128)(2,1)} %param.17) | copy-start | bytes 348676
  124.7 11.2 %copy-start.9 = (bf16[512,227]{0,1:T(8,128)(2,1)S(1)}, bf16[512,227]{0,1:T(8,128)(2,1)}, u32[]{:S(2)}) copy-start(bf16[512,227]{0,1:T(8,128)(2,1)} %param.27) | copy-start | bytes 697348
  124.7 11.1 %collective-permute-start.5 = (bf16[256,512]{1,0:T(8,128)(2,1)S(1)}, bf16[256,512]{1,0:T(8,128)(2,1)S(1)}, u32[]{:S(2)}, u32[]{:S(2)}) collective-permute-start(bf16[256,512]{1,0:T(8,128)(2,1)S(1)} %dec_sums.5), channel_id=1, source_target_pairs={{8,16},{24,32},{40,48},{56,64},{72,80},{88,96},{104,112},{120,128}... | collective-permute-start | bytes 786440 | tf_op jit(solution)/shard_map/ppermute | solution.py:344
  126.8 9.1 %collective-permute-start.4 = (bf16[256,512]{1,0:T(8,128)(2,1)S(1)}, bf16[256,512]{1,0:T(8,128)(2,1)S(1)}, u32[]{:S(2)}, u32[]{:S(2)}) collective-permute-start(bf16[256,512]{1,0:T(8,128)(2,1)S(1)} %dec_sums.4), channel_id=1, source_target_pairs={{0,8},{16,24},{32,40},{48,56},{64,72},{80,88},{96,104},{112,120},{... | collective-permute-start | bytes 786440 | tf_op jit(solution)/shard_map/ppermute | solution.py:347
Sparse Core Ops, SparseCore 0:
  9.7 45.2 all-gather.2

commit v4 on v3

--- a/solution.py
+++ b/solution.py
@@ -35,6 +35,10 @@
     spots = lax.broadcasted_iota(jnp.int16, (count, keys.shape[1]), 0)
     one, none = jnp.bfloat16(1), jnp.bfloat16(0)
     return jnp.where(spots == keys.astype(jnp.int16), one, none)
+
+
+def marks(rows, count):
+    return side([hot_by_row(row, count).astype(jnp.float8_e4m3fn) for row in rows])
 
 
 def columns_of(row):
@@ -109,9 +113,9 @@
         for j in range(chunks):
             high, low = notes[chunks + j], notes[2 * chunks + j]
             key = jnp.where(high // patches == pick, (high % patches) * LANES + low, -1)
-            to.append(hot_by_row(key, nodes))
-            frm.append(hot_by_row(notes[j], grid_rows))
-        counts[:, here] = mm_nt(side(to), side(frm)).astype(jnp.bfloat16)
+            to.append(key)
+            frm.append(notes[j])
+        counts[:, here] = mm_nt(marks(to, nodes), marks(frm, grid_rows)).astype(jnp.bfloat16)
     ready()
     for s in range(patches):
         here = slice(grid_rows * s, grid_rows * (s + 1))
@@ -141,50 +145,34 @@
 
 
 def enc_more(
-    pick, buf, acc, w_embed, w_send, out, lat, sent, counts, embed, send, sems, total, *, chunks
+    pick, buf, acc, w_embed, w_send, out, lat, sent, counts, embed, send, sems, *, chunks
 ):
     copies = fetch(sems, (w_embed, embed), (w_send, send))
     band_sums(pick[0], buf, embed, send, lat, sent, counts, chunks, waits(copies))
-    leaving = []
-    for i, here in enumerate(blocks(out.shape[0])):
-        total[here, :] = acc[here, :] + mm(counts[here, :], sent[...])
-        copy = pltpu.make_async_copy(total.at[here, :], out.at[here, :], sems.at[2 + i])
-        copy.start()
-        leaving.append(copy)
-    waits(leaving)()
+    for here in blocks(out.shape[0]):
+        out[here, :] = acc[here, :] + mm(counts[here, :], sent[...])
 
 
 def enc_last(
-    pick,
-    buf,
-    gain,
-    w_embed,
-    w_send,
-    acc,
-    init,
-    w_node,
-    out,
-    lat,
-    sent,
-    counts,
-    embed,
-    send,
-    sems,
-    total,
-    init_here,
-    node,
-    *,
-    chunks,
+    pick, buf, acc, gain, w_embed, w_send, out, lat, sent, counts, embed, send, sems, *, chunks
 ):
-    copies = fetch(
-        sems, (w_embed, embed), (w_send, send), (acc, total), (w_node, node), (init, init_here)
-    )
+    copies = fetch(sems, (w_embed, embed), (w_send, send))
     band_sums(pick[0], buf, embed, send, lat, sent, counts, chunks, waits(copies))
     for here in blocks(out.shape[0]):
-        summed = total[here, :] + mm(counts[here, :], sent[...])
-        node_in = silu(rms(summed) * gain[...]).astype(jnp.bfloat16)
-        fresh = init_here[here, :].astype(jnp.float32) + mm(node_in, node[...])
-        out[here, :] = fresh.astype(jnp.bfloat16)
+        summed = acc[here, :] + mm(counts[here, :], sent[...])
+        out[here, :] = silu(rms(summed) * gain[...]).astype(jnp.bfloat16)
+
+
+def node_update(node_in, w_node, init, out, node, init_here, sems):
+    parts = blocks(out.shape[0])
+    copies = fetch(
+        sems, (w_node, node), *[(init.at[here, :], init_here.at[here, :]) for here in parts]
+    )
+    copies[0].wait()
+    for i, here in enumerate(parts):
+        fresh = mm(node_in[here, :], node[...])
+        copies[1 + i].wait()
+        out[here, :] = (init_here[here, :].astype(jnp.float32) + fresh).astype(jnp.bfloat16)
 
 
 def picked_rows(pick, src, nodes, j):
@@ -251,9 +239,9 @@
             turn = (rel + 2) & (patches - 1)
             spot = jnp.where(turn < 4, turn ^ 2, turn) ^ (3 * second)
             key = jnp.where(high // patches == place[2 + k], spot * LANES + low, -1)
-            frm.append(hot_by_row(key, nodes))
-            to.append(hot_by_row(dst, grid_rows))
-        block = mm_nt(side(to), side(frm))
+            frm.append(key)
+            to.append(dst)
+        block = mm_nt(marks(to, grid_rows), marks(frm, nodes))
         out[grid_rows * k : grid_rows * (k + 1), :] = block.astype(jnp.bfloat16)
 
 
@@ -271,7 +259,7 @@
     out[...] = fresh.astype(jnp.bfloat16)
 
 
-def call(body, out, *args, vmem=16, scalars=0, remote=0, out_remote=False, scratch=(), flops=0, **static):
+def call(body, out, *args, vmem=16, scalars=0, remote=0, scratch=(), flops=0, **static):
     block = pl.BlockSpec(memory_space=pltpu.VMEM)
     smem = pl.BlockSpec(memory_space=pltpu.SMEM)
     away = pl.BlockSpec(memory_space=pltpu.HBM)
@@ -282,9 +270,9 @@
     moved = sum(a.size * a.dtype.itemsize for a in args) + out.size * out.dtype.itemsize
     return pl.pallas_call(
         functools.partial(body, **static),
-        out_shape=pltpu.HBM(out.shape, out.dtype) if out_remote else out,
+        out_shape=out,
         in_specs=[smem] * scalars + [block] * (len(args) - scalars - remote) + [away] * remote,
-        out_specs=away if out_remote else block,
+        out_specs=block,
         scratch_shapes=list(scratch),
         compiler_params=pltpu.CompilerParams(vmem_limit_bytes=vmem * MIB),
         cost_estimate=pl.CostEstimate(flops=flops, bytes_accessed=moved, transcendentals=0),
@@ -372,7 +360,7 @@
         chunks=chunks,
         scalars=1,
         vmem=20,
-        flops=2 * band_rows * (width * (columns + width) + band_nodes * (edges + width)),
+        flops=band_rows * width,
     )
     scratch = [
         pltpu.VMEM((band_rows, width), bf16),
@@ -380,9 +368,8 @@
         pltpu.VMEM((band_nodes, band_rows), bf16),
         pltpu.VMEM((columns, width), bf16),
         pltpu.VMEM((width, width), bf16),
-        pltpu.SemaphoreType.DMA((6,)),
+        pltpu.SemaphoreType.DMA((2,)),
     ]
-    held = pltpu.VMEM((band_nodes, width), f32)
     acc_shape = shape((band_nodes, width), f32)
     acc = call(
         enc_first, acc_shape, scalars(1), own, w_embed, w_send, remote=2, scratch=scratch, **enc
@@ -396,25 +383,35 @@
         w_embed,
         w_send,
         remote=2,
-        out_remote=True,
-        scratch=scratch + [held],
+        scratch=scratch,
         **enc,
     )
-    one = call(
+    one_shape = shape((band_nodes, width), bf16)
+    node_in = call(
         enc_last,
-        shape((band_nodes, width), bf16),
+        one_shape,
         scalars(2 - far),
         far_load,
+        acc,
         node_gain.reshape(1, width),
         w_embed,
         w_send,
-        acc,
+        remote=2,
+        scratch=scratch,
+        **enc,
+    )
+    one = call(
+        node_update,
+        one_shape,
+        node_in,
+        w_node,
         init_band,
-        w_node,
-        remote=5,
-        scratch=scratch
-        + [held, pltpu.VMEM((band_nodes, width), bf16), pltpu.VMEM((width, width), bf16)],
-        **enc,
+        remote=2,
+        scratch=[
+            pltpu.VMEM((width, width), bf16),
+            pltpu.VMEM((band_nodes, width), bf16),
+            pltpu.SemaphoreType.DMA((1 + band_nodes // 256,)),
+        ],
     )
 
     far_one = over_far(one)

time: 144 us -> 145 us (level)
  the two profiles are of different devices: /device:TPU:512 before, /device:TPU:256 now
where the time goes in v4:
time: 145 us; the launch traced here: 144 us
  blocking collectives  60.1 us (41%)
  Pallas kernels  33.5 us (23%)
  waiting for transfers between devices  19.6 us (14%)
  starting transfers between devices  14.6 us (10%)
  between operations  13.7 us (9%)
  local copies, waits for them, and re-layouts  2.61 us (2%)
    pallas_call x13, Pallas kernels, call(): pl.pallas_call(functools.partial(body, **static), out_shape=out, in_specs...  33.5 us
    all_gather x4, blocking collectives, meet(): lax.all_gather(rows_here, ('grid', 'mesh'), axis=0, tiled=True, axis_inde...  30.8 us
    all_gather x1, blocking collectives, shards(): own = lax.all_gather(load, 'mesh', axis=0, tiled=False)  29.3 us
    ppermute x3, waiting for transfers between devices, over_far(): return lax.ppermute(block, 'grid', far_pairs)  18.9 us
    ppermute x3, starting transfers between devices, over_far(): return lax.ppermute(block, 'grid', far_pairs)  8.86 us
    ppermute x3, starting transfers between devices, over_near(): return lax.ppermute(block, 'grid', near_pairs)  5.75 us
  transfers between devices with their start and end apart: 7, of which 3 were waited for; matrix products, arithmetic and copies ran while one was open for 0% of the time, Pallas kernels for 17%

profile of v4, /device:TPU:256, one launch (start us, length us, event | category | flops | bytes accessed | tf_op | source)
XLA Modules:
  0.0 144.3 jit_solution(11107723284632162360)
XLA Ops:
  6.5 0.7 all-gather.3.cloned.1.call-update
  7.3 1.0 pack.1
  8.2 29.3 %all-gather = bf16[1984,256]{1,0:T(8,128)(2,1)S(1)} all-gather(bf16[248,256]{1,0:T(8,128)(2,1)S(1)} %pack.1), channel_id=2, replica_groups=mesh['grid'=96,'mesh'=8] {'mesh'}, dimensions={0}, use_global_device_ids=true | all-gather | bytes 1142784 | tf_op jit(solution)/shard_map/all_gather | solution.py:354
  37.5 1.9 %collective-permute-start = (bf16[8,248,256]{2,1,0:T(8,128)(2,1)S(1)}, bf16[8,248,256]{2,1,0:T(8,128)(2,1)S(1)}, u32[]{:S(2)}, u32[]{:S(2)}) collective-permute-start(bf16[8,248,256]{2,1,0:T(8,128)(2,1)S(1)} %bitcast.16), channel_id=1, source_target_pairs={{0,8},{16,24},{32,40},{48,56},{64,72},{80,88},{96,104},{112,120},{... | collective-permute-start | bytes 3047432 | tf_op jit(solution)/shard_map/ppermute | solution.py:335
  39.4 3.4 %collective-permute-start.1 = (bf16[8,248,256]{2,1,0:T(8,128)(2,1)S(1)}, bf16[8,248,256]{2,1,0:T(8,128)(2,1)S(1)}, u32[]{:S(2)}, u32[]{:S(2)}) collective-permute-start(bf16[8,248,256]{2,1,0:T(8,128)(2,1)S(1)} %bitcast.17), channel_id=1, source_target_pairs={{8,16},{24,32},{40,48},{56,64},{72,80},{88,96},{104,112},{120,128}... | collective-permute-start | bytes 3047432 | tf_op jit(solution)/shard_map/ppermute | solution.py:332
  42.9 5.6 %enc_first.1.acc = f32[1024,512]{1,0:T(8,128)S(1)} custom-call(s32[1]{0:T(128)} %constant.30.clone.1.pick, bf16[8,248,256]{2,1,0:T(8,128)(2,1)S(1)} %bitcast.18, bf16[227,512]{1,0:T(8,128)(2,1)} %w_embed.5, bf16[512,512]{1,0:T(8,128)(2,1)} %w_send.5), custom_call_target="tpu_custom_call" | custom-call | flops 1048576 | bytes 3869700 | tf_op jit(solution)/shard_map/enc_first/pallas_call | solution.py:271
  48.5 5.9 %enc_more.1.acc = f32[1024,512]{1,0:T(8,128)S(1)} custom-call(s32[1]{0:T(128)} %bitcast.2.pick, bf16[8,248,256]{2,1,0:T(8,128)(2,1)S(1)} %collective-permute-done.near.buf, f32[1024,512]{1,0:T(8,128)S(1)} %enc_first.1.acc, bf16[227,512]{1,0:T(8,128)(2,1)} %w_embed.5, bf16[512,512]{1,0:T(8,128)(2,1)} %w_send.5), custom_call_target="tpu_custom_call" | custom-call | flops 1048576 | bytes 5966852 | tf_op jit(solution)/shard_map/enc_more/pallas_call | solution.py:271
  54.5 4.1 %collective-permute-done.1.far.buf = bf16[8,248,256]{2,1,0:T(8,128)(2,1)S(1)} collective-permute-done((bf16[8,248,256]{2,1,0:T(8,128)(2,1)S(1)}, bf16[8,248,256]{2,1,0:T(8,128)(2,1)S(1)}, u32[]{:S(2)}, u32[]{:S(2)}) %collective-permute-start.1) | collective-permute-done | bytes 1015840 | tf_op jit(solution)/shard_map/ppermute | solution.py:332
  58.5 6.6 %enc_last.1.node_in = bf16[1024,512]{1,0:T(8,128)(2,1)S(1)} custom-call(s32[1]{0:T(128)} %bitcast.3.pick, bf16[8,248,256]{2,1,0:T(8,128)(2,1)S(1)} %collective-permute-done.1.far.buf, f32[1024,512]{1,0:T(8,128)S(1)} %enc_more.1.acc, f32[1,512]{1,0:T(1,128)S(1)} %bitcast.27, bf16[227,512]{1,0:T(8,128)(2,1)} %w_embed.5, bf16[512,512]{1,0:T(8,128)(2,1)} %w_send.5), custom_call_target="tpu_custom_call" | custom-call | flops 1048576 | bytes 4920324 | tf_op jit(solution)/shard_map/enc_last/pallas_call | solution.py:271
  65.2 2.5 %node_update.1.nodes.band_one = bf16[1024,512]{1,0:T(8,128)(2,1)S(1)} custom-call(bf16[1024,512]{1,0:T(8,128)(2,1)S(1)} %enc_last.1.node_in, bf16[512,512]{1,0:T(8,128)(2,1)} %w_node.1, bf16[1024,512]{1,0:T(8,128)(2,1)} %all-gather.3.cloned.1.call-done.init), custom_call_target="tpu_custom_call" | custom-call | bytes 3670016 | tf_op jit(solution)/shard_map/node_update/pallas_call | solution.py:271
  67.7 1.9 %collective-permute-start.3 = (bf16[1024,512]{1,0:T(8,128)(2,1)S(1)}, bf16[1024,512]{1,0:T(8,128)(2,1)}, u32[]{:S(2)}, u32[]{:S(2)}) collective-permute-start(bf16[1024,512]{1,0:T(8,128)(2,1)S(1)} %node_update.1.nodes.band_one), channel_id=1, source_target_pairs={{0,8},{16,24},{32,40},{48,56},{64,72},{80,88},{96,104},{112,120},{... | collective-permute-start | bytes 3145736 | tf_op jit(solution)/shard_map/ppermute | solution.py:335
  69.7 3.4 %collective-permute-start.2 = (bf16[1024,512]{1,0:T(8,128)(2,1)S(1)}, bf16[1024,512]{1,0:T(8,128)(2,1)}, u32[]{:S(2)}, u32[]{:S(2)}) collective-permute-start(bf16[1024,512]{1,0:T(8,128)(2,1)S(1)} %node_update.1.nodes.band_one), channel_id=1, source_target_pairs={{8,16},{24,32},{40,48},{56,64},{72,80},{88,96},{104,112},{120,128}... | collective-permute-start | bytes 3145736 | tf_op jit(solution)/shard_map/ppermute | solution.py:332
  73.1 0.1 stack.30.place
  73.2 0.1 pad_add_fusion.pick
  73.3 1.2 copy-done.1
  74.5 1.2 copy-done.3
  75.7 1.3 dec_counts.1.counts
  77.0 1.3 proc_first.1.acc
  78.4 2.7 %proc_more.1.acc = bf16[1024,512]{1,0:T(8,128)(2,1)S(1)} custom-call(s32[1]{0:T(128)} %bitcast.3.pick, s32[8,128]{1,0:T(8,128)S(1)} %bitcast.24, bf16[1024,512]{1,0:T(8,128)(2,1)} %collective-permute-done.3.nodes, bf16[1024,512]{1,0:T(8,128)(2,1)S(1)} %proc_first.1.acc), custom_call_target="tpu_custom_call" | custom-call | flops 1073741824 | bytes 3149828 | tf_op jit(solution)/shard_map/proc_more/pallas_call | solution.py:271
  81.1 8.1 %collective-permute-done.2.nodes = bf16[1024,512]{1,0:T(8,128)(2,1)} collective-permute-done((bf16[1024,512]{1,0:T(8,128)(2,1)S(1)}, bf16[1024,512]{1,0:T(8,128)(2,1)}, u32[]{:S(2)}, u32[]{:S(2)}) %collective-permute-start.2) | collective-permute-done | bytes 1048608 | tf_op jit(solution)/shard_map/ppermute | solution.py:332
  89.2 4.2 %proc_last.1 = bf16[128,512]{1,0:T(8,128)(2,1)S(1)} custom-call(s32[3]{0:T(128)S(1)} %pad_add_fusion.pick, s32[8,128]{1,0:T(8,128)S(1)} %bitcast.25, s32[8,128]{1,0:T(8,128)S(1)} %bitcast.26, bf16[1024,512]{1,0:T(8,128)(2,1)} %collective-permute-done.2.nodes, bf16[1024,512]{1,0:T(8,128)(2,1)S(1)} %proc_more.1.acc, ...), custom_call_target="tpu_custom_call" | custom-call | flops 1073741824 | bytes 5382156 | tf_op jit(solution)/shard_map/proc_last/pallas_call | solution.py:271
  93.5 5.6 %all_gather.24 = bf16[256,512]{1,0:T(8,128)(2,1)S(1)} all-gather(bf16[128,512]{1,0:T(8,128)(2,1)S(1)} %proc_last.1), channel_id=1, replica_groups={{0,1},{2,3},{4,5},{6,7},{9,10},{11,12},{13,14},{15,8},{16,17},{18,19},{..., dimensions={0}, use_global_device_ids=true | all-gather | bytes 393216 | tf_op jit(solution)/shard_map/all_gather | solution.py:463
  99.1 8.5 %all_gather.25.four = bf16[512,512]{1,0:T(8,128)(2,1)S(1)} all-gather(bf16[256,512]{1,0:T(8,128)(2,1)S(1)} %all_gather.24), channel_id=1, replica_groups={{0,7},{2,1},{4,3},{6,5},{9,8},{11,10},{13,12},{15,14},{16,23},{18,17},{..., dimensions={0}, use_global_device_ids=true | all-gather | bytes 786432 | tf_op jit(solution)/shard_map/all_gather | solution.py:463
  107.6 8.4 %all_gather.26 = bf16[512,512]{1,0:T(8,128)(2,1)S(1)} all-gather(bf16[256,512]{1,0:T(8,128)(2,1)S(1)} %constant_dynamic-slice_fusion.1), channel_id=1, replica_groups={{0,1},{2,3},{4,5},{6,7},{9,10},{11,12},{13,14},{15,8},{16,17},{18,19},{..., dimensions={0}, use_global_device_ids=true | all-gather | bytes 786432 | tf_op jit(solution)/shard_map/all_gather | solution.py:463
  116.1 8.3 %all_gather.27.rest = bf16[512,512]{1,0:T(8,128)(2,1)S(1)} all-gather(bf16[256,512]{1,0:T(8,128)(2,1)S(1)} %constant_dynamic-slice_fusion), channel_id=1, replica_groups={{0,7},{2,1},{4,3},{6,5},{9,8},{11,10},{13,12},{15,14},{16,23},{18,17},{..., dimensions={0}, use_global_device_ids=true | all-gather | bytes 786432 | tf_op jit(solution)/shard_map/all_gather | solution.py:463
  124.3 0.4 dec_sums.5
  124.8 0.4 dec_sums.4
  125.2 2.1 %collective-permute-start.5 = (bf16[256,512]{1,0:T(8,128)(2,1)S(1)}, bf16[256,512]{1,0:T(8,128)(2,1)S(1)}, u32[]{:S(2)}, u32[]{:S(2)}) collective-permute-start(bf16[256,512]{1,0:T(8,128)(2,1)S(1)} %dec_sums.5), channel_id=1, source_target_pairs={{8,16},{24,32},{40,48},{56,64},{72,80},{88,96},{104,112},{120,128}... | collective-permute-start | bytes 786440 | tf_op jit(solution)/shard_map/ppermute | solution.py:332
  127.3 1.9 %collective-permute-start.4 = (bf16[256,512]{1,0:T(8,128)(2,1)S(1)}, bf16[256,512]{1,0:T(8,128)(2,1)S(1)}, u32[]{:S(2)}, u32[]{:S(2)}) collective-permute-start(bf16[256,512]{1,0:T(8,128)(2,1)S(1)} %dec_sums.4), channel_id=1, source_target_pairs={{0,8},{16,24},{32,40},{48,56},{64,72},{80,88},{96,104},{112,120},{... | collective-permute-start | bytes 786440 | tf_op jit(solution)/shard_map/ppermute | solution.py:335
  129.2 0.4 dec_sums.3.own
  129.7 6.7 %collective-permute-done.5.far = bf16[256,512]{1,0:T(8,128)(2,1)S(1)} collective-permute-done((bf16[256,512]{1,0:T(8,128)(2,1)S(1)}, bf16[256,512]{1,0:T(8,128)(2,1)S(1)}, u32[]{:S(2)}, u32[]{:S(2)}) %collective-permute-start.5) | collective-permute-done | bytes 262176 | tf_op jit(solution)/shard_map/ppermute | solution.py:332
  136.4 1.0 dec_last.1
  (31 shorter events, 0.1 us)
Async XLA Ops:
  6.5 58.7 %all-gather.3.cloned.1.call-start = ((), (), s32[]{:S(2)}) async-start(), calls=%async_computation | async-start | bytes 1179648 | tf_op jit(solution)/shard_map/all_gather | solution.py:340
  37.5 11.0 %collective-permute-start = (bf16[8,248,256]{2,1,0:T(8,128)(2,1)S(1)}, bf16[8,248,256]{2,1,0:T(8,128)(2,1)S(1)}, u32[]{:S(2)}, u32[]{:S(2)}) collective-permute-start(bf16[8,248,256]{2,1,0:T(8,128)(2,1)S(1)} %bitcast.16), channel_id=1, source_target_pairs={{0,8},{16,24},{32,40},{48,56},{64,72},{80,88},{96,104},{112,120},{... | collective-permute-start | bytes 3047432 | tf_op jit(solution)/shard_map/ppermute | solution.py:335
  39.4 19.1 %collective-permute-start.1 = (bf16[8,248,256]{2,1,0:T(8,128)(2,1)S(1)}, bf16[8,248,256]{2,1,0:T(8,128)(2,1)S(1)}, u32[]{:S(2)}, u32[]{:S(2)}) collective-permute-start(bf16[8,248,256]{2,1,0:T(8,128)(2,1)S(1)} %bitcast.17), channel_id=1, source_target_pairs={{8,16},{24,32},{40,48},{56,64},{72,80},{88,96},{104,112},{120,128}... | collective-permute-start | bytes 3047432 | tf_op jit(solution)/shard_map/ppermute | solution.py:332
  48.5 5.9 %copy-start.2 = (bf16[8,248,256]{2,1,0:T(8,128)(2,1)}, bf16[8,248,256]{2,1,0:T(8,128)(2,1)S(1)}, u32[]{:S(2)}) copy-start(bf16[8,248,256]{2,1,0:T(8,128)(2,1)S(1)} %collective-permute-done.near.buf) | copy-start | bytes 3047428
  48.5 10.0 %copy-start.12 = (f32[512]{0:T(512)S(1)}, f32[512]{0:T(512)}, u32[]{:S(2)}) copy-start(f32[512]{0:T(512)} %param.22) | copy-start | bytes 6148
  58.5 6.6 %copy-start = (bf16[8,248,256]{2,1,0:T(8,128)(2,1)}, bf16[8,248,256]{2,1,0:T(8,128)(2,1)S(1)}, u32[]{:S(2)}) copy-start(bf16[8,248,256]{2,1,0:T(8,128)(2,1)S(1)} %collective-permute-done.1.far.buf) | copy-start | bytes 3047428
  67.7 10.7 %collective-permute-start.3 = (bf16[1024,512]{1,0:T(8,128)(2,1)S(1)}, bf16[1024,512]{1,0:T(8,128)(2,1)}, u32[]{:S(2)}, u32[]{:S(2)}) collective-permute-start(bf16[1024,512]{1,0:T(8,128)(2,1)S(1)} %node_update.1.nodes.band_one), channel_id=1, source_target_pairs={{0,8},{16,24},{32,40},{48,56},{64,72},{80,88},{96,104},{112,120},{... | collective-permute-start | bytes 3145736 | tf_op jit(solution)/shard_map/ppermute | solution.py:335
  69.7 19.5 %collective-permute-start.2 = (bf16[1024,512]{1,0:T(8,128)(2,1)S(1)}, bf16[1024,512]{1,0:T(8,128)(2,1)}, u32[]{:S(2)}, u32[]{:S(2)}) collective-permute-start(bf16[1024,512]{1,0:T(8,128)(2,1)S(1)} %node_update.1.nodes.band_one), channel_id=1, source_target_pairs={{8,16},{24,32},{40,48},{56,64},{72,80},{88,96},{104,112},{120,128}... | collective-permute-start | bytes 3145736 | tf_op jit(solution)/shard_map/ppermute | solution.py:332
  73.3 1.2 copy-start.1
  74.5 1.2 copy-start.3
  75.7 1.3 copy-start.10
  78.3 10.9 %copy-start.4 = (bf16[512,512]{1,0:T(8,128)(2,1)S(1)}, bf16[512,512]{1,0:T(8,128)(2,1)}, u32[]{:S(2)}) copy-start(bf16[512,512]{1,0:T(8,128)(2,1)} %w_ps.1) | copy-start | bytes 1572868
  78.3 10.9 %copy-start.5 = (bf16[512,512]{1,0:T(8,128)(2,1)S(1)}, bf16[512,512]{1,0:T(8,128)(2,1)}, u32[]{:S(2)}) copy-start(bf16[512,512]{1,0:T(8,128)(2,1)} %w_pr.1) | copy-start | bytes 1572868
  78.4 10.9 %copy-start.6 = (bf16[512,512]{1,0:T(8,128)(2,1)S(1)}, bf16[512,512]{1,0:T(8,128)(2,1)}, u32[]{:S(2)}) copy-start(bf16[512,512]{1,0:T(8,128)(2,1)} %w_po.1) | copy-start | bytes 1572868
  78.4 10.9 %copy-start.7 = (bf16[512,512]{1,0:T(8,128)(2,1)S(1)}, bf16[512,512]{1,0:T(8,128)(2,1)}, u32[]{:S(2)}) copy-start(bf16[512,512]{1,0:T(8,128)(2,1)} %w_ds.1) | copy-start | bytes 1572868
  78.4 10.8 %copy-start.11 = (s32[1024]{0:T(1024)S(1)}, s32[1024]{0:T(1024)}, u32[]{:S(2)}) copy-start(s32[1024]{0:T(1024)} %param.31) | copy-start | bytes 12292
  125.2 11.2 %copy-start.8 = (bf16[256,227]{0,1:T(8,128)(2,1)S(1)}, bf16[256,227]{0,1:T(8,128)(2,1)}, u32[]{:S(2)}) copy-start(bf16[256,227]{0,1:T(8,128)(2,1)} %param.17) | copy-start | bytes 348676
  125.2 11.2 %copy-start.9 = (bf16[512,227]{0,1:T(8,128)(2,1)S(1)}, bf16[512,227]{0,1:T(8,128)(2,1)}, u32[]{:S(2)}) copy-start(bf16[512,227]{0,1:T(8,128)(2,1)} %param.27) | copy-start | bytes 697348
  125.2 11.1 %collective-permute-start.5 = (bf16[256,512]{1,0:T(8,128)(2,1)S(1)}, bf16[256,512]{1,0:T(8,128)(2,1)S(1)}, u32[]{:S(2)}, u32[]{:S(2)}) collective-permute-start(bf16[256,512]{1,0:T(8,128)(2,1)S(1)} %dec_sums.5), channel_id=1, source_target_pairs={{8,16},{24,32},{40,48},{56,64},{72,80},{88,96},{104,112},{120,128}... | collective-permute-start | bytes 786440 | tf_op jit(solution)/shard_map/ppermute | solution.py:332
  127.3 9.1 %collective-permute-start.4 = (bf16[256,512]{1,0:T(8,128)(2,1)S(1)}, bf16[256,512]{1,0:T(8,128)(2,1)S(1)}, u32[]{:S(2)}, u32[]{:S(2)}) collective-permute-start(bf16[256,512]{1,0:T(8,128)(2,1)S(1)} %dec_sums.4), channel_id=1, source_target_pairs={{0,8},{16,24},{32,40},{48,56},{64,72},{80,88},{96,104},{112,120},{... | collective-permute-start | bytes 786440 | tf_op jit(solution)/shard_map/ppermute | solution.py:335
Sparse Core Ops, SparseCore 0:
  9.7 47.5 all-gather.2

commit v5 on v4

--- a/solution.py
+++ b/solution.py
@@ -106,13 +106,14 @@
     patches, _, grid_rows = buf.shape
     columns = w_embed.shape[0]
     nodes = counts.shape[0]
+    across = nodes // LANES
     for s in range(patches):
         here = slice(grid_rows * s, grid_rows * (s + 1))
         notes = notes_of(buf, s, columns, 3 * chunks)
         to, frm = [], []
         for j in range(chunks):
             high, low = notes[chunks + j], notes[2 * chunks + j]
-            key = jnp.where(high // patches == pick, (high % patches) * LANES + low, -1)
+            key = jnp.where(high // across == pick, (high % across) * LANES + low, -1)
             to.append(key)
             frm.append(notes[j])
         counts[:, here] = mm_nt(marks(to, nodes), marks(frm, grid_rows)).astype(jnp.bfloat16)
@@ -154,10 +155,27 @@
 
 
 def enc_last(
-    pick, buf, acc, gain, w_embed, w_send, out, lat, sent, counts, embed, send, sems, *, chunks
+    pick,
+    acc,
+    gain,
+    buf,
+    w_embed,
+    w_send,
+    out,
+    lat,
+    sent,
+    counts,
+    embed,
+    send,
+    sems,
+    load,
+    load_sem,
+    *,
+    chunks,
 ):
+    waits(fetch(load_sem, (buf, load)))()
     copies = fetch(sems, (w_embed, embed), (w_send, send))
-    band_sums(pick[0], buf, embed, send, lat, sent, counts, chunks, waits(copies))
+    band_sums(pick[0], load, embed, send, lat, sent, counts, chunks, waits(copies))
     for here in blocks(out.shape[0]):
         summed = acc[here, :] + mm(counts[here, :], sent[...])
         out[here, :] = silu(rms(summed) * gain[...]).astype(jnp.bfloat16)
@@ -175,63 +193,76 @@
         out[here, :] = (init_here[here, :].astype(jnp.float32) + fresh).astype(jnp.bfloat16)
 
 
-def picked_rows(pick, src, nodes, j):
-    count = nodes.shape[0]
+def sender_marks(pick, src, count, j):
     hot = []
     for i in range(4 * j, 4 * j + 4):
         code = src[i : i + 1, :]
         key = jnp.where(code // count == pick, code % count, -1)
         hot.append(hot_by_column(columns_of(key), count))
-    return mm(jnp.concatenate(hot, axis=0), nodes[...]).astype(jnp.bfloat16)
+    return jnp.concatenate(hot, axis=0)
 
 
 def proc_first(pick, src, nodes, out):
     for j in range(src.shape[0] // 4):
-        out[512 * j : 512 * (j + 1), :] = picked_rows(pick[0], src, nodes, j)
-
-
-def proc_more(pick, src, nodes, acc, out):
-    for j in range(src.shape[0] // 4):
-        at = slice(512 * j, 512 * (j + 1))
-        out[at, :] = acc[at, :] + picked_rows(pick[0], src, nodes, j)
-
-
-def proc_last(
-    pick, src, dst, nodes, acc, band_one, w_ps, w_pr, w_po, w_ds, out, *, last_band
-):
-    band, mine = pick[1], out.shape[0]
-    band_nodes = nodes.shape[0]
+        hot = sender_marks(pick[0], src, nodes.shape[0], j)
+        out[512 * j : 512 * (j + 1), :] = mm(hot, nodes[...]).astype(jnp.bfloat16)
+
+
+def proc_more(pick, src, dst, nodes, acc, band_one, w_ps, w_pr, base, hot):
+    count = nodes.shape[0]
+    mine = LANES
     own = band_one[pl.ds(pl.multiple_of(pick[2] * mine, mine), mine), :]
     recv = mm(own, w_pr[...])
     top = recv.astype(jnp.bfloat16)
     rest = (recv - top.astype(jnp.float32)).astype(jnp.bfloat16)
     recv_pair = jnp.concatenate([top, rest], axis=0)
+    for j in range(src.shape[0] // 4):
+        at = slice(512 * j, 512 * (j + 1))
+        near = mm(sender_marks(pick[0], src, count, j), nodes[...]).astype(jnp.bfloat16)
+        recv_hot = []
+        for i in range(4 * j, 4 * j + 4):
+            one = hot_by_column(columns_of(dst[i : i + 1, :]), mine)
+            recv_hot.append(side([one, one]))
+        recv_rows = mm(jnp.concatenate(recv_hot, axis=0), recv_pair)
+        base[at, :] = mm(acc[at, :] + near, w_ps[...]) + recv_rows
+        hot[at, :] = sender_marks(pick[1], src, count, j)
+
+
+def proc_last(pick, src, dst, nodes, base, hot, band_one, w_ps, w_po, w_ds, out, *, last_band):
+    band, mine = pick[0], out.shape[0]
+    band_nodes = nodes.shape[0]
+    own = band_one[pl.ds(pl.multiple_of(pick[1] * mine, mine), mine), :]
     total = jnp.zeros(own.shape, jnp.float32)
     for j in range(src.shape[0] // 4):
         at = slice(512 * j, 512 * (j + 1))
-        rows = acc[at, :] + picked_rows(pick[0], src, nodes, j)
-        recv_hot, back = [], []
+        rows = mm(hot[at, :], nodes[...]).astype(jnp.bfloat16)
+        back = []
         for i in range(4 * j, 4 * j + 4):
-            to = dst[i : i + 1, :]
-            one = hot_by_column(columns_of(to), LANES)
-            recv_hot.append(side([one, one]))
             target = band + src[i : i + 1, :] // band_nodes - 1
             valid = (target >= 0) & (target <= last_band)
-            back.append(hot_by_row(jnp.where(valid, to, -1), mine))
-        recv_rows = mm(jnp.concatenate(recv_hot, axis=0), recv_pair)
-        msg = silu(mm(rows, w_ps[...]) + recv_rows).astype(jnp.bfloat16)
+            back.append(hot_by_row(jnp.where(valid, dst[i : i + 1, :], -1), mine))
+        msg = silu(mm(rows, w_ps[...]) + base[at, :]).astype(jnp.bfloat16)
         total += mm(side(back), msg)
     norm = rms(total).astype(jnp.bfloat16)
     two = (own.astype(jnp.float32) + mm(norm, w_po[...])).astype(jnp.bfloat16)
     out[...] = silu(mm(two, w_ds[...])).astype(jnp.bfloat16)
 
 
-def dec_counts(place, own, near, far, out, *, columns, skip, chunks):
+def dec_counts(place, own, near, far, far_rest, out, held, sems, *, columns, skip, chunks):
     patches, _, grid_rows = own.shape
     patch, second = place[0], place[1]
     nodes = out.shape[1]
-    for k, buf in enumerate((own, near, far)):
-        notes = notes_of(buf, patch, columns, skip + 3 * chunks)[skip:]
+    half = far.shape[0]
+    upper = patch >= half
+    spot = jnp.where(upper, patch - half, patch)
+    here = [own.at[patch], near.at[patch], far.at[spot], far_rest.at[spot]]
+    waits(fetch(sems, *[(a, held.at[i]) for i, a in enumerate(here)]))()
+    for k in range(3):
+        count = skip + 3 * chunks
+        notes = notes_of(held, k, columns, count)[skip:]
+        if k == 2:
+            later = notes_of(held, 3, columns, count)[skip:]
+            notes = [jnp.where(upper, b, a) for a, b in zip(notes, later)]
         to, frm = [], []
         for j in range(chunks):
             high, low, dst = notes[j], notes[chunks + j], notes[2 * chunks + j]
@@ -267,12 +298,13 @@
     args[len(args) - remote :] = [
         pltpu.with_memory_space_constraint(a, pltpu.HBM) for a in args[len(args) - remote :]
     ]
-    moved = sum(a.size * a.dtype.itemsize for a in args) + out.size * out.dtype.itemsize
+    outs = out if isinstance(out, tuple) else (out,)
+    moved = sum(a.size * a.dtype.itemsize for a in (*args, *outs))
     return pl.pallas_call(
         functools.partial(body, **static),
         out_shape=out,
         in_specs=[smem] * scalars + [block] * (len(args) - scalars - remote) + [away] * remote,
-        out_specs=block,
+        out_specs=(block,) * len(out) if isinstance(out, tuple) else block,
         scratch_shapes=list(scratch),
         compiler_params=pltpu.CompilerParams(vmem_limit_bytes=vmem * MIB),
         cost_estimate=pl.CostEstimate(flops=flops, bytes_accessed=moved, transcendentals=0),
@@ -352,7 +384,8 @@
         scratch=[pltpu.VMEM(a.shape, a.dtype) for a in parts] + [pltpu.SemaphoreType.DMA((5,))],
     )
     own = lax.all_gather(load, "mesh", axis=0, tiled=False)
-    far_load = over_far(own)
+    far_load = over_far(own[: patches // 2])
+    far_after = over_far(own[patches // 2 :])
     near_load = over_near(own)
 
     band_rows = patches * grid_rows
@@ -362,17 +395,19 @@
         vmem=20,
         flops=band_rows * width,
     )
-    scratch = [
-        pltpu.VMEM((band_rows, width), bf16),
-        pltpu.VMEM((band_rows, width), bf16),
-        pltpu.VMEM((band_nodes, band_rows), bf16),
-        pltpu.VMEM((columns, width), bf16),
-        pltpu.VMEM((width, width), bf16),
-        pltpu.SemaphoreType.DMA((2,)),
-    ]
+    def scratch(rows):
+        return [
+            pltpu.VMEM((rows, width), bf16),
+            pltpu.VMEM((rows, width), bf16),
+            pltpu.VMEM((band_nodes, rows), bf16),
+            pltpu.VMEM((columns, width), bf16),
+            pltpu.VMEM((width, width), bf16),
+            pltpu.SemaphoreType.DMA((2,)),
+        ]
+
     acc_shape = shape((band_nodes, width), f32)
     acc = call(
-        enc_first, acc_shape, scalars(1), own, w_embed, w_send, remote=2, scratch=scratch, **enc
+        enc_first, acc_shape, scalars(1), own, w_embed, w_send, remote=2, scratch=scratch(band_rows), **enc
     )
     acc = call(
         enc_more,
@@ -383,7 +418,19 @@
         w_embed,
         w_send,
         remote=2,
-        scratch=scratch,
+        scratch=scratch(band_rows),
+        **enc,
+    )
+    acc = call(
+        enc_more,
+        acc_shape,
+        scalars(2 - far),
+        far_load,
+        acc,
+        w_embed,
+        w_send,
+        remote=2,
+        scratch=scratch(band_rows // 2),
         **enc,
     )
     one_shape = shape((band_nodes, width), bf16)
@@ -391,13 +438,14 @@
         enc_last,
         one_shape,
         scalars(2 - far),
-        far_load,
         acc,
         node_gain.reshape(1, width),
+        far_after,
         w_embed,
         w_send,
-        remote=2,
-        scratch=scratch,
+        remote=3,
+        scratch=scratch(band_rows // 2)
+        + [pltpu.VMEM(far_after.shape, bf16), pltpu.SemaphoreType.DMA((1,))],
         **enc,
     )
     one = call(
@@ -432,25 +480,40 @@
         own,
         near_load,
         far_load,
+        far_after,
         scalars=1,
+        remote=4,
+        scratch=[pltpu.VMEM((4, load_rows, grid_rows), bf16), pltpu.SemaphoreType.DMA((4,))],
         flops=6 * grid_rows * band_nodes * dec_edges,
         columns=columns,
         skip=3 * chunks,
         chunks=dec_edges // LANES,
     )
 
-    got = call(proc_more, pick_shape, scalars(near), src, near_one, got, **pick)
-    sent = call(
-        proc_last,
-        shape((mine, width), bf16),
-        scalars(far, band, patch),
+    base, hot = call(
+        proc_more,
+        (shape((proc_edges, width), f32), shape((proc_edges, band_nodes), bf16)),
+        scalars(near, far, patch),
         src,
         dst,
-        far_one,
+        near_one,
         got,
         one,
         w_proc_send,
         w_proc_recv,
+        **pick,
+    )
+    sent = call(
+        proc_last,
+        shape((mine, width), bf16),
+        scalars(band, patch),
+        src,
+        dst,
+        far_one,
+        base,
+        hot,
+        one,
+        w_proc_send,
         w_proc_out,
         w_dec_send,
         last_band=bands - 1,

time: 145 us -> 151 us (1.041)
  starting transfers between devices: 14.6 us -> 20.1 us
  Pallas kernels: 33.5 us -> 36.1 us
    ppermute x3 -> x4, starting transfers between devices: 8.86 us -> 14.2 us  [over_far(): return lax.ppermute(block, 'grid', far_pairs)]
    pallas_call x13 -> x14, Pallas kernels: 33.5 us -> 36.1 us  [call(): pl.pallas_call(functools.partial(body, **static), out_shape=out, in_specs...]
    unnamed x26, local copies, waits for them, and re-layouts: 2.49 us -> 0.86 us
    ppermute x3 -> x4, waiting for transfers between devices: 18.9 us -> 17.5 us  [over_far(): return lax.ppermute(block, 'grid', far_pairs)]
  transfers between devices with their start and end apart: 7 -> 8, of which waited for: 3 -> 2; matrix products, arithmetic and copies ran while one was open for 0% -> 1% of each run, Pallas kernels for 17% -> 19%
where the time goes in v5:
time: 151 us
  blocking collectives  60.1 us (40%)
  Pallas kernels  36.1 us (24%)
  starting transfers between devices  20.1 us (13%)
  waiting for transfers between devices  18.3 us (12%)
  between operations  13.8 us (9%)
  local copies, waits for them, and re-layouts  2.04 us (1%)
    pallas_call x14, Pallas kernels, call(): pl.pallas_call(functools.partial(body, **static), out_shape=out, in_specs...  36.1 us
    all_gather x4, blocking collectives, meet(): lax.all_gather(rows_here, ('grid', 'mesh'), axis=0, tiled=True, axis_inde...  30.8 us
    all_gather x1, blocking collectives, shards(): own = lax.all_gather(load, 'mesh', axis=0, tiled=False)  29.3 us
    ppermute x4, waiting for transfers between devices, over_far(): return lax.ppermute(block, 'grid', far_pairs)  17.5 us
    ppermute x4, starting transfers between devices, over_far(): return lax.ppermute(block, 'grid', far_pairs)  14.2 us
    ppermute x3, starting transfers between devices, over_near(): return lax.ppermute(block, 'grid', near_pairs)  5.88 us
  transfers between devices with their start and end apart: 8, of which 2 were waited for; matrix products, arithmetic and copies ran while one was open for 1% of the time, Pallas kernels for 19%

profile of v5, /device:TPU:256, one launch (start us, length us, event | category | flops | bytes accessed | tf_op | source)
XLA Modules:
  0.0 150.5 jit_solution(15669099148369082991)
XLA Ops:
  6.5 0.7 all-gather.3.cloned.1.call-update
  7.3 1.0 pack.1
  8.2 29.3 %all-gather = bf16[1984,256]{1,0:T(8,128)(2,1)S(1)} all-gather(bf16[248,256]{1,0:T(8,128)(2,1)S(1)} %pack.1), channel_id=2, replica_groups=mesh['grid'=96,'mesh'=8] {'mesh'}, dimensions={0}, use_global_device_ids=true | all-gather | bytes 1142784 | tf_op jit(solution)/shard_map/all_gather | solution.py:386
  37.5 1.9 %collective-permute-start = (bf16[8,248,256]{2,1,0:T(8,128)(2,1)S(1)}, bf16[8,248,256]{2,1,0:T(8,128)(2,1)S(1)}, u32[]{:S(2)}, u32[]{:S(2)}) collective-permute-start(bf16[8,248,256]{2,1,0:T(8,128)(2,1)S(1)} %bitcast.18), channel_id=1, source_target_pairs={{0,8},{16,24},{32,40},{48,56},{64,72},{80,88},{96,104},{112,120},{... | collective-permute-start | bytes 3047432 | tf_op jit(solution)/shard_map/ppermute | solution.py:367
  39.4 1.1 fusion
  40.5 3.4 %collective-permute-start.1 = (bf16[4,248,256]{2,1,0:T(8,128)(2,1)}, bf16[4,248,256]{2,1,0:T(8,128)(2,1)S(1)}, u32[]{:S(2)}, u32[]{:S(2)}) collective-permute-start(bf16[4,248,256]{2,1,0:T(8,128)(2,1)} %bitcast.10), channel_id=1, source_target_pairs={{8,16},{24,32},{40,48},{56,64},{72,80},{88,96},{104,112},{120,128}... | collective-permute-start | bytes 1523720 | tf_op jit(solution)/shard_map/ppermute | solution.py:364
  43.9 5.5 %collective-permute-start.2 = (bf16[4,248,256]{2,1,0:T(8,128)(2,1)}, bf16[4,248,256]{2,1,0:T(8,128)(2,1)S(1)}, u32[]{:S(2)}, u32[]{:S(2)}) collective-permute-start(bf16[4,248,256]{2,1,0:T(8,128)(2,1)} %bitcast.11), channel_id=1, source_target_pairs={{8,16},{24,32},{40,48},{56,64},{72,80},{88,96},{104,112},{120,128}... | collective-permute-start | bytes 1523720 | tf_op jit(solution)/shard_map/ppermute | solution.py:364
  49.4 5.6 %enc_first.1.acc = f32[1024,512]{1,0:T(8,128)S(1)} custom-call(s32[1]{0:T(128)} %constant.30.clone.1.pick, bf16[8,248,256]{2,1,0:T(8,128)(2,1)S(1)} %bitcast.19, bf16[227,512]{1,0:T(8,128)(2,1)} %w_embed.7, bf16[512,512]{1,0:T(8,128)(2,1)} %w_send.7), custom_call_target="tpu_custom_call" | custom-call | flops 1048576 | bytes 3869700 | tf_op jit(solution)/shard_map/enc_first/pallas_call | solution.py:303
  55.1 5.9 %enc_more.2.acc = f32[1024,512]{1,0:T(8,128)S(1)} custom-call(s32[1]{0:T(128)} %bitcast.2.pick, bf16[8,248,256]{2,1,0:T(8,128)(2,1)S(1)} %collective-permute-done.near.buf, f32[1024,512]{1,0:T(8,128)S(1)} %enc_first.1.acc, bf16[227,512]{1,0:T(8,128)(2,1)} %w_embed.7, bf16[512,512]{1,0:T(8,128)(2,1)} %w_send.7), custom_call_target="tpu_custom_call" | custom-call | flops 1048576 | bytes 5966852 | tf_op jit(solution)/shard_map/enc_more/pallas_call | solution.py:303
  61.0 3.8 %enc_more.3.acc = f32[1024,512]{1,0:T(8,128)S(1)} custom-call(s32[1]{0:T(128)} %bitcast.3.pick, bf16[4,248,256]{2,1,0:T(8,128)(2,1)S(1)} %collective-permute-done.1.far.buf, f32[1024,512]{1,0:T(8,128)S(1)} %enc_more.2.acc, bf16[227,512]{1,0:T(8,128)(2,1)} %w_embed.7, bf16[512,512]{1,0:T(8,128)(2,1)} %w_send.7), custom_call_target="tpu_custom_call" | custom-call | flops 1048576 | bytes 5458948 | tf_op jit(solution)/shard_map/enc_more/pallas_call | solution.py:303
  64.9 0.8 copy-done.12
  65.7 5.0 %enc_last.1.node_in = bf16[1024,512]{1,0:T(8,128)(2,1)S(1)} custom-call(s32[1]{0:T(128)} %bitcast.3.pick, f32[1024,512]{1,0:T(8,128)S(1)} %enc_more.3.acc, f32[1,512]{1,0:T(1,128)S(1)} %bitcast.29, bf16[4,248,256]{2,1,0:T(8,128)(2,1)} %copy-done.12, bf16[227,512]{1,0:T(8,128)(2,1)} %w_embed.7, bf16[512,512]{1,0:T(8,128)(2,1)} %w_send.7), custom_call_target="tpu_custom_call" | custom-call | flops 1048576 | bytes 4412420 | tf_op jit(solution)/shard_map/enc_last/pallas_call | solution.py:303
  70.7 2.5 %node_update.1.nodes.band_one = bf16[1024,512]{1,0:T(8,128)(2,1)S(1)} custom-call(bf16[1024,512]{1,0:T(8,128)(2,1)S(1)} %enc_last.1.node_in, bf16[512,512]{1,0:T(8,128)(2,1)} %w_node.1, bf16[1024,512]{1,0:T(8,128)(2,1)} %all-gather.3.cloned.1.call-done.init), custom_call_target="tpu_custom_call" | custom-call | bytes 3670016 | tf_op jit(solution)/shard_map/node_update/pallas_call | solution.py:303
  73.2 1.9 %collective-permute-start.4 = (bf16[1024,512]{1,0:T(8,128)(2,1)S(1)}, bf16[1024,512]{1,0:T(8,128)(2,1)S(1)}, u32[]{:S(2)}, u32[]{:S(2)}) collective-permute-start(bf16[1024,512]{1,0:T(8,128)(2,1)S(1)} %node_update.1.nodes.band_one), channel_id=1, source_target_pairs={{0,8},{16,24},{32,40},{48,56},{64,72},{80,88},{96,104},{112,120},{... | collective-permute-start | bytes 3145736 | tf_op jit(solution)/shard_map/ppermute | solution.py:367
  75.1 3.4 %collective-permute-start.3 = (bf16[1024,512]{1,0:T(8,128)(2,1)S(1)}, bf16[1024,512]{1,0:T(8,128)(2,1)S(1)}, u32[]{:S(2)}, u32[]{:S(2)}) collective-permute-start(bf16[1024,512]{1,0:T(8,128)(2,1)S(1)} %node_update.1.nodes.band_one), channel_id=1, source_target_pairs={{8,16},{24,32},{40,48},{56,64},{72,80},{88,96},{104,112},{120,128}... | collective-permute-start | bytes 3145736 | tf_op jit(solution)/shard_map/ppermute | solution.py:364
  78.6 0.1 stack.35.place
  78.8 2.4 %dec_counts.1.counts = bf16[768,1024]{1,0:T(8,128)(2,1)S(1)} custom-call(s32[5]{0:T(128)S(1)} %stack.35.place, bf16[8,248,256]{2,1,0:T(8,128)(2,1)} %bitcast.20, bf16[8,248,256]{2,1,0:T(8,128)(2,1)} %copy-done.1, bf16[4,248,256]{2,1,0:T(8,128)(2,1)} %copy-done.3, bf16[4,248,256]{2,1,0:T(8,128)(2,1)} %copy-done.12), custom_call_target="tpu_custom_call" | custom-call | flops 1207959552 | bytes 4620308 | tf_op jit(solution)/shard_map/dec_counts/pallas_call | solution.py:303
  81.3 1.3 proc_first.1.acc
  82.7 3.0 %proc_more.1 = (f32[1024,512]{1,0:T(8,128)S(1)}, bf16[1024,1024]{1,0:T(8,128)(2,1)S(1)}) custom-call(s32[3]{0:T(128)S(1)} %pad_add_fusion.1.pick, s32[8,128]{1,0:T(8,128)S(1)} %bitcast.25, s32[8,128]{1,0:T(8,128)S(1)} %bitcast.27, bf16[1024,512]{1,0:T(8,128)(2,1)S(1)} %collective-permute-done.4.nodes, bf16[1024,512]{1,0:T(8,128)(2,1)S(1)} %proc_first.1.acc, ...), custom_call_target="tpu_custom_call" | custom-call | flops 1073741824 | bytes 8396812 | tf_op jit(solution)/shard_map/proc_more/pallas_call | solution.py:303
  85.7 8.9 %collective-permute-done.3.nodes = bf16[1024,512]{1,0:T(8,128)(2,1)S(1)} collective-permute-done((bf16[1024,512]{1,0:T(8,128)(2,1)S(1)}, bf16[1024,512]{1,0:T(8,128)(2,1)S(1)}, u32[]{:S(2)}, u32[]{:S(2)}) %collective-permute-start.3) | collective-permute-done | bytes 1048608 | tf_op jit(solution)/shard_map/ppermute | solution.py:364
  94.6 3.2 %proc_last.1 = bf16[128,512]{1,0:T(8,128)(2,1)S(1)} custom-call(s32[2]{0:T(128)S(1)} %pad_add_fusion.pick, s32[8,128]{1,0:T(8,128)S(1)} %bitcast.26, s32[8,128]{1,0:T(8,128)S(1)} %bitcast.28, bf16[1024,512]{1,0:T(8,128)(2,1)S(1)} %collective-permute-done.3.nodes, f32[1024,512]{1,0:T(8,128)S(1)} %get-tuple-element.7.base, ...), custom_call_target="tpu_custom_call" | custom-call | flops 1073741824 | bytes 8003592 | tf_op jit(solution)/shard_map/proc_last/pallas_call | solution.py:303
  97.8 5.6 %all_gather.24 = bf16[256,512]{1,0:T(8,128)(2,1)S(1)} all-gather(bf16[128,512]{1,0:T(8,128)(2,1)S(1)} %proc_last.1), channel_id=1, replica_groups={{0,1},{2,3},{4,5},{6,7},{9,10},{11,12},{13,14},{15,8},{16,17},{18,19},{..., dimensions={0}, use_global_device_ids=true | all-gather | bytes 393216 | tf_op jit(solution)/shard_map/all_gather | solution.py:526
  103.5 8.5 %all_gather.25.four = bf16[512,512]{1,0:T(8,128)(2,1)S(1)} all-gather(bf16[256,512]{1,0:T(8,128)(2,1)S(1)} %all_gather.24), channel_id=1, replica_groups={{0,7},{2,1},{4,3},{6,5},{9,8},{11,10},{13,12},{15,14},{16,23},{18,17},{..., dimensions={0}, use_global_device_ids=true | all-gather | bytes 786432 | tf_op jit(solution)/shard_map/all_gather | solution.py:526
  112.0 8.4 %all_gather.26 = bf16[512,512]{1,0:T(8,128)(2,1)S(1)} all-gather(bf16[256,512]{1,0:T(8,128)(2,1)S(1)} %constant_dynamic-slice_fusion.1), channel_id=1, replica_groups={{0,1},{2,3},{4,5},{6,7},{9,10},{11,12},{13,14},{15,8},{16,17},{18,19},{..., dimensions={0}, use_global_device_ids=true | all-gather | bytes 786432 | tf_op jit(solution)/shard_map/all_gather | solution.py:526
  120.4 8.3 %all_gather.27.rest = bf16[512,512]{1,0:T(8,128)(2,1)S(1)} all-gather(bf16[256,512]{1,0:T(8,128)(2,1)S(1)} %constant_dynamic-slice_fusion), channel_id=1, replica_groups={{0,7},{2,1},{4,3},{6,5},{9,8},{11,10},{13,12},{15,14},{16,23},{18,17},{..., dimensions={0}, use_global_device_ids=true | all-gather | bytes 786432 | tf_op jit(solution)/shard_map/all_gather | solution.py:526
  128.7 0.4 dec_sums.5
  129.1 0.4 dec_sums.4
  129.6 2.1 %collective-permute-start.5 = (bf16[256,512]{1,0:T(8,128)(2,1)S(1)}, bf16[256,512]{1,0:T(8,128)(2,1)S(1)}, u32[]{:S(2)}, u32[]{:S(2)}) collective-permute-start(bf16[256,512]{1,0:T(8,128)(2,1)S(1)} %dec_sums.4), channel_id=1, source_target_pairs={{0,8},{16,24},{32,40},{48,56},{64,72},{80,88},{96,104},{112,120},{... | collective-permute-start | bytes 786440 | tf_op jit(solution)/shard_map/ppermute | solution.py:367
  131.6 1.9 %collective-permute-start.6 = (bf16[256,512]{1,0:T(8,128)(2,1)S(1)}, bf16[256,512]{1,0:T(8,128)(2,1)S(1)}, u32[]{:S(2)}, u32[]{:S(2)}) collective-permute-start(bf16[256,512]{1,0:T(8,128)(2,1)S(1)} %dec_sums.5), channel_id=1, source_target_pairs={{8,16},{24,32},{40,48},{56,64},{72,80},{88,96},{104,112},{120,128}... | collective-permute-start | bytes 786440 | tf_op jit(solution)/shard_map/ppermute | solution.py:364
  133.6 0.4 dec_sums.3.own
  134.0 8.6 %collective-permute-done.6.far = bf16[256,512]{1,0:T(8,128)(2,1)S(1)} collective-permute-done((bf16[256,512]{1,0:T(8,128)(2,1)S(1)}, bf16[256,512]{1,0:T(8,128)(2,1)S(1)}, u32[]{:S(2)}, u32[]{:S(2)}) %collective-permute-start.6) | collective-permute-done | bytes 262176 | tf_op jit(solution)/shard_map/ppermute | solution.py:364
  142.6 1.0 dec_last.1
  (36 shorter events, 0.3 us)
Async XLA Ops:
  6.5 64.1 %all-gather.3.cloned.1.call-start = ((), (), s32[]{:S(2)}) async-start(), calls=%async_computation | async-start | bytes 1179648 | tf_op jit(solution)/shard_map/all_gather | solution.py:372
  37.5 17.5 %copy-start = (bf16[1984,256]{1,0:T(8,128)(2,1)}, bf16[1984,256]{1,0:T(8,128)(2,1)S(1)}, u32[]{:S(2)}) copy-start(bf16[1984,256]{1,0:T(8,128)(2,1)S(1)} %all-gather) | copy-start | bytes 3047428
  37.5 17.5 %collective-permute-start = (bf16[8,248,256]{2,1,0:T(8,128)(2,1)S(1)}, bf16[8,248,256]{2,1,0:T(8,128)(2,1)S(1)}, u32[]{:S(2)}, u32[]{:S(2)}) collective-permute-start(bf16[8,248,256]{2,1,0:T(8,128)(2,1)S(1)} %bitcast.18), channel_id=1, source_target_pairs={{0,8},{16,24},{32,40},{48,56},{64,72},{80,88},{96,104},{112,120},{... | collective-permute-start | bytes 3047432 | tf_op jit(solution)/shard_map/ppermute | solution.py:367
  40.5 20.5 %collective-permute-start.1 = (bf16[4,248,256]{2,1,0:T(8,128)(2,1)}, bf16[4,248,256]{2,1,0:T(8,128)(2,1)S(1)}, u32[]{:S(2)}, u32[]{:S(2)}) collective-permute-start(bf16[4,248,256]{2,1,0:T(8,128)(2,1)} %bitcast.10), channel_id=1, source_target_pairs={{8,16},{24,32},{40,48},{56,64},{72,80},{88,96},{104,112},{120,128}... | collective-permute-start | bytes 1523720 | tf_op jit(solution)/shard_map/ppermute | solution.py:364
  43.9 20.9 %collective-permute-start.2 = (bf16[4,248,256]{2,1,0:T(8,128)(2,1)}, bf16[4,248,256]{2,1,0:T(8,128)(2,1)S(1)}, u32[]{:S(2)}, u32[]{:S(2)}) collective-permute-start(bf16[4,248,256]{2,1,0:T(8,128)(2,1)} %bitcast.11), channel_id=1, source_target_pairs={{8,16},{24,32},{40,48},{56,64},{72,80},{88,96},{104,112},{120,128}... | collective-permute-start | bytes 1523720 | tf_op jit(solution)/shard_map/ppermute | solution.py:364
  55.1 5.9 %copy-start.1 = (bf16[8,248,256]{2,1,0:T(8,128)(2,1)}, bf16[8,248,256]{2,1,0:T(8,128)(2,1)S(1)}, u32[]{:S(2)}) copy-start(bf16[8,248,256]{2,1,0:T(8,128)(2,1)S(1)} %collective-permute-done.near.buf) | copy-start | bytes 3047428
  61.0 3.8 %copy-start.3 = (bf16[4,248,256]{2,1,0:T(8,128)(2,1)}, bf16[4,248,256]{2,1,0:T(8,128)(2,1)S(1)}, u32[]{:S(2)}) copy-start(bf16[4,248,256]{2,1,0:T(8,128)(2,1)S(1)} %collective-permute-done.1.far.buf) | copy-start | bytes 1523716
  61.0 4.6 %copy-start.11 = (f32[512]{0:T(512)S(1)}, f32[512]{0:T(512)}, u32[]{:S(2)}) copy-start(f32[512]{0:T(512)} %param.22) | copy-start | bytes 6148
  64.9 0.8 copy-start.12
  73.2 9.4 %collective-permute-start.4 = (bf16[1024,512]{1,0:T(8,128)(2,1)S(1)}, bf16[1024,512]{1,0:T(8,128)(2,1)S(1)}, u32[]{:S(2)}, u32[]{:S(2)}) collective-permute-start(bf16[1024,512]{1,0:T(8,128)(2,1)S(1)} %node_update.1.nodes.band_one), channel_id=1, source_target_pairs={{0,8},{16,24},{32,40},{48,56},{64,72},{80,88},{96,104},{112,120},{... | collective-permute-start | bytes 3145736 | tf_op jit(solution)/shard_map/ppermute | solution.py:367
  75.1 19.4 %collective-permute-start.3 = (bf16[1024,512]{1,0:T(8,128)(2,1)S(1)}, bf16[1024,512]{1,0:T(8,128)(2,1)S(1)}, u32[]{:S(2)}, u32[]{:S(2)}) collective-permute-start(bf16[1024,512]{1,0:T(8,128)(2,1)S(1)} %node_update.1.nodes.band_one), channel_id=1, source_target_pairs={{8,16},{24,32},{40,48},{56,64},{72,80},{88,96},{104,112},{120,128}... | collective-permute-start | bytes 3145736 | tf_op jit(solution)/shard_map/ppermute | solution.py:364
  78.8 2.5 %copy-start.9 = (s32[1024]{0:T(1024)S(1)}, s32[1024]{0:T(1024)}, u32[]{:S(2)}) copy-start(s32[1024]{0:T(1024)} %param.30) | copy-start | bytes 12292
  81.3 1.4 copy-start.2
  81.3 1.4 copy-start.4
  81.3 1.4 copy-start.10
  82.7 11.9 %copy-start.5 = (bf16[512,512]{1,0:T(8,128)(2,1)S(1)}, bf16[512,512]{1,0:T(8,128)(2,1)}, u32[]{:S(2)}) copy-start(bf16[512,512]{1,0:T(8,128)(2,1)} %w_po.1) | copy-start | bytes 1572868
  82.7 11.9 %copy-start.6 = (bf16[512,512]{1,0:T(8,128)(2,1)S(1)}, bf16[512,512]{1,0:T(8,128)(2,1)}, u32[]{:S(2)}) copy-start(bf16[512,512]{1,0:T(8,128)(2,1)} %w_ds.1) | copy-start | bytes 1572868
  129.5 13.1 %copy-start.7 = (bf16[256,227]{0,1:T(8,128)(2,1)S(1)}, bf16[256,227]{0,1:T(8,128)(2,1)}, u32[]{:S(2)}) copy-start(bf16[256,227]{0,1:T(8,128)(2,1)} %param.17) | copy-start | bytes 348676
  129.6 13.1 %copy-start.8 = (bf16[512,227]{0,1:T(8,128)(2,1)S(1)}, bf16[512,227]{0,1:T(8,128)(2,1)}, u32[]{:S(2)}) copy-start(bf16[512,227]{0,1:T(8,128)(2,1)} %param.27) | copy-start | bytes 697348
  129.6 4.4 %collective-permute-start.5 = (bf16[256,512]{1,0:T(8,128)(2,1)S(1)}, bf16[256,512]{1,0:T(8,128)(2,1)S(1)}, u32[]{:S(2)}, u32[]{:S(2)}) collective-permute-start(bf16[256,512]{1,0:T(8,128)(2,1)S(1)} %dec_sums.4), channel_id=1, source_target_pairs={{0,8},{16,24},{32,40},{48,56},{64,72},{80,88},{96,104},{112,120},{... | collective-permute-start | bytes 786440 | tf_op jit(solution)/shard_map/ppermute | solution.py:367
  131.6 11.0 %collective-permute-start.6 = (bf16[256,512]{1,0:T(8,128)(2,1)S(1)}, bf16[256,512]{1,0:T(8,128)(2,1)S(1)}, u32[]{:S(2)}, u32[]{:S(2)}) collective-permute-start(bf16[256,512]{1,0:T(8,128)(2,1)S(1)} %dec_sums.5), channel_id=1, source_target_pairs={{8,16},{24,32},{40,48},{56,64},{72,80},{88,96},{104,112},{120,128}... | collective-permute-start | bytes 786440 | tf_op jit(solution)/shard_map/ppermute | solution.py:364
Sparse Core Ops, SparseCore 0:
  9.7 47.5 all-gather.2

commit v6 on v4

--- a/solution.py
+++ b/solution.py
@@ -175,51 +175,55 @@
         out[here, :] = (init_here[here, :].astype(jnp.float32) + fresh).astype(jnp.bfloat16)
 
 
-def picked_rows(pick, src, nodes, j):
-    count = nodes.shape[0]
+def sender_marks(pick, src, count, j):
     hot = []
     for i in range(4 * j, 4 * j + 4):
         code = src[i : i + 1, :]
         key = jnp.where(code // count == pick, code % count, -1)
         hot.append(hot_by_column(columns_of(key), count))
-    return mm(jnp.concatenate(hot, axis=0), nodes[...]).astype(jnp.bfloat16)
+    return jnp.concatenate(hot, axis=0)
 
 
 def proc_first(pick, src, nodes, out):
     for j in range(src.shape[0] // 4):
-        out[512 * j : 512 * (j + 1), :] = picked_rows(pick[0], src, nodes, j)
-
-
-def proc_more(pick, src, nodes, acc, out):
-    for j in range(src.shape[0] // 4):
-        at = slice(512 * j, 512 * (j + 1))
-        out[at, :] = acc[at, :] + picked_rows(pick[0], src, nodes, j)
-
-
-def proc_last(
-    pick, src, dst, nodes, acc, band_one, w_ps, w_pr, w_po, w_ds, out, *, last_band
-):
-    band, mine = pick[1], out.shape[0]
-    band_nodes = nodes.shape[0]
+        hot = sender_marks(pick[0], src, nodes.shape[0], j)
+        out[512 * j : 512 * (j + 1), :] = mm(hot, nodes[...]).astype(jnp.bfloat16)
+
+
+def proc_more(pick, src, dst, nodes, acc, band_one, w_ps, w_pr, base, hot):
+    count = nodes.shape[0]
+    mine = LANES
     own = band_one[pl.ds(pl.multiple_of(pick[2] * mine, mine), mine), :]
     recv = mm(own, w_pr[...])
     top = recv.astype(jnp.bfloat16)
     rest = (recv - top.astype(jnp.float32)).astype(jnp.bfloat16)
     recv_pair = jnp.concatenate([top, rest], axis=0)
+    for j in range(src.shape[0] // 4):
+        at = slice(512 * j, 512 * (j + 1))
+        near = mm(sender_marks(pick[0], src, count, j), nodes[...]).astype(jnp.bfloat16)
+        recv_hot = []
+        for i in range(4 * j, 4 * j + 4):
+            one = hot_by_column(columns_of(dst[i : i + 1, :]), mine)
+            recv_hot.append(side([one, one]))
+        recv_rows = mm(jnp.concatenate(recv_hot, axis=0), recv_pair)
+        base[at, :] = mm(acc[at, :] + near, w_ps[...]) + recv_rows
+        hot[at, :] = sender_marks(pick[1], src, count, j)
+
+
+def proc_last(pick, src, dst, nodes, base, hot, band_one, w_ps, w_po, w_ds, out, *, last_band):
+    band, mine = pick[0], out.shape[0]
+    band_nodes = nodes.shape[0]
+    own = band_one[pl.ds(pl.multiple_of(pick[1] * mine, mine), mine), :]
     total = jnp.zeros(own.shape, jnp.float32)
     for j in range(src.shape[0] // 4):
         at = slice(512 * j, 512 * (j + 1))
-        rows = acc[at, :] + picked_rows(pick[0], src, nodes, j)
-        recv_hot, back = [], []
+        rows = mm(hot[at, :], nodes[...]).astype(jnp.bfloat16)
+        back = []
         for i in range(4 * j, 4 * j + 4):
-            to = dst[i : i + 1, :]
-            one = hot_by_column(columns_of(to), LANES)
-            recv_hot.append(side([one, one]))
             target = band + src[i : i + 1, :] // band_nodes - 1
             valid = (target >= 0) & (target <= last_band)
-            back.append(hot_by_row(jnp.where(valid, to, -1), mine))
-        recv_rows = mm(jnp.concatenate(recv_hot, axis=0), recv_pair)
-        msg = silu(mm(rows, w_ps[...]) + recv_rows).astype(jnp.bfloat16)
+            back.append(hot_by_row(jnp.where(valid, dst[i : i + 1, :], -1), mine))
+        msg = silu(mm(rows, w_ps[...]) + base[at, :]).astype(jnp.bfloat16)
         total += mm(side(back), msg)
     norm = rms(total).astype(jnp.bfloat16)
     two = (own.astype(jnp.float32) + mm(norm, w_po[...])).astype(jnp.bfloat16)
@@ -252,7 +256,7 @@
     out[...] = total.astype(out.dtype)
 
 
-def dec_last(own, near, far, grid_vars, w_out, out):
+def dec_last(own, far, near, grid_vars, w_out, out):
     total = own[...] + near[...].astype(jnp.float32) + far[...].astype(jnp.float32)
     norm = rms(total).astype(jnp.bfloat16)
     fresh = grid_vars[...].astype(jnp.float32) + mm_nt(w_out[...], norm)
@@ -267,12 +271,13 @@
     args[len(args) - remote :] = [
         pltpu.with_memory_space_constraint(a, pltpu.HBM) for a in args[len(args) - remote :]
     ]
-    moved = sum(a.size * a.dtype.itemsize for a in args) + out.size * out.dtype.itemsize
+    outs = out if isinstance(out, tuple) else (out,)
+    moved = sum(a.size * a.dtype.itemsize for a in (*args, *outs))
     return pl.pallas_call(
         functools.partial(body, **static),
         out_shape=out,
         in_specs=[smem] * scalars + [block] * (len(args) - scalars - remote) + [away] * remote,
-        out_specs=block,
+        out_specs=(block,) * len(out) if isinstance(out, tuple) else block,
         scratch_shapes=list(scratch),
         compiler_params=pltpu.CompilerParams(vmem_limit_bytes=vmem * MIB),
         cost_estimate=pl.CostEstimate(flops=flops, bytes_accessed=moved, transcendentals=0),
@@ -439,18 +444,30 @@
         chunks=dec_edges // LANES,
     )
 
-    got = call(proc_more, pick_shape, scalars(near), src, near_one, got, **pick)
-    sent = call(
-        proc_last,
-        shape((mine, width), bf16),
-        scalars(far, band, patch),
+    base, hot = call(
+        proc_more,
+        (shape((proc_edges, width), f32), shape((proc_edges, band_nodes), bf16)),
+        scalars(near, far, patch),
         src,
         dst,
-        far_one,
+        near_one,
         got,
         one,
         w_proc_send,
         w_proc_recv,
+        **pick,
+    )
+    sent = call(
+        proc_last,
+        shape((mine, width), bf16),
+        scalars(band, patch),
+        src,
+        dst,
+        far_one,
+        base,
+        hot,
+        one,
+        w_proc_send,
         w_proc_out,
         w_dec_send,
         last_band=bands - 1,
@@ -481,8 +498,8 @@
         dec_last,
         shape((columns, grid_rows), bf16),
         own_sums,
+        far_sums,
         near_sums,
-        far_sums,
         grid_turned,
         w_dec_out.T,
         flops=flops,

time: 145 us -> 144 us (level)
  transfers between devices with their start and end apart: 7 -> 7, of which waited for: 3 -> 3; matrix products, arithmetic and copies ran while one was open for 0% -> 0% of each run, Pallas kernels for 17% -> 18%
where the time goes in v6:
time: 144 us; the launch traced here: 143 us
  blocking collectives  60.1 us (42%)
  Pallas kernels  33.6 us (23%)
  waiting for transfers between devices  18.3 us (13%)
  starting transfers between devices  14.6 us (10%)
  between operations  13.7 us (10%)
  local copies, waits for them, and re-layouts  2.61 us (2%)
    pallas_call x13, Pallas kernels, call(): pl.pallas_call(functools.partial(body, **static), out_shape=out, in_specs...  33.6 us
    all_gather x4, blocking collectives, meet(): lax.all_gather(rows_here, ('grid', 'mesh'), axis=0, tiled=True, axis_inde...  30.8 us
    all_gather x1, blocking collectives, shards(): own = lax.all_gather(load, 'mesh', axis=0, tiled=False)  29.3 us
    ppermute x3, waiting for transfers between devices, over_far(): return lax.ppermute(block, 'grid', far_pairs)  17.6 us
    ppermute x3, starting transfers between devices, over_far(): return lax.ppermute(block, 'grid', far_pairs)  8.88 us
    ppermute x3, starting transfers between devices, over_near(): return lax.ppermute(block, 'grid', near_pairs)  5.75 us
  transfers between devices with their start and end apart: 7, of which 3 were waited for; matrix products, arithmetic and copies ran while one was open for 0% of the time, Pallas kernels for 18%

profile of v6, /device:TPU:256, one launch (start us, length us, event | category | flops | bytes accessed | tf_op | source)
XLA Modules:
  0.0 143.1 jit_solution(6029389898911186019)
XLA Ops:
  6.5 0.7 all-gather.3.cloned.1.call-update
  7.3 1.0 pack.1
  8.2 29.3 %all-gather = bf16[1984,256]{1,0:T(8,128)(2,1)S(1)} all-gather(bf16[248,256]{1,0:T(8,128)(2,1)S(1)} %pack.1), channel_id=2, replica_groups=mesh['grid'=96,'mesh'=8] {'mesh'}, dimensions={0}, use_global_device_ids=true | all-gather | bytes 1142784 | tf_op jit(solution)/shard_map/all_gather | solution.py:359
  37.5 1.9 %collective-permute-start = (bf16[8,248,256]{2,1,0:T(8,128)(2,1)S(1)}, bf16[8,248,256]{2,1,0:T(8,128)(2,1)S(1)}, u32[]{:S(2)}, u32[]{:S(2)}) collective-permute-start(bf16[8,248,256]{2,1,0:T(8,128)(2,1)S(1)} %bitcast.16), channel_id=1, source_target_pairs={{0,8},{16,24},{32,40},{48,56},{64,72},{80,88},{96,104},{112,120},{... | collective-permute-start | bytes 3047432 | tf_op jit(solution)/shard_map/ppermute | solution.py:340
  39.4 3.4 %collective-permute-start.1 = (bf16[8,248,256]{2,1,0:T(8,128)(2,1)S(1)}, bf16[8,248,256]{2,1,0:T(8,128)(2,1)S(1)}, u32[]{:S(2)}, u32[]{:S(2)}) collective-permute-start(bf16[8,248,256]{2,1,0:T(8,128)(2,1)S(1)} %bitcast.17), channel_id=1, source_target_pairs={{8,16},{24,32},{40,48},{56,64},{72,80},{88,96},{104,112},{120,128}... | collective-permute-start | bytes 3047432 | tf_op jit(solution)/shard_map/ppermute | solution.py:337
  42.9 5.6 %enc_first.1.acc = f32[1024,512]{1,0:T(8,128)S(1)} custom-call(s32[1]{0:T(128)} %constant.30.clone.1.pick, bf16[8,248,256]{2,1,0:T(8,128)(2,1)S(1)} %bitcast.18, bf16[227,512]{1,0:T(8,128)(2,1)} %w_embed.5, bf16[512,512]{1,0:T(8,128)(2,1)} %w_send.5), custom_call_target="tpu_custom_call" | custom-call | flops 1048576 | bytes 3869700 | tf_op jit(solution)/shard_map/enc_first/pallas_call | solution.py:276
  48.5 5.9 %enc_more.1.acc = f32[1024,512]{1,0:T(8,128)S(1)} custom-call(s32[1]{0:T(128)} %bitcast.2.pick, bf16[8,248,256]{2,1,0:T(8,128)(2,1)S(1)} %collective-permute-done.near.buf, f32[1024,512]{1,0:T(8,128)S(1)} %enc_first.1.acc, bf16[227,512]{1,0:T(8,128)(2,1)} %w_embed.5, bf16[512,512]{1,0:T(8,128)(2,1)} %w_send.5), custom_call_target="tpu_custom_call" | custom-call | flops 1048576 | bytes 5966852 | tf_op jit(solution)/shard_map/enc_more/pallas_call | solution.py:276
  54.5 4.1 %collective-permute-done.1.far.buf = bf16[8,248,256]{2,1,0:T(8,128)(2,1)S(1)} collective-permute-done((bf16[8,248,256]{2,1,0:T(8,128)(2,1)S(1)}, bf16[8,248,256]{2,1,0:T(8,128)(2,1)S(1)}, u32[]{:S(2)}, u32[]{:S(2)}) %collective-permute-start.1) | collective-permute-done | bytes 1015840 | tf_op jit(solution)/shard_map/ppermute | solution.py:337
  58.5 6.6 %enc_last.1.node_in = bf16[1024,512]{1,0:T(8,128)(2,1)S(1)} custom-call(s32[1]{0:T(128)} %bitcast.3.pick, bf16[8,248,256]{2,1,0:T(8,128)(2,1)S(1)} %collective-permute-done.1.far.buf, f32[1024,512]{1,0:T(8,128)S(1)} %enc_more.1.acc, f32[1,512]{1,0:T(1,128)S(1)} %bitcast.28, bf16[227,512]{1,0:T(8,128)(2,1)} %w_embed.5, bf16[512,512]{1,0:T(8,128)(2,1)} %w_send.5), custom_call_target="tpu_custom_call" | custom-call | flops 1048576 | bytes 4920324 | tf_op jit(solution)/shard_map/enc_last/pallas_call | solution.py:276
  65.2 2.5 %node_update.1.nodes.band_one = bf16[1024,512]{1,0:T(8,128)(2,1)S(1)} custom-call(bf16[1024,512]{1,0:T(8,128)(2,1)S(1)} %enc_last.1.node_in, bf16[512,512]{1,0:T(8,128)(2,1)} %w_node.1, bf16[1024,512]{1,0:T(8,128)(2,1)} %all-gather.3.cloned.1.call-done.init), custom_call_target="tpu_custom_call" | custom-call | bytes 3670016 | tf_op jit(solution)/shard_map/node_update/pallas_call | solution.py:276
  67.7 1.9 %collective-permute-start.3 = (bf16[1024,512]{1,0:T(8,128)(2,1)S(1)}, bf16[1024,512]{1,0:T(8,128)(2,1)}, u32[]{:S(2)}, u32[]{:S(2)}) collective-permute-start(bf16[1024,512]{1,0:T(8,128)(2,1)S(1)} %node_update.1.nodes.band_one), channel_id=1, source_target_pairs={{0,8},{16,24},{32,40},{48,56},{64,72},{80,88},{96,104},{112,120},{... | collective-permute-start | bytes 3145736 | tf_op jit(solution)/shard_map/ppermute | solution.py:340
  69.6 3.4 %collective-permute-start.2 = (bf16[1024,512]{1,0:T(8,128)(2,1)S(1)}, bf16[1024,512]{1,0:T(8,128)(2,1)S(1)}, u32[]{:S(2)}, u32[]{:S(2)}) collective-permute-start(bf16[1024,512]{1,0:T(8,128)(2,1)S(1)} %node_update.1.nodes.band_one), channel_id=1, source_target_pairs={{8,16},{24,32},{40,48},{56,64},{72,80},{88,96},{104,112},{120,128}... | collective-permute-start | bytes 3145736 | tf_op jit(solution)/shard_map/ppermute | solution.py:337
  73.1 0.1 stack.34.place
  73.2 0.1 pad_add_fusion.1.pick
  73.3 1.2 copy-done.1
  74.6 1.2 copy-done.3
  75.8 1.3 dec_counts.1.counts
  77.1 1.3 proc_first.1.acc
  78.5 3.8 %proc_more.1 = (f32[1024,512]{1,0:T(8,128)S(1)}, bf16[1024,1024]{1,0:T(8,128)(2,1)S(1)}) custom-call(s32[3]{0:T(128)S(1)} %pad_add_fusion.1.pick, s32[8,128]{1,0:T(8,128)S(1)} %bitcast.24, s32[8,128]{1,0:T(8,128)S(1)} %bitcast.26, bf16[1024,512]{1,0:T(8,128)(2,1)} %collective-permute-done.3.nodes, bf16[1024,512]{1,0:T(8,128)(2,1)S(1)} %proc_first.1.acc, ...), custom_call_target="tpu_custom_call" | custom-call | flops 1073741824 | bytes 8396812 | tf_op jit(solution)/shard_map/proc_more/pallas_call | solution.py:276
  82.3 6.8 %collective-permute-done.2.nodes = bf16[1024,512]{1,0:T(8,128)(2,1)S(1)} collective-permute-done((bf16[1024,512]{1,0:T(8,128)(2,1)S(1)}, bf16[1024,512]{1,0:T(8,128)(2,1)S(1)}, u32[]{:S(2)}, u32[]{:S(2)}) %collective-permute-start.2) | collective-permute-done | bytes 1048608 | tf_op jit(solution)/shard_map/ppermute | solution.py:337
  89.1 3.2 %proc_last.1 = bf16[128,512]{1,0:T(8,128)(2,1)S(1)} custom-call(s32[2]{0:T(128)S(1)} %pad_add_fusion.pick, s32[8,128]{1,0:T(8,128)S(1)} %bitcast.25, s32[8,128]{1,0:T(8,128)S(1)} %bitcast.27, bf16[1024,512]{1,0:T(8,128)(2,1)S(1)} %collective-permute-done.2.nodes, f32[1024,512]{1,0:T(8,128)S(1)} %get-tuple-element.7.base, ...), custom_call_target="tpu_custom_call" | custom-call | flops 1073741824 | bytes 8003592 | tf_op jit(solution)/shard_map/proc_last/pallas_call | solution.py:276
  92.3 5.6 %all_gather.24 = bf16[256,512]{1,0:T(8,128)(2,1)S(1)} all-gather(bf16[128,512]{1,0:T(8,128)(2,1)S(1)} %proc_last.1), channel_id=1, replica_groups={{0,1},{2,3},{4,5},{6,7},{9,10},{11,12},{13,14},{15,8},{16,17},{18,19},{..., dimensions={0}, use_global_device_ids=true | all-gather | bytes 393216 | tf_op jit(solution)/shard_map/all_gather | solution.py:480
  98.0 8.5 %all_gather.25.four = bf16[512,512]{1,0:T(8,128)(2,1)S(1)} all-gather(bf16[256,512]{1,0:T(8,128)(2,1)S(1)} %all_gather.24), channel_id=1, replica_groups={{0,7},{2,1},{4,3},{6,5},{9,8},{11,10},{13,12},{15,14},{16,23},{18,17},{..., dimensions={0}, use_global_device_ids=true | all-gather | bytes 786432 | tf_op jit(solution)/shard_map/all_gather | solution.py:480
  106.5 8.4 %all_gather.26 = bf16[512,512]{1,0:T(8,128)(2,1)S(1)} all-gather(bf16[256,512]{1,0:T(8,128)(2,1)S(1)} %constant_dynamic-slice_fusion.1), channel_id=1, replica_groups={{0,1},{2,3},{4,5},{6,7},{9,10},{11,12},{13,14},{15,8},{16,17},{18,19},{..., dimensions={0}, use_global_device_ids=true | all-gather | bytes 786432 | tf_op jit(solution)/shard_map/all_gather | solution.py:480
  114.9 8.3 %all_gather.27.rest = bf16[512,512]{1,0:T(8,128)(2,1)S(1)} all-gather(bf16[256,512]{1,0:T(8,128)(2,1)S(1)} %constant_dynamic-slice_fusion), channel_id=1, replica_groups={{0,7},{2,1},{4,3},{6,5},{9,8},{11,10},{13,12},{15,14},{16,23},{18,17},{..., dimensions={0}, use_global_device_ids=true | all-gather | bytes 786432 | tf_op jit(solution)/shard_map/all_gather | solution.py:480
  123.2 0.4 dec_sums.5
  123.6 0.4 dec_sums.4
  124.1 2.1 %collective-permute-start.4 = (bf16[256,512]{1,0:T(8,128)(2,1)S(1)}, bf16[256,512]{1,0:T(8,128)(2,1)S(1)}, u32[]{:S(2)}, u32[]{:S(2)}) collective-permute-start(bf16[256,512]{1,0:T(8,128)(2,1)S(1)} %dec_sums.4), channel_id=1, source_target_pairs={{8,16},{24,32},{40,48},{56,64},{72,80},{88,96},{104,112},{120,128}... | collective-permute-start | bytes 786440 | tf_op jit(solution)/shard_map/ppermute | solution.py:337
  126.2 1.9 %collective-permute-start.5 = (bf16[256,512]{1,0:T(8,128)(2,1)S(1)}, bf16[256,512]{1,0:T(8,128)(2,1)S(1)}, u32[]{:S(2)}, u32[]{:S(2)}) collective-permute-start(bf16[256,512]{1,0:T(8,128)(2,1)S(1)} %dec_sums.5), channel_id=1, source_target_pairs={{0,8},{16,24},{32,40},{48,56},{64,72},{80,88},{96,104},{112,120},{... | collective-permute-start | bytes 786440 | tf_op jit(solution)/shard_map/ppermute | solution.py:340
  128.1 0.4 dec_sums.3.own
  128.5 6.7 %collective-permute-done.4.far = bf16[256,512]{1,0:T(8,128)(2,1)S(1)} collective-permute-done((bf16[256,512]{1,0:T(8,128)(2,1)S(1)}, bf16[256,512]{1,0:T(8,128)(2,1)S(1)}, u32[]{:S(2)}, u32[]{:S(2)}) %collective-permute-start.4) | collective-permute-done | bytes 262176 | tf_op jit(solution)/shard_map/ppermute | solution.py:337
  135.3 1.0 dec_last.1
  (32 shorter events, 0.2 us)
Async XLA Ops:
  6.5 58.6 %all-gather.3.cloned.1.call-start = ((), (), s32[]{:S(2)}) async-start(), calls=%async_computation | async-start | bytes 1179648 | tf_op jit(solution)/shard_map/all_gather | solution.py:345
  37.5 11.0 %collective-permute-start = (bf16[8,248,256]{2,1,0:T(8,128)(2,1)S(1)}, bf16[8,248,256]{2,1,0:T(8,128)(2,1)S(1)}, u32[]{:S(2)}, u32[]{:S(2)}) collective-permute-start(bf16[8,248,256]{2,1,0:T(8,128)(2,1)S(1)} %bitcast.16), channel_id=1, source_target_pairs={{0,8},{16,24},{32,40},{48,56},{64,72},{80,88},{96,104},{112,120},{... | collective-permute-start | bytes 3047432 | tf_op jit(solution)/shard_map/ppermute | solution.py:340
  39.4 19.1 %collective-permute-start.1 = (bf16[8,248,256]{2,1,0:T(8,128)(2,1)S(1)}, bf16[8,248,256]{2,1,0:T(8,128)(2,1)S(1)}, u32[]{:S(2)}, u32[]{:S(2)}) collective-permute-start(bf16[8,248,256]{2,1,0:T(8,128)(2,1)S(1)} %bitcast.17), channel_id=1, source_target_pairs={{8,16},{24,32},{40,48},{56,64},{72,80},{88,96},{104,112},{120,128}... | collective-permute-start | bytes 3047432 | tf_op jit(solution)/shard_map/ppermute | solution.py:337
  48.5 5.9 %copy-start.2 = (bf16[8,248,256]{2,1,0:T(8,128)(2,1)}, bf16[8,248,256]{2,1,0:T(8,128)(2,1)S(1)}, u32[]{:S(2)}) copy-start(bf16[8,248,256]{2,1,0:T(8,128)(2,1)S(1)} %collective-permute-done.near.buf) | copy-start | bytes 3047428
  48.5 10.0 %copy-start.12 = (f32[512]{0:T(512)S(1)}, f32[512]{0:T(512)}, u32[]{:S(2)}) copy-start(f32[512]{0:T(512)} %param.22) | copy-start | bytes 6148
  58.5 6.6 %copy-start = (bf16[8,248,256]{2,1,0:T(8,128)(2,1)}, bf16[8,248,256]{2,1,0:T(8,128)(2,1)S(1)}, u32[]{:S(2)}) copy-start(bf16[8,248,256]{2,1,0:T(8,128)(2,1)S(1)} %collective-permute-done.1.far.buf) | copy-start | bytes 3047428
  67.7 10.7 %collective-permute-start.3 = (bf16[1024,512]{1,0:T(8,128)(2,1)S(1)}, bf16[1024,512]{1,0:T(8,128)(2,1)}, u32[]{:S(2)}, u32[]{:S(2)}) collective-permute-start(bf16[1024,512]{1,0:T(8,128)(2,1)S(1)} %node_update.1.nodes.band_one), channel_id=1, source_target_pairs={{0,8},{16,24},{32,40},{48,56},{64,72},{80,88},{96,104},{112,120},{... | collective-permute-start | bytes 3145736 | tf_op jit(solution)/shard_map/ppermute | solution.py:340
  69.6 19.4 %collective-permute-start.2 = (bf16[1024,512]{1,0:T(8,128)(2,1)S(1)}, bf16[1024,512]{1,0:T(8,128)(2,1)S(1)}, u32[]{:S(2)}, u32[]{:S(2)}) collective-permute-start(bf16[1024,512]{1,0:T(8,128)(2,1)S(1)} %node_update.1.nodes.band_one), channel_id=1, source_target_pairs={{8,16},{24,32},{40,48},{56,64},{72,80},{88,96},{104,112},{120,128}... | collective-permute-start | bytes 3145736 | tf_op jit(solution)/shard_map/ppermute | solution.py:337
  73.3 1.2 copy-start.1
  74.6 1.2 copy-start.3
  75.8 1.4 copy-start.10
  77.1 1.4 copy-start.4
  77.1 1.4 copy-start.5
  77.1 1.4 copy-start.11
  78.5 10.6 %copy-start.6 = (bf16[512,512]{1,0:T(8,128)(2,1)S(1)}, bf16[512,512]{1,0:T(8,128)(2,1)}, u32[]{:S(2)}) copy-start(bf16[512,512]{1,0:T(8,128)(2,1)} %w_po.1) | copy-start | bytes 1572868
  78.5 10.6 %copy-start.7 = (bf16[512,512]{1,0:T(8,128)(2,1)S(1)}, bf16[512,512]{1,0:T(8,128)(2,1)}, u32[]{:S(2)}) copy-start(bf16[512,512]{1,0:T(8,128)(2,1)} %w_ds.1) | copy-start | bytes 1572868
  124.1 11.2 %copy-start.8 = (bf16[256,227]{0,1:T(8,128)(2,1)S(1)}, bf16[256,227]{0,1:T(8,128)(2,1)}, u32[]{:S(2)}) copy-start(bf16[256,227]{0,1:T(8,128)(2,1)} %param.17) | copy-start | bytes 348676
  124.1 11.2 %copy-start.9 = (bf16[512,227]{0,1:T(8,128)(2,1)S(1)}, bf16[512,227]{0,1:T(8,128)(2,1)}, u32[]{:S(2)}) copy-start(bf16[512,227]{0,1:T(8,128)(2,1)} %param.27) | copy-start | bytes 697348
  124.1 11.1 %collective-permute-start.4 = (bf16[256,512]{1,0:T(8,128)(2,1)S(1)}, bf16[256,512]{1,0:T(8,128)(2,1)S(1)}, u32[]{:S(2)}, u32[]{:S(2)}) collective-permute-start(bf16[256,512]{1,0:T(8,128)(2,1)S(1)} %dec_sums.4), channel_id=1, source_target_pairs={{8,16},{24,32},{40,48},{56,64},{72,80},{88,96},{104,112},{120,128}... | collective-permute-start | bytes 786440 | tf_op jit(solution)/shard_map/ppermute | solution.py:337
  126.2 9.1 %collective-permute-start.5 = (bf16[256,512]{1,0:T(8,128)(2,1)S(1)}, bf16[256,512]{1,0:T(8,128)(2,1)S(1)}, u32[]{:S(2)}, u32[]{:S(2)}) collective-permute-start(bf16[256,512]{1,0:T(8,128)(2,1)S(1)} %dec_sums.5), channel_id=1, source_target_pairs={{0,8},{16,24},{32,40},{48,56},{64,72},{80,88},{96,104},{112,120},{... | collective-permute-start | bytes 786440 | tf_op jit(solution)/shard_map/ppermute | solution.py:340
Sparse Core Ops, SparseCore 0:
  9.7 47.5 all-gather.2
